TPU v7x, 32 devices: a whole 2x2x4 slice. The times are simulated.
32 devices in a mesh: dp: 2 (over x), ctx: 4 (over z), exp: 4 (over y, core).
Axes of the slice: x: 2, y: 2, z: 4, core: 2. Of those that a mesh axis runs over, the one named last changes fastest.
Arguments:
- tokens: bfloat16 [8, 2048, 1536], P(('dp', 'exp'), 'ctx'), may hold values from -6 to 6
- attn_gain: float32 [1536], replicated, may hold values from 0.5 to 1.5
- w_query: bfloat16 [1536, 1536], replicated, may hold values from -0.15625 to 0.15625
- key_matrix: bfloat16 [1536, 256], replicated, may hold values from -0.15625 to 0.15625
- value_matrix: bfloat16 [1536, 256], replicated, may hold values from -0.15625 to 0.15625
- w_out: bfloat16 [1536, 1536], replicated, may hold values from -2 to 2
- ffn_gain: float32 [1536], replicated, may hold values from 0.5 to 1.5
- expert_gate_up: bfloat16 [8, 1536, 1536], P('exp'), may hold values from -0.15625 to 0.15625
- expert_down: bfloat16 [8, 768, 1536], P('exp'), may hold values from -0.21875 to 0.21875
- expert_ids: int32 [8, 2048, 4], P(('dp', 'exp'), 'ctx'), may hold values from 0 to 7, all different within a row; in each aligned block of 512 rows (0 to 511, 512 to 1023, ..., all dimensions but the last counted through in order) at most 320 rows name the same one
- gate_weights: float32 [8, 2048, 4], P(('dp', 'exp'), 'ctx'), may hold values from 0.2 to 0.6
- span_order: int32 [8, 8], P(('dp', 'exp')), may hold values from 0 to 7, each once within a row
- out_grad: bfloat16 [8, 2048, 1536], P(('dp', 'exp'), 'ctx'), may hold values from -6 to 6
Outputs:
- layer_output: bfloat16 [8, 2048, 1536], P(('dp', 'exp'), 'ctx')
- tokens_grad: bfloat16 [8, 2048, 1536], P(('dp', 'exp'), 'ctx')
- attn_gain_grad: float32 [1536], P(('dp', 'ctx', 'exp'))
- w_query_grad: float32 [1536, 1536], P(('dp', 'ctx', 'exp'))
- w_key_grad: float32 [1536, 256], P(('dp', 'ctx', 'exp'))
- w_value_grad: float32 [1536, 256], P(('dp', 'ctx', 'exp'))
- w_out_grad: float32 [1536, 1536], P(('dp', 'ctx', 'exp'))
- ffn_gain_grad: float32 [1536], P(('dp', 'ctx', 'exp'))
- expert_gate_up_grad: float32 [8, 1536, 1536], P('exp', ('dp', 'ctx'))
- expert_down_grad: float32 [8, 768, 1536], P('exp', ('dp', 'ctx'))
Inputs may be any that keep to these rules, and one draw needn't show every extreme that they name: `expert_ids`: within the 512 rows of one device, each row names 4 different experts and no expert is named by more than 320 of them; in every draw some expert is named by exactly 320 rows of some such block. `span_order`: each row is a permutation of the 2 * 4 spans of 256 positions of its sequence.
All inputs are finite; a program needn't handle non-finite values.
Results may differ from a plain program's by a relative error of at most 0.028.
Values may be sent and summed in bfloat16 or wider, within the bound.
A program may use at most 320 MiB of HBM per device.

v0:
```python
import jax
import jax.numpy as jnp
from jax import lax
from jax.sharding import PartitionSpec as P

MODEL_WIDTH = 1536
QUERY_HEADS = 12
KEY_VALUE_HEADS = 2
HEAD_SIZE = 128
FF = 768
TOPK = 4
EXP_DEV = 2
TOK_DEV = 512
HALF = 256


epsilon = 1e-06
rope_base = 1000000.0
causal_masked_score = -1e30


def from_behind(value, axis, steps):
    count = lax.axis_size(axis)
    pairs = [(source, (source + steps) % count) for source in range(count)]
    return lax.ppermute(value, axis, pairs)


def as_sent(value):

    def short(part):
        return part.astype(jnp.bfloat16) if part.dtype == jnp.float32 else part

    return jax.tree.map(short, value)


def rms_scale(values, gain_vector):
    return (
        values
        * lax.rsqrt(jnp.mean(values * values, axis=-1, keepdims=True) + epsilon)
        * gain_vector
    )


def apply_rotary(values, rotary_angles):
    middle = values.shape[-1] // 2
    cosine = jnp.cos(rotary_angles)[:, None, :]
    sine_part = jnp.sin(rotary_angles)[:, None, :]
    front_half = values[..., :middle]
    back_half = values[..., middle:]
    return jnp.concatenate(
        [front_half * cosine - back_half * sine_part, back_half * cosine + front_half * sine_part],
        axis=-1,
    )


def angle_table(positions):
    exponent = jnp.arange(HEAD_SIZE // 2, dtype=jnp.float32) * (-2.0 / HEAD_SIZE)
    frequency = jnp.power(jnp.float32(rope_base), exponent)
    return positions.astype(jnp.float32)[:, None] * frequency[None, :]


def per_device(
    tokens,
    attn_gain,
    w_query,
    key_matrix,
    value_matrix,
    w_out,
    ffn_gain,
    expert_gate_up,
    expert_down,
    expert_ids,
    gate_weights,
    span_order,
    out_grad,
):
    cycle_size = lax.axis_size("ctx")
    cycle_here = lax.axis_index("ctx")
    experts = EXP_DEV * lax.axis_size("exp")
    capacity = TOK_DEV * TOPK * 5 // (4 * experts)
    query_group_count = QUERY_HEADS // KEY_VALUE_HEADS
    score_scale = HEAD_SIZE ** (-0.5)
    resident_rows = tokens.shape[1]
    layer_input = tokens[0].astype(jnp.float32)
    span_row = span_order[0]
    offsets = jnp.arange(HALF, dtype=jnp.int32)

    def device_positions(device):
        span_pair = lax.dynamic_slice_in_dim(span_row, 2 * device, 2, 0)
        return (span_pair[:, None] * HALF + offsets[None, :]).reshape(-1)

    query_positions = device_positions(cycle_here)
    rotary_angles = angle_table(query_positions)

    def rotate_here(values):
        return apply_rotary(values, rotary_angles)

    normed_full, norm_one_back = jax.vjp(rms_scale, layer_input, attn_gain)
    normalized_input = normed_full.astype(jnp.bfloat16)
    query_linear = jnp.dot(normalized_input, w_query, preferred_element_type=jnp.float32).reshape(
        resident_rows, QUERY_HEADS, HEAD_SIZE
    )
    key_linear = jnp.dot(normalized_input, key_matrix, preferred_element_type=jnp.float32).reshape(
        resident_rows, KEY_VALUE_HEADS, HEAD_SIZE
    )
    value_lin = jnp.dot(normalized_input, value_matrix, preferred_element_type=jnp.float32).reshape(
        resident_rows, KEY_VALUE_HEADS, HEAD_SIZE
    )
    query_rotated, query_back = jax.vjp(rotate_here, query_linear)
    key_rot, key_pullback = jax.vjp(rotate_here, key_linear)
    query_rows = query_rotated.astype(jnp.bfloat16).reshape(
        resident_rows, KEY_VALUE_HEADS, query_group_count, HEAD_SIZE
    )
    key_heads = key_rot.astype(jnp.bfloat16)
    value_head_rows = value_lin.astype(jnp.bfloat16)

    def block_scores(key_block, source):
        key_positions = device_positions(source)
        allowed = (key_positions[None, :] <= query_positions[:, None])[None, None]
        raw_scores = jnp.einsum(
            "qkgd,skd->kgqs", query_rows, key_block, preferred_element_type=jnp.float32
        )
        return (jnp.where(allowed, raw_scores * score_scale, causal_masked_score), allowed)

    def fold_block(softmax_state, key_block, value_block, source):
        row_max, row_total, accumulated = softmax_state
        scores, allowed = block_scores(key_block, source)
        new_max = jnp.maximum(row_max, jnp.max(scores, axis=-1))
        rescale = jnp.exp(row_max - new_max)
        weights_exp = jnp.where(allowed, jnp.exp(scores - new_max[..., None]), 0.0)
        row_total = row_total * rescale + jnp.sum(weights_exp, axis=-1)
        update = jnp.einsum(
            "kgqs,skd->kgqd",
            weights_exp.astype(jnp.bfloat16),
            value_block,
            preferred_element_type=jnp.float32,
        )
        return (new_max, row_total, accumulated * rescale[..., None] + update)

    start_state = (
        jnp.full(
            (KEY_VALUE_HEADS, query_group_count, resident_rows), causal_masked_score, jnp.float32
        ),
        jnp.zeros((KEY_VALUE_HEADS, query_group_count, resident_rows), jnp.float32),
        jnp.zeros((KEY_VALUE_HEADS, query_group_count, resident_rows, HEAD_SIZE), jnp.float32),
    )
    own_state = fold_block(start_state, key_heads, value_head_rows, cycle_here)

    def forward_step(distance, carried_state):
        key_block, value_block, row_max, row_total, accumulated = carried_state
        key_block, value_block = from_behind((key_block, value_block), "ctx", 1)
        source = (cycle_here - distance) % cycle_size
        new_state = fold_block((row_max, row_total, accumulated), key_block, value_block, source)
        return (key_block, value_block) + new_state

    carried = lax.fori_loop(1, cycle_size, forward_step, (key_heads, value_head_rows) + own_state)
    row_max, row_total, accumulated = (carried[2], carried[3], carried[4])
    log_total = row_max + jnp.log(row_total)
    attention_output = jnp.transpose(accumulated / row_total[..., None], (2, 0, 1, 3)).reshape(
        resident_rows, QUERY_HEADS * HEAD_SIZE
    )
    attended_low = attention_output.astype(jnp.bfloat16)
    residual_mid = layer_input + jnp.dot(attended_low, w_out, preferred_element_type=jnp.float32)
    normed_ffn_full, norm_two_back = jax.vjp(rms_scale, residual_mid, ffn_gain)
    normed_ffn = normed_ffn_full.astype(jnp.bfloat16)
    flat_ids = expert_ids[0].reshape(-1)
    expert_match = (flat_ids[:, None] == jnp.arange(experts, dtype=jnp.int32)[None, :]).astype(
        jnp.int32
    )
    rank_in_block = jnp.sum((jnp.cumsum(expert_match, axis=0) - 1) * expert_match, axis=1)
    slot_index = flat_ids * capacity + rank_in_block
    route_owner = jnp.arange(resident_rows * TOPK, dtype=jnp.int32) // TOPK
    slot_owner = (
        jnp.full((experts * capacity,), resident_rows, dtype=jnp.int32)
        .at[slot_index]
        .set(route_owner)
    )
    padded = jnp.concatenate([normed_ffn, jnp.zeros((1, MODEL_WIDTH), jnp.bfloat16)], axis=0)
    send_rows = padded[slot_owner].reshape(experts, capacity, MODEL_WIDTH)
    routed_rows = lax.all_to_all(send_rows, "exp", split_axis=0, concat_axis=1, tiled=True)
    projected = jnp.einsum(
        "erd,edf->erf", routed_rows, expert_gate_up, preferred_element_type=jnp.float32
    )
    hidden = (jax.nn.gelu(projected[..., :FF]) * projected[..., FF:]).astype(jnp.bfloat16)
    projected, hidden = (projected, hidden)
    expert_result = jnp.einsum(
        "erf,efd->erd", hidden, expert_down, preferred_element_type=jnp.float32
    ).astype(jnp.bfloat16)
    returned = lax.all_to_all(
        expert_result, "exp", split_axis=1, concat_axis=0, tiled=True
    ).reshape(experts * capacity, MODEL_WIDTH)
    route_gates = gate_weights[0]
    routed_out = returned[slot_index].reshape(resident_rows, TOPK, MODEL_WIDTH)
    mixture = jnp.sum(routed_out.astype(jnp.float32) * route_gates[..., None], axis=1)
    layer_output = residual_mid + mixture
    output_grad = out_grad[0].astype(jnp.float32)
    route_grad = (
        (output_grad[:, None, :] * route_gates[..., None])
        .astype(jnp.bfloat16)
        .reshape(resident_rows * TOPK, MODEL_WIDTH)
    )
    send_grad = (
        jnp.zeros((experts * capacity, MODEL_WIDTH), jnp.bfloat16)
        .at[slot_index]
        .set(route_grad)
        .reshape(experts, capacity, MODEL_WIDTH)
    )
    result_grad = lax.all_to_all(send_grad, "exp", split_axis=0, concat_axis=1, tiled=True)
    down_grad = jnp.einsum("erf,erd->efd", hidden, result_grad, preferred_element_type=jnp.float32)
    hidden_grad = jnp.einsum(
        "erd,efd->erf", result_grad, expert_down, preferred_element_type=jnp.float32
    )
    gate_lin = projected[..., :FF]
    up_lin = projected[..., FF:]
    activated, gelu_back = jax.vjp(jax.nn.gelu, gate_lin)
    gate_lin_grad = gelu_back(hidden_grad * up_lin)[0]
    projected_grad = jnp.concatenate([gate_lin_grad, hidden_grad * activated], axis=-1).astype(
        jnp.bfloat16
    )
    gate_up_grad = jnp.einsum(
        "erd,erf->edf", routed_rows, projected_grad, preferred_element_type=jnp.float32
    )
    rows_grad = jnp.einsum(
        "erf,edf->erd", projected_grad, expert_gate_up, preferred_element_type=jnp.float32
    ).astype(jnp.bfloat16)
    returned_grad = lax.all_to_all(
        rows_grad, "exp", split_axis=1, concat_axis=0, tiled=True
    ).reshape(experts * capacity, MODEL_WIDTH)
    normed_ffn_grad = jnp.sum(
        returned_grad[slot_index].reshape(resident_rows, TOPK, MODEL_WIDTH).astype(jnp.float32),
        axis=1,
    )
    mid_norm_grad, ffn_gain_part = norm_two_back(normed_ffn_grad)
    mid_grad = output_grad + mid_norm_grad
    gate_up_share, down_share = (
        lax.psum_scatter(
            gate_up_grad.astype(jnp.bfloat16), ("dp", "ctx"), scatter_dimension=1, tiled=True
        ).astype(jnp.float32),
        lax.psum_scatter(
            down_grad.astype(jnp.bfloat16), ("dp", "ctx"), scatter_dimension=1, tiled=True
        ).astype(jnp.float32),
    )
    attn_grad = mid_grad.astype(jnp.bfloat16)
    w_out_grad = jnp.einsum(
        "tf,td->fd", attended_low, attn_grad, preferred_element_type=jnp.float32
    )
    attention_output_grad = jnp.einsum(
        "td,fd->tf", attn_grad, w_out, preferred_element_type=jnp.float32
    ).astype(jnp.bfloat16)
    head_gradients = attention_output_grad.reshape(
        resident_rows, KEY_VALUE_HEADS, query_group_count, HEAD_SIZE
    )
    delta_rows = jnp.sum(
        (attention_output_grad.astype(jnp.float32) * attention_output).reshape(
            resident_rows, KEY_VALUE_HEADS, query_group_count, HEAD_SIZE
        ),
        axis=-1,
    )
    row_delta = jnp.transpose(delta_rows, (1, 2, 0))

    def block_grads(key_block, value_block, source):
        scores, allowed = block_scores(key_block, source)
        probabilities = jnp.where(allowed, jnp.exp(scores - log_total[..., None]), 0.0)
        prob_grad = jnp.einsum(
            "qkgd,skd->kgqs", head_gradients, value_block, preferred_element_type=jnp.float32
        )
        score_grad = (probabilities * (prob_grad - row_delta[..., None]) * score_scale).astype(
            jnp.bfloat16
        )
        query_part = jnp.einsum(
            "kgqs,skd->qkgd", score_grad, key_block, preferred_element_type=jnp.float32
        )
        key_part = jnp.einsum(
            "kgqs,qkgd->skd", score_grad, query_rows, preferred_element_type=jnp.float32
        )
        value_part = jnp.einsum(
            "kgqs,qkgd->skd",
            probabilities.astype(jnp.bfloat16),
            head_gradients,
            preferred_element_type=jnp.float32,
        )
        return (query_part, key_part, value_part)

    def return_grads(grad_pair):
        return jax.tree.map(
            lambda part, own: part.astype(own.dtype),
            from_behind(as_sent(grad_pair), "ctx", 1),
            grad_pair,
        )

    query_own, key_own, value_own = block_grads(key_heads, value_head_rows, cycle_here)

    def backward_step(distance, carried_state):
        key_block, value_block, key_acc, value_acc, query_acc = carried_state
        key_block, value_block = from_behind((key_block, value_block), "ctx", 1)
        key_acc, value_acc = return_grads((key_acc, value_acc))
        source = (cycle_here - distance) % cycle_size
        query_part, key_part, value_part = block_grads(key_block, value_block, source)
        return (
            key_block,
            value_block,
            key_acc + key_part,
            value_acc + value_part,
            query_acc + query_part,
        )

    back_carried = lax.fori_loop(
        1, cycle_size, backward_step, (key_heads, value_head_rows, key_own, value_own, query_own)
    )
    query_grad = back_carried[4]
    key_gradient, value_gradient = return_grads((back_carried[2], back_carried[3]))
    query_lin_grad = (
        query_back(query_grad.reshape(resident_rows, QUERY_HEADS, HEAD_SIZE))[0]
        .reshape(resident_rows, QUERY_HEADS * HEAD_SIZE)
        .astype(jnp.bfloat16)
    )
    key_linear_grad = (
        key_pullback(key_gradient)[0]
        .reshape(resident_rows, KEY_VALUE_HEADS * HEAD_SIZE)
        .astype(jnp.bfloat16)
    )
    value_linear_grad = value_gradient.reshape(resident_rows, KEY_VALUE_HEADS * HEAD_SIZE).astype(
        jnp.bfloat16
    )
    w_query_grad = jnp.einsum(
        "td,tf->df", normalized_input, query_lin_grad, preferred_element_type=jnp.float32
    )
    w_key_grad = jnp.einsum(
        "td,tf->df", normalized_input, key_linear_grad, preferred_element_type=jnp.float32
    )
    w_value_grad = jnp.einsum(
        "td,tf->df", normalized_input, value_linear_grad, preferred_element_type=jnp.float32
    )
    normed_grad = jnp.einsum(
        "tf,df->td", query_lin_grad, w_query, preferred_element_type=jnp.float32
    )
    normed_grad = normed_grad + jnp.einsum(
        "tf,df->td", key_linear_grad, key_matrix, preferred_element_type=jnp.float32
    )
    normed_grad = normed_grad + jnp.einsum(
        "tf,df->td", value_linear_grad, value_matrix, preferred_element_type=jnp.float32
    )
    input_norm_grad, attn_gain_part = norm_one_back(normed_grad)
    input_grad = (mid_grad + input_norm_grad).astype(jnp.bfloat16)
    shares = (
        lax.psum_scatter(attn_gain_part, ("dp", "ctx", "exp"), scatter_dimension=0, tiled=True),
        lax.psum_scatter(w_query_grad, ("dp", "ctx", "exp"), scatter_dimension=0, tiled=True),
        lax.psum_scatter(w_key_grad, ("dp", "ctx", "exp"), scatter_dimension=0, tiled=True),
        lax.psum_scatter(w_value_grad, ("dp", "ctx", "exp"), scatter_dimension=0, tiled=True),
        lax.psum_scatter(w_out_grad, ("dp", "ctx", "exp"), scatter_dimension=0, tiled=True),
        lax.psum_scatter(ffn_gain_part, ("dp", "ctx", "exp"), scatter_dimension=0, tiled=True),
    )
    return (
        layer_output.astype(jnp.bfloat16)[None],
        input_grad[None],
        shares[0],
        shares[1],
        shares[2],
        shares[3],
        shares[4],
        shares[5],
        gate_up_share,
        down_share,
    )


def solution(mesh):
    placed = (
        P(("dp", "exp"), "ctx", None),
        P(),
        P(),
        P(),
        P(),
        P(),
        P(),
        P("exp", None, None),
        P("exp", None, None),
        P(("dp", "exp"), "ctx", None),
        P(("dp", "exp"), "ctx", None),
        P(("dp", "exp"), None),
        P(("dp", "exp"), "ctx", None),
    )
    return jax.shard_map(
        per_device,
        mesh=mesh,
        in_specs=placed,
        out_specs=(
            P(("dp", "exp"), "ctx", None),
            P(("dp", "exp"), "ctx", None),
            P(("dp", "ctx", "exp")),
            P(("dp", "ctx", "exp"), None),
            P(("dp", "ctx", "exp"), None),
            P(("dp", "ctx", "exp"), None),
            P(("dp", "ctx", "exp"), None),
            P(("dp", "ctx", "exp")),
            P("exp", ("dp", "ctx"), None),
            P("exp", ("dp", "ctx"), None),
        ),
        check_vma=False,
    )
```

profile of v0, /device:TPU:0, one launch (start us, length us, event | category | flops | bytes accessed | tf_op | source)
XLA Modules:
  0.0 1377.7 jit_solution(686749756179290976)
XLA Ops:
  21.2 15.0 %mul.571 = f32[2048,1536]{1,0:T(8,128)} reshape(f32[512,4,1536]{2,1,0:T(4,128)} %mul.570) | data formatting | bytes 25165824 | tf_op jit(solution)/shard_map/mul | solution.py:198
  36.2 16.2 %scatter_custom_fusion.1 = bf16[2560,1536]{1,0:T(8,128)(2,1)} fusion(s32[2048]{0:T(1024)S(1)} %bitcast.393, f32[2048,1536]{1,0:T(8,128)} %mul.571, f32[2048]{0:T(1024)S(1)} %mul.572, bf16[]{:T(256)} %constant.277.clone.1), kind=kCustom, calls=%fused_computation.87 | custom fusion | flops 6291456 | bytes 20455426 | tf_op jit(solution)/shard_map/scatter | solution.py:205
  98.6 96.3 %while.48 = (s32[]{:T(128)}, bf16[512,2,128]{2,0,1:T(8,128)(2,1)}, bf16[512,2,128]{2,0,1:T(8,128)(2,1)}, f32[2,6,512]{2,1,0:T(8,128)S(1)}, f32[2,6,512]{2,1,0:T(...) while((s32[]{:T(128)}, bf16[512,2,128]{2,0,1:T(8,128)(2,1)}, ...), condition=%wide.region_6.7_spmd.clone, body=%wide.region_3.6_spmd.clone.sunk | while | flops 1653355520 | bytes 75907560 | solution.py:156
  103.9 12.8 collective-permute-done
  134.3 14.0 %collective-permute-done = bf16[512,2,128]{2,0,1:T(8,128)(2,1)S(1)} collective-permute-done((bf16[512,2,128]{2,0,1:T(8,128)(2,1)}, bf16[512,2,128]{2,0,1:T(8,128)(2,1)S(1)}, u32[]{:S(2)}, u32[]{:S(2)}) %collective-permute-start) | collective-permute-done | bytes 262176 | tf_op jit(solution)/shard_map/while/body/eval_jaxpr/ppermute | solution.py:25
  164.7 14.4 %collective-permute-done = bf16[512,2,128]{2,0,1:T(8,128)(2,1)S(1)} collective-permute-done((bf16[512,2,128]{2,0,1:T(8,128)(2,1)}, bf16[512,2,128]{2,0,1:T(8,128)(2,1)S(1)}, u32[]{:S(2)}, u32[]{:S(2)}) %collective-permute-start) | collective-permute-done | bytes 262176 | tf_op jit(solution)/shard_map/while/body/eval_jaxpr/ppermute | solution.py:25
  217.5 10.0 gather_fusion
  240.0 80.7 %all-to-all-done = bf16[8,320,1536]{2,1,0:T(8,128)(2,1)} async-done(((bf16[8,320,1536]{2,1,0:T(8,128)(2,1)}), bf16[8,320,1536]{2,1,0:T(8,128)(2,1)}, u32[]{:S(2)}, u32[]{:S(2)}) %all-to-all-start) | async-done | bytes 7864352 | tf_op jit(solution)/shard_map/all_to_all | solution.py:180
  324.4 19.8 %fusion.141 = f32[2,1280,1536]{2,1,0:T(8,128)} fusion(bf16[2,1280,1536]{2,1,0:T(8,128)(2,1)S(1)} %bitcast.363, bf16[2,1536,1536]{2,1,0:T(8,128)(2,1)} %param.24), kind=kOutput, calls=%fused_computation.211 | convolution fusion | flops 12079595520 | bytes 33030144 | tf_op jit(solution)/shard_map/erd,edf->erf/dot_general | solution.py:181
  344.2 19.9 %fusion.58 = (bf16[2,1280,768]{2,1,0:T(8,128)(2,1)}, bf16[2,1280,768]{2,1,0:T(8,128)(2,1)}, bf16[2,1280,768]{2,1,0:T(8,128)(2,1)}) fusion(f32[2,1280,1536]{2,1,0:T(8,128)} %fusion.141, bf16[2,1280,1536]{2,1,0:T(8,128)(2,1)} %bitcast.365, bf16[2,768,1536]{2,1,0:T(8,128)(2,1)} %param.25), kind=kOutput, calls=%fused_computation.81 | convolution fusion | flops 6090915840 | bytes 40108032 | tf_op jit(solution)/shard_map/erd,efd->erf/dot_general | solution.py:210
  364.1 19.5 %convolution_convert_fusion.1 = bf16[2,1280,1536]{2,1,0:T(8,128)(2,1)} fusion(bf16[2,1536,1536]{2,1,0:T(8,128)(2,1)} %param.24, bf16[2,1280,768]{2,1,0:T(8,128)(2,1)} %get-tuple-element.796, bf16[2,1280,768]{2,1,0:T(8,128)(2,1)} %get-tuple-element.795), kind=kOutput, calls=%fused_computation.70 | convolution fusion | flops 12099256320 | bytes 25165824 | tf_op jit(solution)/shard_map/erf,edf->erd/dot_general | solution.py:223
  383.7 15.6 %copy.116 = bf16[2,1280,1536]{2,0,1:T(2,128)(2,1)} copy(bf16[2,1280,1536]{2,1,0:T(8,128)(2,1)} %convolution_convert_fusion.1) | data formatting | bytes 15728640 | tf_op jit(solution)/shard_map/convert_element_type | solution.py:225
  404.9 11.5 convolution_convert_fusion.3
  416.5 9.4 convolution_convert_fusion.2
  425.9 43.7 %copy.109 = bf16[2,1280,1536]{2,0,1:T(2,128)(2,1)} copy(bf16[2,1280,1536]{2,1,0:T(8,128)(2,1)S(1)} %convolution_convert_fusion.2) | data formatting | bytes 15728640 | tf_op jit(solution)/shard_map/convert_element_type | solution.py:188
  469.6 22.8 %all-to-all-done.3 = bf16[2,1280,1536]{2,0,1:T(2,128)(2,1)} async-done(((bf16[2,1280,1536]{2,0,1:T(2,128)(2,1)}), bf16[2,1280,1536]{2,0,1:T(2,128)(2,1)}, u32[]{:S(2)}, u32[]{:S(2)}) %all-to-all-start.3) | async-done | bytes 7864352 | tf_op jit(solution)/shard_map/all_to_all | solution.py:226
  500.9 19.5 %convolution_convert_fusion = bf16[2,1536,1536]{2,1,0:T(8,128)(2,1)} fusion(bf16[2,1280,1536]{2,1,0:T(8,128)(2,1)} %bitcast.364, bf16[2,1280,768]{2,1,0:T(8,128)(2,1)} %get-tuple-element.796, bf16[2,1280,768]{2,1,0:T(8,128)(2,1)} %get-tuple-element.795), kind=kOutput, calls=%fused_computation.69 | convolution fusion | flops 12100042752 | bytes 25165824 | tf_op jit(solution)/shard_map/erd,erf->edf/dot_general | solution.py:220
  528.5 17.9 %gather_fusion.2 = bf16[2048,1536]{1,0:T(8,128)(2,1)} fusion(bf16[2560,1536]{1,0:T(8,128)(2,1)} %bitcast.355, s32[2048]{0:T(1024)S(1)} %broadcast_clamp_fusion), kind=kCustom, calls=%fused_computation.2 | custom fusion | bytes 12591104 | tf_op jit(solution)/shard_map/gather | solution.py:230
  546.4 12.3 reshape.539
  558.7 13.2 reduce_sum.139
  575.2 10.3 all-to-all-done.1
  593.3 17.6 %gather_fusion.1 = bf16[2048,1536]{1,0:T(8,128)(2,1)} fusion(bf16[2560,1536]{1,0:T(8,128)(2,1)} %bitcast.354, s32[2048]{0:T(1024)S(1)} %broadcast_clamp_fusion), kind=kCustom, calls=%fused_computation.1 | custom fusion | bytes 12591104 | tf_op jit(solution)/shard_map/gather | solution.py:193
  610.9 12.3 reshape.537
  623.2 32.6 %multiply_reduce_fusion = f32[512,1536]{1,0:T(8,128)S(1)} fusion(f32[512,4,1536]{2,1,0:T(4,128)} %reshape.537, f32[512,4]{1,0:T(8,128)S(1)} %copy.111), kind=kLoop, calls=%fused_computation.65 | loop fusion | flops 5505024 | bytes 15736832 | tf_op jit(solution)/shard_map/reduce_sum | solution.py:194
  702.3 175.4 %while.49 = (s32[]{:T(128)}, bf16[512,2,128]{2,0,1:T(8,128)(2,1)}, bf16[512,2,128]{2,0,1:T(8,128)(2,1)}, bf16[512,2,128]{2,0,1:T(8,128)(2,1)}, bf16[512,2,128]{2...) while((s32[]{:T(128)}, bf16[512,2,128]{2,0,1:T(8,128)(2,1)}, ...), condition=%wide.region_18.19_spmd.clone, body=%wide.region_17.18_spmd.clone.sunk | while | flops 4069262336 | bytes 108815000 | solution.py:307
  708.8 20.7 %collective-permute-done.2 = bf16[512,2,128]{2,0,1:T(8,128)(2,1)S(1)} collective-permute-done((bf16[512,2,128]{2,0,1:T(8,128)(2,1)}, bf16[512,2,128]{2,0,1:T(8,128)(2,1)S(1)}, u32[]{:S(2)}, u32[]{:S(2)}) %collective-permute-start.2) | collective-permute-done | bytes 262176 | tf_op jit(solution)/shard_map/while/body/eval_jaxpr/ppermute | solution.py:25
  768.1 19.8 %collective-permute-done.2 = bf16[512,2,128]{2,0,1:T(8,128)(2,1)S(1)} collective-permute-done((bf16[512,2,128]{2,0,1:T(8,128)(2,1)}, bf16[512,2,128]{2,0,1:T(8,128)(2,1)S(1)}, u32[]{:S(2)}, u32[]{:S(2)}) %collective-permute-start.2) | collective-permute-done | bytes 262176 | tf_op jit(solution)/shard_map/while/body/eval_jaxpr/ppermute | solution.py:25
  826.4 18.8 %collective-permute-done.2 = bf16[512,2,128]{2,0,1:T(8,128)(2,1)S(1)} collective-permute-done((bf16[512,2,128]{2,0,1:T(8,128)(2,1)}, bf16[512,2,128]{2,0,1:T(8,128)(2,1)S(1)}, u32[]{:S(2)}, u32[]{:S(2)}) %collective-permute-start.2) | collective-permute-done | bytes 262176 | tf_op jit(solution)/shard_map/while/body/eval_jaxpr/ppermute | solution.py:25
  934.9 37.7 %all-reduce.7 = (f32[1536]{0:T(1024)S(1)}, f32[1536]{0:T(1024)S(1)}) all-reduce(f32[1536]{0:T(1024)S(1)} %get-tuple-element.741, f32[1536]{0:T(1024)S(1)} %copy-done.59), channel_id=2, replica_groups=mesh['dp'=2,'ctx'=4,'exp'=4] {'dp','ctx','exp'}, use_global_device_ids=true, to_apply=%region_21.22.clone | all-reduce | flops 3072 | bytes 24576
  986.1 101.8 %reduce-scatter.11.cloned.1.call-done = f32[48,256]{1,0:T(8,128)} async-done(((f32[1536,256]{1,0:T(8,128)}), f32[48,256]{1,0:T(8,128)}) %reduce-scatter.11.cloned.1.call-update) | async-done | bytes 49168 | tf_op jit(solution)/shard_map/reduce_scatter | solution.py:349
  1087.9 140.9 %reduce-scatter.13.cloned.1.call-done = f32[48,1536]{1,0:T(8,128)} async-done(((f32[1536,1536]{1,0:T(8,128)}), f32[48,1536]{1,0:T(8,128)}) %reduce-scatter.13.cloned.1.call-update) | async-done | bytes 294928 | tf_op jit(solution)/shard_map/reduce_scatter | solution.py:350
  1228.8 141.9 %reduce-scatter.7.cloned.1.call-done = f32[48,1536]{1,0:T(8,128)} async-done(((f32[1536,1536]{1,0:T(8,128)}), f32[48,1536]{1,0:T(8,128)}) %reduce-scatter.7.cloned.1.call-update) | async-done | bytes 294928 | tf_op jit(solution)/shard_map/reduce_scatter | solution.py:347
  (415 shorter events, 418.8 us)
Async XLA Ops:
  52.5 175.1 %all-to-all-start.2 = ((bf16[8,320,1536]{2,1,0:T(8,128)(2,1)}), bf16[8,320,1536]{2,1,0:T(8,128)(2,1)}, u32[]{:S(2)}, u32[]{:S(2)}) async-start(bf16[8,320,1536]{2,1,0:T(8,128)(2,1)} %bitcast.359), calls=%async_computation.2 | async-start | bytes 15728640 | tf_op jit(solution)/shard_map/all_to_all | solution.py:208
  98.8 24.3 %collective-permute-start.1 = (bf16[512,2,128]{2,0,1:T(8,128)(2,1)}, bf16[512,2,128]{2,0,1:T(8,128)(2,1)}, u32[]{:S(2)}, u32[]{:S(2)}) collective-permute-start(bf16[512,2,128]{2,0,1:T(8,128)(2,1)} %get-tuple-element.985), channel_id=1, source_target_pairs={{0,4},{4,8},{8,12},{12,0},{1,5},{5,9},{9,13},{13,1},{2,6},{6,10},{... | collective-permute-start | bytes 786440 | tf_op jit(solution)/shard_map/while/body/eval_jaxpr/ppermute | solution.py:25
  101.9 14.8 %collective-permute-start = (bf16[512,2,128]{2,0,1:T(8,128)(2,1)}, bf16[512,2,128]{2,0,1:T(8,128)(2,1)S(1)}, u32[]{:S(2)}, u32[]{:S(2)}) collective-permute-start(bf16[512,2,128]{2,0,1:T(8,128)(2,1)} %get-tuple-element.984), channel_id=1, source_target_pairs={{0,4},{4,8},{8,12},{12,0},{1,5},{5,9},{9,13},{13,1},{2,6},{6,10},{... | collective-permute-start | bytes 786440 | tf_op jit(solution)/shard_map/while/body/eval_jaxpr/ppermute | solution.py:25
  132.6 22.1 %collective-permute-start.1 = (bf16[512,2,128]{2,0,1:T(8,128)(2,1)}, bf16[512,2,128]{2,0,1:T(8,128)(2,1)}, u32[]{:S(2)}, u32[]{:S(2)}) collective-permute-start(bf16[512,2,128]{2,0,1:T(8,128)(2,1)} %get-tuple-element.985), channel_id=1, source_target_pairs={{0,4},{4,8},{8,12},{12,0},{1,5},{5,9},{9,13},{13,1},{2,6},{6,10},{... | collective-permute-start | bytes 786440 | tf_op jit(solution)/shard_map/while/body/eval_jaxpr/ppermute | solution.py:25
  132.6 15.7 %collective-permute-start = (bf16[512,2,128]{2,0,1:T(8,128)(2,1)}, bf16[512,2,128]{2,0,1:T(8,128)(2,1)S(1)}, u32[]{:S(2)}, u32[]{:S(2)}) collective-permute-start(bf16[512,2,128]{2,0,1:T(8,128)(2,1)} %get-tuple-element.984), channel_id=1, source_target_pairs={{0,4},{4,8},{8,12},{12,0},{1,5},{5,9},{9,13},{13,1},{2,6},{6,10},{... | collective-permute-start | bytes 786440 | tf_op jit(solution)/shard_map/while/body/eval_jaxpr/ppermute | solution.py:25
  164.2 21.2 %collective-permute-start.1 = (bf16[512,2,128]{2,0,1:T(8,128)(2,1)}, bf16[512,2,128]{2,0,1:T(8,128)(2,1)}, u32[]{:S(2)}, u32[]{:S(2)}) collective-permute-start(bf16[512,2,128]{2,0,1:T(8,128)(2,1)} %get-tuple-element.985), channel_id=1, source_target_pairs={{0,4},{4,8},{8,12},{12,0},{1,5},{5,9},{9,13},{13,1},{2,6},{6,10},{... | collective-permute-start | bytes 786440 | tf_op jit(solution)/shard_map/while/body/eval_jaxpr/ppermute | solution.py:25
  164.2 14.9 %collective-permute-start = (bf16[512,2,128]{2,0,1:T(8,128)(2,1)}, bf16[512,2,128]{2,0,1:T(8,128)(2,1)S(1)}, u32[]{:S(2)}, u32[]{:S(2)}) collective-permute-start(bf16[512,2,128]{2,0,1:T(8,128)(2,1)} %get-tuple-element.984), channel_id=1, source_target_pairs={{0,4},{4,8},{8,12},{12,0},{1,5},{5,9},{9,13},{13,1},{2,6},{6,10},{... | collective-permute-start | bytes 786440 | tf_op jit(solution)/shard_map/while/body/eval_jaxpr/ppermute | solution.py:25
  227.6 93.1 %all-to-all-start = ((bf16[8,320,1536]{2,1,0:T(8,128)(2,1)}), bf16[8,320,1536]{2,1,0:T(8,128)(2,1)}, u32[]{:S(2)}, u32[]{:S(2)}) async-start(bf16[8,320,1536]{2,1,0:T(8,128)(2,1)} %bitcast.360), calls=%async_computation | async-start | bytes 15728640 | tf_op jit(solution)/shard_map/all_to_all | solution.py:180
  399.3 93.1 %all-to-all-start.3 = ((bf16[2,1280,1536]{2,0,1:T(2,128)(2,1)}), bf16[2,1280,1536]{2,0,1:T(2,128)(2,1)}, u32[]{:S(2)}, u32[]{:S(2)}) async-start(bf16[2,1280,1536]{2,0,1:T(2,128)(2,1)} %copy.116), calls=%async_computation.3 | async-start | bytes 15728640 | tf_op jit(solution)/shard_map/all_to_all | solution.py:226
  404.9 573.2 %reduce-scatter.17.cloned.1.call-start = ((), (), s32[]{:S(2)}) async-start(), calls=%async_computation.15 | async-start | bytes 5308416 | tf_op jit(solution)/shard_map/reduce_scatter | solution.py:239
  492.4 93.1 %all-to-all-start.1 = ((bf16[2,1280,1536]{2,0,1:T(2,128)(2,1)}), bf16[2,1280,1536]{2,0,1:T(2,128)(2,1)}, u32[]{:S(2)}, u32[]{:S(2)}) async-start(bf16[2,1280,1536]{2,0,1:T(2,128)(2,1)} %copy.109), calls=%async_computation.1 | async-start | bytes 15728640 | tf_op jit(solution)/shard_map/all_to_all | solution.py:189
  498.0 482.3 %reduce-scatter.15.cloned.1.call-start = ((), (), s32[]{:S(2)}) async-start(), calls=%async_computation.14 | async-start | bytes 10616832 | tf_op jit(solution)/shard_map/reduce_scatter | solution.py:236
  520.4 465.7 %reduce-scatter.9.cloned.1.call-start = ((), (), s32[]{:S(2)}) async-start(), calls=%async_computation.11 | async-start | bytes 1622016 | tf_op jit(solution)/shard_map/reduce_scatter | solution.py:348
  702.3 186.8 %copy-start.15 = (bf16[1,512,1536]{2,1,0:T(8,128)(2,1)S(1)}, bf16[1,512,1536]{2,1,0:T(8,128)(2,1)}, u32[]{:S(2)}) copy-start(bf16[1,512,1536]{2,1,0:T(8,128)(2,1)} %param.17) | copy-start | bytes 4718596
  702.3 186.8 %copy-start.67 = (f32[1536]{0:T(1024)S(1)}, f32[1536]{0:T(1024)}, u32[]{:S(2)}) copy-start(f32[1536]{0:T(1024)} %param.18) | copy-start | bytes 18436
  702.7 40.8 %collective-permute-start.5 = (bf16[512,2,128]{2,0,1:T(8,128)(2,1)}, bf16[512,2,128]{2,0,1:T(8,128)(2,1)}, u32[]{:S(2)}, u32[]{:S(2)}) collective-permute-start(bf16[512,2,128]{2,0,1:T(8,128)(2,1)} %get-tuple-element.1038), channel_id=1, source_target_pairs={{0,4},{4,8},{8,12},{12,0},{1,5},{5,9},{9,13},{13,1},{2,6},{6,10},{... | collective-permute-start | bytes 786440 | tf_op jit(solution)/shard_map/while/body/eval_jaxpr/ppermute | solution.py:25
  702.8 50.1 %collective-permute-start.4 = (bf16[512,2,128]{2,0,1:T(8,128)(2,1)}, bf16[512,2,128]{2,0,1:T(8,128)(2,1)}, u32[]{:S(2)}, u32[]{:S(2)}) collective-permute-start(bf16[512,2,128]{2,0,1:T(8,128)(2,1)} %get-tuple-element.1037), channel_id=1, source_target_pairs={{0,4},{4,8},{8,12},{12,0},{1,5},{5,9},{9,13},{13,1},{2,6},{6,10},{... | collective-permute-start | bytes 786440 | tf_op jit(solution)/shard_map/while/body/eval_jaxpr/ppermute | solution.py:25
  702.9 33.0 %collective-permute-start.3 = (bf16[512,2,128]{2,0,1:T(8,128)(2,1)}, bf16[512,2,128]{2,0,1:T(8,128)(2,1)}, u32[]{:S(2)}, u32[]{:S(2)}) collective-permute-start(bf16[512,2,128]{2,0,1:T(8,128)(2,1)} %get-tuple-element.1036), channel_id=1, source_target_pairs={{0,4},{4,8},{8,12},{12,0},{1,5},{5,9},{9,13},{13,1},{2,6},{6,10},{... | collective-permute-start | bytes 786440 | tf_op jit(solution)/shard_map/while/body/eval_jaxpr/ppermute | solution.py:25
  703.6 25.9 %collective-permute-start.2 = (bf16[512,2,128]{2,0,1:T(8,128)(2,1)}, bf16[512,2,128]{2,0,1:T(8,128)(2,1)S(1)}, u32[]{:S(2)}, u32[]{:S(2)}) collective-permute-start(bf16[512,2,128]{2,0,1:T(8,128)(2,1)} %get-tuple-element.1035), channel_id=1, source_target_pairs={{0,4},{4,8},{8,12},{12,0},{1,5},{5,9},{9,13},{13,1},{2,6},{6,10},{... | collective-permute-start | bytes 786440 | tf_op jit(solution)/shard_map/while/body/eval_jaxpr/ppermute | solution.py:25
  762.0 39.8 %collective-permute-start.5 = (bf16[512,2,128]{2,0,1:T(8,128)(2,1)}, bf16[512,2,128]{2,0,1:T(8,128)(2,1)}, u32[]{:S(2)}, u32[]{:S(2)}) collective-permute-start(bf16[512,2,128]{2,0,1:T(8,128)(2,1)} %get-tuple-element.1038), channel_id=1, source_target_pairs={{0,4},{4,8},{8,12},{12,0},{1,5},{5,9},{9,13},{13,1},{2,6},{6,10},{... | collective-permute-start | bytes 786440 | tf_op jit(solution)/shard_map/while/body/eval_jaxpr/ppermute | solution.py:25
  762.0 49.2 %collective-permute-start.4 = (bf16[512,2,128]{2,0,1:T(8,128)(2,1)}, bf16[512,2,128]{2,0,1:T(8,128)(2,1)}, u32[]{:S(2)}, u32[]{:S(2)}) collective-permute-start(bf16[512,2,128]{2,0,1:T(8,128)(2,1)} %get-tuple-element.1037), channel_id=1, source_target_pairs={{0,4},{4,8},{8,12},{12,0},{1,5},{5,9},{9,13},{13,1},{2,6},{6,10},{... | collective-permute-start | bytes 786440 | tf_op jit(solution)/shard_map/while/body/eval_jaxpr/ppermute | solution.py:25
  762.0 32.2 %collective-permute-start.3 = (bf16[512,2,128]{2,0,1:T(8,128)(2,1)}, bf16[512,2,128]{2,0,1:T(8,128)(2,1)}, u32[]{:S(2)}, u32[]{:S(2)}) collective-permute-start(bf16[512,2,128]{2,0,1:T(8,128)(2,1)} %get-tuple-element.1036), channel_id=1, source_target_pairs={{0,4},{4,8},{8,12},{12,0},{1,5},{5,9},{9,13},{13,1},{2,6},{6,10},{... | collective-permute-start | bytes 786440 | tf_op jit(solution)/shard_map/while/body/eval_jaxpr/ppermute | solution.py:25
  762.8 25.0 %collective-permute-start.2 = (bf16[512,2,128]{2,0,1:T(8,128)(2,1)}, bf16[512,2,128]{2,0,1:T(8,128)(2,1)S(1)}, u32[]{:S(2)}, u32[]{:S(2)}) collective-permute-start(bf16[512,2,128]{2,0,1:T(8,128)(2,1)} %get-tuple-element.1035), channel_id=1, source_target_pairs={{0,4},{4,8},{8,12},{12,0},{1,5},{5,9},{9,13},{13,1},{2,6},{6,10},{... | collective-permute-start | bytes 786440 | tf_op jit(solution)/shard_map/while/body/eval_jaxpr/ppermute | solution.py:25
  820.3 38.9 %collective-permute-start.5 = (bf16[512,2,128]{2,0,1:T(8,128)(2,1)}, bf16[512,2,128]{2,0,1:T(8,128)(2,1)}, u32[]{:S(2)}, u32[]{:S(2)}) collective-permute-start(bf16[512,2,128]{2,0,1:T(8,128)(2,1)} %get-tuple-element.1038), channel_id=1, source_target_pairs={{0,4},{4,8},{8,12},{12,0},{1,5},{5,9},{9,13},{13,1},{2,6},{6,10},{... | collective-permute-start | bytes 786440 | tf_op jit(solution)/shard_map/while/body/eval_jaxpr/ppermute | solution.py:25
  820.3 48.3 %collective-permute-start.4 = (bf16[512,2,128]{2,0,1:T(8,128)(2,1)}, bf16[512,2,128]{2,0,1:T(8,128)(2,1)}, u32[]{:S(2)}, u32[]{:S(2)}) collective-permute-start(bf16[512,2,128]{2,0,1:T(8,128)(2,1)} %get-tuple-element.1037), channel_id=1, source_target_pairs={{0,4},{4,8},{8,12},{12,0},{1,5},{5,9},{9,13},{13,1},{2,6},{6,10},{... | collective-permute-start | bytes 786440 | tf_op jit(solution)/shard_map/while/body/eval_jaxpr/ppermute | solution.py:25
  820.3 31.2 %collective-permute-start.3 = (bf16[512,2,128]{2,0,1:T(8,128)(2,1)}, bf16[512,2,128]{2,0,1:T(8,128)(2,1)}, u32[]{:S(2)}, u32[]{:S(2)}) collective-permute-start(bf16[512,2,128]{2,0,1:T(8,128)(2,1)} %get-tuple-element.1036), channel_id=1, source_target_pairs={{0,4},{4,8},{8,12},{12,0},{1,5},{5,9},{9,13},{13,1},{2,6},{6,10},{... | collective-permute-start | bytes 786440 | tf_op jit(solution)/shard_map/while/body/eval_jaxpr/ppermute | solution.py:25
  821.1 24.1 %collective-permute-start.2 = (bf16[512,2,128]{2,0,1:T(8,128)(2,1)}, bf16[512,2,128]{2,0,1:T(8,128)(2,1)S(1)}, u32[]{:S(2)}, u32[]{:S(2)}) collective-permute-start(bf16[512,2,128]{2,0,1:T(8,128)(2,1)} %get-tuple-element.1035), channel_id=1, source_target_pairs={{0,4},{4,8},{8,12},{12,0},{1,5},{5,9},{9,13},{13,1},{2,6},{6,10},{... | collective-permute-start | bytes 786440 | tf_op jit(solution)/shard_map/while/body/eval_jaxpr/ppermute | solution.py:25
  878.8 8.4 collective-permute-start.6
  891.0 196.9 %reduce-scatter.11.cloned.1.call-start = ((), (), s32[]{:S(2)}) async-start(), calls=%async_computation.12 | async-start | bytes 1622016 | tf_op jit(solution)/shard_map/reduce_scatter | solution.py:349
  893.0 8.4 collective-permute-start.7
  904.8 323.9 %reduce-scatter.13.cloned.1.call-start = ((), (), s32[]{:S(2)}) async-start(), calls=%async_computation.13 | async-start | bytes 9732096 | tf_op jit(solution)/shard_map/reduce_scatter | solution.py:350
  912.0 458.7 %reduce-scatter.7.cloned.1.call-start = ((), (), s32[]{:S(2)}) async-start(), calls=%async_computation.10 | async-start | bytes 9732096 | tf_op jit(solution)/shard_map/reduce_scatter | solution.py:347
  (88 other events, 1393.1 us)
Sparse Core Ops, SparseCore 0:
  416.6 93.7 reduce-scatter.16
  520.5 161.8 reduce-scatter.14
  891.1 94.9 reduce-scatter.8
  991.8 96.0 reduce-scatter.10
  1094.2 134.5 reduce-scatter.12
  1236.1 134.5 reduce-scatter.6
where the time goes:
time: 1390 us; the launch traced here: 1380 us
  waiting for transfers between devices  618 us (44%)
  matrix products  288 us (21%)
  local copies, waits for them, and re-layouts  261 us (19%)
  other arithmetic  112 us (8%)
  starting transfers between devices  43.8 us (3%)
  blocking collectives  37.7 us (3%)
  between operations  15.4 us (1%)
    reduce_scatter x1, waiting for transfers between devices, per_device(): lax.psum_scatter(w_query_grad, ('dp', 'ctx', 'exp'), scatter_dimension=0,...  142 us
    reduce_scatter x1, waiting for transfers between devices, per_device(): lax.psum_scatter(w_out_grad, ('dp', 'ctx', 'exp'), scatter_dimension=0, t...  141 us
    ppermute x20, waiting for transfers between devices, from_behind(): return lax.ppermute(value, axis, pairs)  117 us
    reduce_scatter x1, waiting for transfers between devices, per_device(): lax.psum_scatter(w_value_grad, ('dp', 'ctx', 'exp'), scatter_dimension=0,...  102 us
    all_to_all x1, waiting for transfers between devices, per_device(): lax.all_to_all(send_rows, 'exp', split_axis=0, concat_axis=1, tiled=True)  80.7 us
    convert_element_type x1, local copies, waits for them, and re-layouts, per_device(): expert_result = jnp.einsum('erf,efd->erd', hidden, expert_down, preferred...  43.7 us
    unnamed x1, blocking collectives  37.7 us
    reduce_sum x1, other arithmetic, per_device(): jnp.sum(routed_out.astype(jnp.float32) * route_gates[..., None], axis=1)  32.6 us
  transfers between devices with their start and end apart: 30, of which 15 were waited for; matrix products, arithmetic and copies ran while one was open for 38% of the time, Pallas kernels for 0%

commit v1 on v0

v1 whole, which is shorter than its diff:
```python
import functools
import math

import jax
import jax.numpy as jnp
from jax import lax
from jax.experimental import pallas as pl
from jax.experimental.pallas import tpu as pltpu
from jax.sharding import PartitionSpec as P

MODEL_WIDTH = 1536
QUERY_HEADS = 12
KEY_VALUE_HEADS = 2
GROUP = QUERY_HEADS // KEY_VALUE_HEADS
HEAD_SIZE = 128
KV_WIDTH = KEY_VALUE_HEADS * HEAD_SIZE
FF = 768
TOPK = 4
EXP_DEV = 2
TOK_DEV = 512
HALF = 256

epsilon = 1e-06
rope_base = 1000000.0
masked_score = -1e30
score_scale = HEAD_SIZE ** (-0.5)
score_to_log2 = score_scale * math.log2(math.e)
gelu_c = math.sqrt(2.0 / math.pi)

f32 = jnp.float32
bf16 = jnp.bfloat16
NT = (((1,), (1,)), ((), ()))
TN = (((0,), (0,)), ((), ()))
VMEM_BYTES = 60 * 1024 * 1024


def dot(a, b):
    return jnp.dot(a, b, preferred_element_type=f32)


def dot_nt(a, b):
    return lax.dot_general(a, b, NT, preferred_element_type=f32)


def dot_tn(a, b):
    return lax.dot_general(a, b, TN, preferred_element_type=f32)


def params(**more):
    return pltpu.CompilerParams(vmem_limit_bytes=VMEM_BYTES, **more)


def cost(flops, size, exps=0):
    return pl.CostEstimate(flops=int(flops), bytes_accessed=int(size), transcendentals=int(exps))


def whole(shape):
    return pl.BlockSpec(shape, lambda *_: (0,) * len(shape))


def rotate(values, cosine, signed_sine):
    return values * cosine + pltpu.roll(values, HEAD_SIZE // 2, 1) * signed_sine


def rotate_back(values, cosine, signed_sine):
    return values * cosine - pltpu.roll(values, HEAD_SIZE // 2, 1) * signed_sine


def norm_kv_kernel(x_ref, gain_ref, wk_ref, wv_ref, cos_ref, sin_ref, normed_ref, kv_ref):
    x = x_ref[...].astype(f32)
    r = lax.rsqrt(jnp.mean(x * x, axis=-1, keepdims=True) + epsilon)
    normed = (x * r * gain_ref[...]).astype(bf16)
    normed_ref[...] = normed
    keys = dot(normed, wk_ref[...])
    cosine, sine = cos_ref[...], sin_ref[...]
    for head in range(KEY_VALUE_HEADS):
        span = slice(head * HEAD_SIZE, (head + 1) * HEAD_SIZE)
        kv_ref[:, span] = rotate(keys[:, span], cosine, sine).astype(bf16)
    kv_ref[:, KV_WIDTH:] = dot(normed, wv_ref[...]).astype(bf16)


def norm_kv(x, gain, wk, wv, cosine, sine):
    rows = x.shape[0]
    return pl.pallas_call(
        norm_kv_kernel,
        out_shape=(
            jax.ShapeDtypeStruct((rows, MODEL_WIDTH), bf16),
            jax.ShapeDtypeStruct((rows, 2 * KV_WIDTH), bf16),
        ),
        compiler_params=params(),
        cost_estimate=cost(4 * rows * MODEL_WIDTH * KV_WIDTH, 5e6),
        name="norm_kv",
    )(x, gain, wk, wv, cosine, sine)


Q_TILE = 512


def query_kernel(normed_ref, wq_ref, cos_ref, sin_ref, q_ref):
    lin = dot(normed_ref[...], wq_ref[...])
    cosine, sine = cos_ref[...], sin_ref[...]
    for head in range(Q_TILE // HEAD_SIZE):
        span = slice(head * HEAD_SIZE, (head + 1) * HEAD_SIZE)
        q_ref[:, span] = rotate(lin[:, span], cosine, sine).astype(bf16)


def query_projection(normed, wq, cosine, sine):
    rows = normed.shape[0]
    return pl.pallas_call(
        query_kernel,
        grid=(MODEL_WIDTH // Q_TILE,),
        in_specs=[
            whole((rows, MODEL_WIDTH)),
            pl.BlockSpec((MODEL_WIDTH, Q_TILE), lambda t: (0, t)),
            whole((rows, HEAD_SIZE)),
            whole((rows, HEAD_SIZE)),
        ],
        out_specs=pl.BlockSpec((rows, Q_TILE), lambda t: (0, t)),
        out_shape=jax.ShapeDtypeStruct((rows, MODEL_WIDTH), bf16),
        compiler_params=params(),
        cost_estimate=cost(2 * rows * MODEL_WIDTH * MODEL_WIDTH, 8e6),
        name="query_projection",
    )(normed, wq, cosine, sine)


def attention_kernel(
    q_ref, k_ref, v_ref, qpos_ref, kpos_ref, wo_ref, x_ref, gain_ref,
    att_ref, att_low_ref, lse_ref, mid_ref, nf_ref, lse_cols,
):
    head = pl.program_id(0)
    rows = q_ref.shape[0]
    half = rows // 2
    keys, values = k_ref[...], v_ref[...]
    lane = lax.broadcasted_iota(jnp.int32, (half, HEAD_SIZE), 1)
    for part in range(2):
        band = slice(part * half, (part + 1) * half)
        scores = dot_nt(q_ref[band, :], keys)
        scores = jnp.where(kpos_ref[...] <= qpos_ref[band, :], scores, masked_score)
        top = jnp.max(scores, axis=-1, keepdims=True) * score_to_log2
        weights = jnp.exp2(scores * score_to_log2 - top)
        total = jnp.sum(weights, axis=-1, keepdims=True)
        out = dot(weights.astype(bf16), values) / total
        columns = pl.ds(pl.multiple_of(head * HEAD_SIZE, HEAD_SIZE), HEAD_SIZE)
        att_ref[band, columns] = out
        att_low_ref[band, columns] = out.astype(bf16)
        lse = top + jnp.log2(total)
        lse_cols[band, :] = jnp.where(lane == head, lse, lse_cols[band, :])

    @pl.when(head == QUERY_HEADS - 1)
    def _():
        lse_ref[...] = lse_cols[...].T[: lse_ref.shape[0], :]
        for part in range(2):
            band = slice(part * half, (part + 1) * half)
            mid = x_ref[band, :].astype(f32) + dot(att_low_ref[band, :], wo_ref[...])
            mid_ref[band, :] = mid
            r = lax.rsqrt(jnp.mean(mid * mid, axis=-1, keepdims=True) + epsilon)
            nf_ref[band, :] = (mid * r * gain_ref[...]).astype(bf16)


HEAD_ROWS = 16


def attention_forward(q, kv_all, qpos_col, kpos_row, wo, x, gain):
    rows, keys = q.shape[0], kv_all.shape[0]
    return pl.pallas_call(
        attention_kernel,
        grid=(QUERY_HEADS,),
        in_specs=[
            pl.BlockSpec((rows, HEAD_SIZE), lambda h: (0, h)),
            pl.BlockSpec((keys, HEAD_SIZE), lambda h: (0, h // GROUP)),
            pl.BlockSpec((keys, HEAD_SIZE), lambda h: (0, KEY_VALUE_HEADS + h // GROUP)),
            whole((rows, 1)),
            whole((1, keys)),
            whole((MODEL_WIDTH, MODEL_WIDTH)),
            whole((rows, MODEL_WIDTH)),
            whole((1, MODEL_WIDTH)),
        ],
        out_specs=(
            whole((rows, MODEL_WIDTH)),
            whole((rows, MODEL_WIDTH)),
            whole((HEAD_ROWS, rows)),
            whole((rows, MODEL_WIDTH)),
            whole((rows, MODEL_WIDTH)),
        ),
        out_shape=(
            jax.ShapeDtypeStruct((rows, MODEL_WIDTH), f32),
            jax.ShapeDtypeStruct((rows, MODEL_WIDTH), bf16),
            jax.ShapeDtypeStruct((HEAD_ROWS, rows), f32),
            jax.ShapeDtypeStruct((rows, MODEL_WIDTH), f32),
            jax.ShapeDtypeStruct((rows, MODEL_WIDTH), bf16),
        ),
        scratch_shapes=[pltpu.VMEM((rows, HEAD_SIZE), f32)],
        compiler_params=params(),
        cost_estimate=cost(8 * rows * keys * MODEL_WIDTH, 2e7, rows * keys * QUERY_HEADS),
        name="attention_forward",
    )(q, kv_all, kv_all, qpos_col, kpos_row, wo, x, gain)


def expert_kernel(
    pos_row_ref, pos_col_ref, gate_row_ref, x_ref, g_ref, wgu_ref, wd_ref, *rest
):
    (y_ref, dx_ref, rows_ref, hidden_ref, slot_grad_ref, pg_ref, y_acc, dx_acc) = rest[-8:]
    expert = pl.program_id(0)
    capacity = rows_ref.shape[-2]
    tokens = x_ref.shape[0]
    slot_r = lax.broadcasted_iota(jnp.int32, (capacity, tokens), 0)
    match = slot_r == pos_row_ref[0]
    pick = match.astype(bf16)
    slot_c = lax.broadcasted_iota(jnp.int32, (tokens, capacity), 1)
    place = (slot_c == pos_col_ref[0]).astype(bf16)
    gates = jnp.sum(jnp.where(match, gate_row_ref[0], 0.0), axis=1, keepdims=True)
    rows = dot(pick, x_ref[...]).astype(bf16)
    slot_grad = (dot(pick, g_ref[...]) * gates).astype(bf16)
    rows_ref[0, 0] = rows
    slot_grad_ref[0, 0] = slot_grad
    projected = dot(rows, wgu_ref[0])
    gate, up = projected[:, :FF], projected[:, FF:]
    square = gate * gate
    tangent = jnp.tanh(gelu_c * (gate + 0.044715 * (square * gate)))
    half_plus = 0.5 + 0.5 * tangent
    activated = gate * half_plus
    slope = half_plus + 0.5 * gate * (1.0 - tangent * tangent) * (
        gelu_c * (1.0 + (3.0 * 0.044715) * square)
    )
    hidden = (activated * up).astype(bf16)
    hidden_ref[0, 0] = hidden
    result = (dot(hidden, wd_ref[0]) * gates).astype(bf16)
    hidden_grad = dot_nt(slot_grad, wd_ref[0])
    pg_ref[0, 0, :, :FF] = (hidden_grad * up * slope).astype(bf16)
    pg_ref[0, 0, :, FF:] = (hidden_grad * activated).astype(bf16)
    rows_grad = dot_nt(pg_ref[0, 0], wgu_ref[0]).astype(bf16)
    y_part = dot(place, result)
    dx_part = dot(place, rows_grad)

    @pl.when(expert == 0)
    def _():
        y_acc[...] = y_part
        dx_acc[...] = dx_part

    @pl.when(expert != 0)
    def _():
        y_acc[...] += y_part
        dx_acc[...] += dx_part

    @pl.when(expert == EXP_DEV - 1)
    def _():
        y_ref[...] = y_acc[...].astype(bf16)
        dx_ref[...] = dx_acc[...].astype(bf16)


def expert_block(block, blocks, capacity, pos, gates, x, g, wgu, wd, kept):
    tokens = x.shape[0]
    kept_shapes = tuple(
        jax.ShapeDtypeStruct((EXP_DEV, blocks, capacity, width), bf16)
        for width in (MODEL_WIDTH, FF, MODEL_WIDTH, 2 * FF)
    )
    kept_specs = tuple(
        pl.BlockSpec((1, 1, capacity, s.shape[-1]), lambda e: (e, block, 0, 0)) for s in kept_shapes
    )
    aliases = {} if kept is None else {7 + i: 2 + i for i in range(4)}
    flops = EXP_DEV * 2 * capacity * (4 * tokens * MODEL_WIDTH + 9 * MODEL_WIDTH * FF)
    out = pl.pallas_call(
        expert_kernel,
        grid=(EXP_DEV,),
        in_specs=[
            pl.BlockSpec((1, 1, tokens), lambda e: (e, 0, 0)),
            pl.BlockSpec((1, tokens, 1), lambda e: (e, 0, 0)),
            pl.BlockSpec((1, 1, tokens), lambda e: (e, 0, 0)),
            whole((tokens, MODEL_WIDTH)),
            whole((tokens, MODEL_WIDTH)),
            pl.BlockSpec((1, MODEL_WIDTH, 2 * FF), lambda e: (e, 0, 0)),
            pl.BlockSpec((1, FF, MODEL_WIDTH), lambda e: (e, 0, 0)),
        ]
        + [pl.BlockSpec(memory_space=pl.ANY) for _ in aliases],
        out_specs=(whole((tokens, MODEL_WIDTH)), whole((tokens, MODEL_WIDTH))) + kept_specs,
        out_shape=(
            jax.ShapeDtypeStruct((tokens, MODEL_WIDTH), bf16),
            jax.ShapeDtypeStruct((tokens, MODEL_WIDTH), bf16),
        )
        + kept_shapes,
        scratch_shapes=[pltpu.VMEM((tokens, MODEL_WIDTH), f32)] * 2,
        input_output_aliases=aliases,
        compiler_params=params(),
        cost_estimate=cost(flops, 3e7),
        name="expert_block",
    )(pos[:, None, :], pos[:, :, None], gates[:, None, :], x, g, wgu, wd, *(kept or ()))
    return out[0], out[1], out[2:]


def middle_kernel(*refs):
    count = len(refs) - 11
    parts = refs[:count]
    mid_ref, g_ref, gain_ref, wo_ref, att_ref = refs[count : count + 5]
    mg_ref, mgl_ref, ag_ref, delta_ref, dgain_ref, delta_cols = refs[count + 5 :]
    rows = mid_ref.shape[0]
    half = rows // 2
    lane = lax.broadcasted_iota(jnp.int32, (half, HEAD_SIZE), 1)
    dgain = jnp.zeros((1, MODEL_WIDTH), f32)
    for part in range(2):
        band = slice(part * half, (part + 1) * half)
        nf_grad = parts[0][band, :].astype(f32)
        for other in parts[1:]:
            nf_grad += other[band, :].astype(f32)
        mid = mid_ref[band, :]
        r = lax.rsqrt(jnp.mean(mid * mid, axis=-1, keepdims=True) + epsilon)
        u = nf_grad * gain_ref[...]
        inner = jnp.mean(u * mid, axis=-1, keepdims=True)
        grad = g_ref[band, :].astype(f32) + r * u - mid * (r * r * r * inner)
        dgain += jnp.sum(nf_grad * mid * r, axis=0, keepdims=True)
        mg_ref[band, :] = grad
        low = grad.astype(bf16)
        mgl_ref[band, :] = low
        att_grad = dot_nt(low, wo_ref[...]).astype(bf16)
        ag_ref[band, :] = att_grad
        delta = jnp.zeros((half, HEAD_SIZE), f32)
        for head in range(QUERY_HEADS):
            span = slice(head * HEAD_SIZE, (head + 1) * HEAD_SIZE)
            one = jnp.sum(att_grad[:, span].astype(f32) * att_ref[band, span], axis=-1, keepdims=True)
            delta = jnp.where(lane == head, one, delta)
        delta_cols[band, :] = delta
    dgain_ref[...] = dgain
    delta_ref[...] = delta_cols[...].T[: delta_ref.shape[0], :]


def middle_backward(parts, mid, g, gain, wo, att):
    rows = mid.shape[0]
    return pl.pallas_call(
        middle_kernel,
        out_shape=(
            jax.ShapeDtypeStruct((rows, MODEL_WIDTH), f32),
            jax.ShapeDtypeStruct((rows, MODEL_WIDTH), bf16),
            jax.ShapeDtypeStruct((rows, MODEL_WIDTH), bf16),
            jax.ShapeDtypeStruct((HEAD_ROWS, rows), f32),
            jax.ShapeDtypeStruct((1, MODEL_WIDTH), f32),
        ),
        scratch_shapes=[pltpu.VMEM((rows, HEAD_SIZE), f32)],
        compiler_params=params(),
        cost_estimate=cost(2 * rows * MODEL_WIDTH * MODEL_WIDTH, 2e7),
        name="middle_backward",
    )(*parts, mid, g, gain, wo, att)


def attention_back_kernel(first, *refs):
    (q_ref, ag_ref, k_ref, v_ref, lse_ref, delta_ref, kpos_ref, qpos_ref) = refs[:8]
    rest = refs[8:]
    if not first:
        dq_in, dkv_in = rest[:2]
        rest = rest[2:]
    dq_ref, dkv_ref, dk_acc, dv_acc = rest
    group, member = pl.program_id(0), pl.program_id(1)
    head = group * GROUP + member
    q, ag, keys, values = q_ref[...], ag_ref[...], k_ref[...], v_ref[...]
    scores = dot_nt(keys, q)
    weights = jnp.exp2(scores * score_to_log2 - lse_ref[pl.ds(head, 1), :])
    weights = jnp.where(kpos_ref[...] <= qpos_ref[...], weights, 0.0)
    weights_grad = dot_nt(values, ag)
    score_grad = (weights * (weights_grad - delta_ref[pl.ds(head, 1), :]) * score_scale).astype(bf16)
    dv = dot(weights.astype(bf16), ag)
    dk = dot(score_grad, q)
    dq = dot_tn(score_grad, keys)
    if not first:
        dq += dq_in[...]
    dq_ref[...] = dq

    @pl.when(member == 0)
    def _():
        dk_acc[...] = dk
        dv_acc[...] = dv

    @pl.when(member != 0)
    def _():
        dk_acc[...] += dk
        dv_acc[...] += dv

    @pl.when(member == GROUP - 1)
    def _():
        for place, total in ((group, dk_acc), (KEY_VALUE_HEADS + group, dv_acc)):
            columns = pl.ds(pl.multiple_of(place * HEAD_SIZE, HEAD_SIZE), HEAD_SIZE)
            value = total[...]
            if not first:
                value += dkv_in[:, columns].astype(f32)
            dkv_ref[:, columns] = value.astype(bf16)


def attention_backward(q, ag, kv, lse, delta, kpos_col, qpos_row, dq, dkv):
    first = dq is None
    rows, keys = q.shape[0], kv.shape[0]
    by_head = pl.BlockSpec((rows, HEAD_SIZE), lambda g, m: (0, g * GROUP + m))
    in_specs = [
        by_head,
        by_head,
        pl.BlockSpec((keys, HEAD_SIZE), lambda g, m: (0, g)),
        pl.BlockSpec((keys, HEAD_SIZE), lambda g, m: (0, KEY_VALUE_HEADS + g)),
        whole((HEAD_ROWS, rows)),
        whole((HEAD_ROWS, rows)),
        whole((keys, 1)),
        whole((1, rows)),
    ]
    args = [q, ag, kv, kv, lse, delta, kpos_col, qpos_row]
    if not first:
        in_specs += [by_head, whole((keys, 2 * KV_WIDTH))]
        args += [dq, dkv]
    return pl.pallas_call(
        functools.partial(attention_back_kernel, first),
        grid=(KEY_VALUE_HEADS, GROUP),
        in_specs=in_specs,
        out_specs=(by_head, whole((keys, 2 * KV_WIDTH))),
        out_shape=(
            jax.ShapeDtypeStruct((rows, MODEL_WIDTH), f32),
            jax.ShapeDtypeStruct((keys, 2 * KV_WIDTH), bf16),
        ),
        scratch_shapes=[pltpu.VMEM((keys, HEAD_SIZE), f32)] * 2,
        compiler_params=params(),
        cost_estimate=cost(10 * rows * keys * MODEL_WIDTH, 1e7, rows * keys * QUERY_HEADS),
        name="attention_backward",
    )(*args)


def unrotate_kernel(dq_ref, cos_ref, sin_ref, out_ref):
    cosine, sine = cos_ref[...], sin_ref[...]
    for head in range(QUERY_HEADS):
        span = slice(head * HEAD_SIZE, (head + 1) * HEAD_SIZE)
        out_ref[:, span] = rotate_back(dq_ref[:, span], cosine, sine).astype(bf16)


def unrotate(dq, cosine, sine):
    return pl.pallas_call(
        unrotate_kernel,
        out_shape=jax.ShapeDtypeStruct(dq.shape, bf16),
        compiler_params=params(),
        cost_estimate=cost(dq.size * 4, dq.size * 6),
        name="unrotate",
    )(dq, cosine, sine)


def input_kernel(
    dql_ref, dkv_ref, wq_ref, wk_ref, wv_ref, cos_ref, sin_ref, x_ref, gain_ref, mg_ref,
    dkvl_ref, dx_ref, dgain_ref,
):
    cosine, sine = cos_ref[...], sin_ref[...]
    for head in range(KEY_VALUE_HEADS):
        span = slice(head * HEAD_SIZE, (head + 1) * HEAD_SIZE)
        dkvl_ref[:, span] = rotate_back(dkv_ref[:, span].astype(f32), cosine, sine).astype(bf16)
    dkvl_ref[:, KV_WIDTH:] = dkv_ref[:, KV_WIDTH:]
    rows = x_ref.shape[0]
    half = rows // 2
    dgain = jnp.zeros((1, MODEL_WIDTH), f32)
    for part in range(2):
        band = slice(part * half, (part + 1) * half)
        grad = dot_nt(dql_ref[band, :], wq_ref[...])
        grad += dot_nt(dkvl_ref[band, :KV_WIDTH], wk_ref[...])
        grad += dot_nt(dkvl_ref[band, KV_WIDTH:], wv_ref[...])
        x = x_ref[band, :].astype(f32)
        r = lax.rsqrt(jnp.mean(x * x, axis=-1, keepdims=True) + epsilon)
        v = grad * gain_ref[...]
        inner = jnp.mean(v * x, axis=-1, keepdims=True)
        dgain += jnp.sum(grad * x * r, axis=0, keepdims=True)
        dx_ref[band, :] = (mg_ref[band, :] + r * v - x * (r * r * r * inner)).astype(bf16)
    dgain_ref[...] = dgain


def input_backward(dql, dkv, wq, wk, wv, cosine, sine, x, gain, mg):
    rows = x.shape[0]
    return pl.pallas_call(
        input_kernel,
        out_shape=(
            jax.ShapeDtypeStruct((rows, 2 * KV_WIDTH), bf16),
            jax.ShapeDtypeStruct((rows, MODEL_WIDTH), bf16),
            jax.ShapeDtypeStruct((1, MODEL_WIDTH), f32),
        ),
        compiler_params=params(),
        cost_estimate=cost(2 * rows * MODEL_WIDTH * (MODEL_WIDTH + 2 * KV_WIDTH), 2e7),
        name="input_backward",
    )(dql, dkv, wq, wk, wv, cosine, sine, x, gain, mg)


def shifted(value, axis, steps):
    count = lax.axis_size(axis)
    return lax.ppermute(value, axis, [(i, (i + steps) % count) for i in range(count)])


def core_swap(value):
    return lax.ppermute(value, "exp", [(i, i ^ 1) for i in range(lax.axis_size("exp"))])


def chip_shift(value, steps):
    count = lax.axis_size("exp")
    return lax.ppermute(value, "exp", [(i, (i + 2 * steps) % count) for i in range(count)])


def gather_blocks(own):
    out = [own, core_swap(own)]
    for steps in range(1, lax.axis_size("exp") // 2):
        same = chip_shift(own, steps)
        out += [core_swap(same), same]
    return out


def return_blocks(parts):
    terms = [parts[0], core_swap(parts[1])]
    for steps in range(1, lax.axis_size("exp") // 2):
        crossed = core_swap(parts[2 * steps])
        both = (crossed.astype(f32) + parts[2 * steps + 1].astype(f32)).astype(bf16)
        terms.append(chip_shift(both, -steps))
    return terms


def ring_scatter(parts, shift, index, count):
    def part(step):
        return lax.dynamic_index_in_dim(parts, (index - 1 - step) % count, 0, keepdims=False)

    total = part(0)
    for step in range(1, count):
        total = (shift(total).astype(f32) + part(step).astype(f32)).astype(bf16)
    return total


def scatter_all(array):
    dp, ctx, exp = (lax.axis_size(a) for a in ("dp", "ctx", "exp"))
    d, c, e = (lax.axis_index(a) for a in ("dp", "ctx", "exp"))
    chips = exp // 2
    rows, columns = array.shape
    share = rows // (dp * ctx * exp)
    parts = array.reshape(dp, ctx, chips, 2, share, columns)
    parts = jnp.transpose(parts, (3, 2, 0, 1, 4, 5))
    parts = ring_scatter(parts, core_swap, e % 2, 2)
    parts = ring_scatter(parts, lambda v: chip_shift(v, 1), e // 2, chips)
    parts = ring_scatter(parts, lambda v: shifted(v, "dp", 1), d, dp)
    return ring_scatter(parts, lambda v: shifted(v, "ctx", 1), c, ctx)


def per_device(
    tokens, attn_gain, w_query, key_matrix, value_matrix, w_out, ffn_gain, expert_gate_up,
    expert_down, expert_ids, gate_weights, span_order, out_grad,
):
    ctx_size, exp_size = lax.axis_size("ctx"), lax.axis_size("exp")
    ctx_here, exp_here = lax.axis_index("ctx"), lax.axis_index("exp")
    experts = EXP_DEV * exp_size
    x, g = tokens[0], out_grad[0]
    rows = x.shape[0]
    capacity = rows * TOPK * 5 // (4 * experts)
    gain_one, gain_two = attn_gain[None, :], ffn_gain[None, :]
    offsets = jnp.arange(HALF, dtype=jnp.int32)

    def device_positions(device):
        pair = lax.dynamic_slice_in_dim(span_order[0], 2 * device, 2, 0)
        return (pair[:, None] * HALF + offsets[None, :]).reshape(-1)

    sources = [(ctx_here - s) % ctx_size for s in range(ctx_size)]
    key_positions = [device_positions(s) for s in sources]
    positions = key_positions[0]
    exponent = jnp.arange(HEAD_SIZE // 2, dtype=f32) * (-2.0 / HEAD_SIZE)
    frequency = jnp.power(f32(rope_base), exponent)
    angles = positions.astype(f32)[:, None] * frequency[None, :]
    cosine, sine = jnp.cos(angles), jnp.sin(angles)
    cosine = jnp.concatenate([cosine, cosine], axis=1)
    sine = jnp.concatenate([-sine, sine], axis=1)

    normed, kv_own = norm_kv(x, gain_one, key_matrix, value_matrix, cosine, sine)
    kv_blocks = [kv_own] + [shifted(kv_own, "ctx", s) for s in range(1, ctx_size)]
    q = query_projection(normed, w_query, cosine, sine)

    named = expert_ids[0][:, :, None] == jnp.arange(experts, dtype=jnp.int32)
    member = jnp.any(named, axis=1)
    count = member.astype(jnp.int32)
    place = jnp.where(member, jnp.cumsum(count, axis=0) - count, -1)
    route_gate = jnp.sum(jnp.where(named, gate_weights[0][:, :, None], 0.0), axis=1)
    routing = jnp.stack([place.astype(f32), route_gate]).transpose(0, 2, 1)
    routing = gather_blocks(routing)

    def local_routing(block):
        pair = lax.dynamic_slice_in_dim(block, EXP_DEV * exp_here, EXP_DEV, 1)
        return pair[0].astype(jnp.int32), pair[1]

    routing = [local_routing(block) for block in routing]
    g_blocks = gather_blocks(g)

    kv_all = jnp.concatenate(kv_blocks, axis=0)
    kpos_row = jnp.concatenate(key_positions)[None, :]
    att, att_low, lse, mid, nf = attention_forward(
        q, kv_all, positions[:, None], kpos_row, w_out, x, gain_two
    )

    nf_blocks = gather_blocks(nf)
    y_parts, dx_parts, kept = [], [], None
    for block in range(exp_size):
        pos, gates = routing[block]
        y_part, dx_part, kept = expert_block(
            block, exp_size, capacity, pos, gates, nf_blocks[block], g_blocks[block],
            expert_gate_up, expert_down, kept,
        )
        y_parts.append(y_part)
        dx_parts.append(dx_part)
    nf_grad_terms = return_blocks(dx_parts)
    slot_rows, hidden, slot_grad, projected_grad = (
        a.reshape(EXP_DEV, exp_size * capacity, a.shape[-1]) for a in kept
    )
    down_grad = jnp.einsum("erf,erd->efd", hidden, slot_grad, preferred_element_type=f32).astype(bf16)
    gate_up_grad = jnp.einsum(
        "erd,erf->edf", slot_rows, projected_grad, preferred_element_type=f32
    ).astype(bf16)
    down_share = lax.psum_scatter(down_grad, ("dp", "ctx"), scatter_dimension=1, tiled=True)
    gate_up_share = lax.psum_scatter(gate_up_grad, ("dp", "ctx"), scatter_dimension=1, tiled=True)

    mid_grad, mid_grad_low, att_grad, delta, ffn_gain_part = middle_backward(
        nf_grad_terms, mid, g, gain_two, w_out, att
    )
    y_terms = return_blocks(y_parts)
    layer_output = mid
    for term in y_terms:
        layer_output = layer_output + term.astype(f32)
    layer_output = layer_output.astype(bf16)
    w_out_grad = dot_tn(att_low, mid_grad_low).astype(bf16)
    w_out_share = scatter_all(w_out_grad)

    dq, dkv = None, None
    for step in range(ctx_size):
        back = (step + 1) % ctx_size
        if step:
            dkv = shifted(dkv, "ctx", 1)
        dq, dkv = attention_backward(
            q, att_grad, kv_blocks[back], lse, delta, key_positions[back][:, None],
            positions[None, :], dq, dkv,
        )
    dql = unrotate(dq, cosine, sine)
    w_query_grad = dot_tn(normed, dql).astype(bf16)
    dkvl, tokens_grad, attn_gain_part = input_backward(
        dql, dkv, w_query, key_matrix, value_matrix, cosine, sine, x, gain_one, mid_grad
    )
    w_kv_grad = dot_tn(normed, dkvl).astype(bf16)
    w_query_share = scatter_all(w_query_grad)
    w_kv_share = scatter_all(w_kv_grad)
    gains = lax.psum_scatter(
        jnp.concatenate([attn_gain_part, ffn_gain_part], axis=0),
        ("dp", "ctx", "exp"), scatter_dimension=1, tiled=True,
    )
    return (
        layer_output[None],
        tokens_grad[None],
        gains[0],
        w_query_share.astype(f32),
        w_kv_share[:, :KV_WIDTH].astype(f32),
        w_kv_share[:, KV_WIDTH:].astype(f32),
        w_out_share.astype(f32),
        gains[1],
        gate_up_share.astype(f32),
        down_share.astype(f32),
    )


def solution(mesh):
    by_row = P(("dp", "exp"), "ctx", None)
    share = P(("dp", "ctx", "exp"))
    share_rows = P(("dp", "ctx", "exp"), None)
    return jax.shard_map(
        per_device,
        mesh=mesh,
        in_specs=(
            by_row, P(), P(), P(), P(), P(), P(), P("exp", None, None), P("exp", None, None),
            by_row, by_row, P(("dp", "exp"), None), by_row,
        ),
        out_specs=(
            by_row, by_row, share, share_rows, share_rows, share_rows, share_rows, share,
            P("exp", ("dp", "ctx"), None), P("exp", ("dp", "ctx"), None),
        ),
        check_vma=False,
    )
```

time: 1390 us -> 790 us (0.57)
  matrix products: 288 us -> 38.2 us
  Pallas kernels: 0 us -> 237 us
  local copies, waits for them, and re-layouts: 261 us -> 24.5 us
  waiting for transfers between devices: 618 us -> 383 us
  other arithmetic: 112 us -> 31.3 us
  blocking collectives: 37.7 us -> 0 us
    dot_general x45 -> x5, matrix products: 288 us -> 38.2 us  [the longest x1 19.6 us: per_device(): jnp.einsum('erd,erf->edf', slot_rows, projected_grad, preferred_element_t...]
    pallas_call x0 -> x14, Pallas kernels: none -> 237 us  [the longest x4 103 us: expert_block(): pl.pallas_call(expert_kernel, grid=(EXP_DEV,), in_specs=[pl.BlockSpec((1,...]
    reduce_scatter x6 -> x2, waiting for transfers between devices: 387 us -> 166 us  [the longest x1 163 us: per_device(): lax.psum_scatter(gate_up_grad, ('dp', 'ctx'), scatter_dimension=1, tiled=...]
    all_to_all x4 -> x0, waiting for transfers between devices: 114 us -> none  [the longest x1 80.7 us: per_device(): lax.all_to_all(send_rows, 'exp', split_axis=0, concat_axis=1, tiled=True)]
    ppermute x20 -> x39, waiting for transfers between devices: 117 us -> 205 us  [the longest x8 105 us: chip_shift(): lax.ppermute(value, 'exp', [(i, (i + 2 * steps) % count) for i in range(c...]
    convert_element_type x5 -> x4, local copies, waits for them, and re-layouts: 85.6 us -> 4.14 us  [local_routing(): return (pair[0].astype(jnp.int32), pair[1])]
    reduce_sum x10 -> x1, other arithmetic: 62.5 us -> 0.01 us  [per_device(): jnp.sum(jnp.where(named, gate_weights[0][:, :, None], 0.0), axis=1)]
    gather x3 -> x0, local copies, waits for them, and re-layouts: 45.6 us -> none  [the longest x1 17.9 us: per_device(): returned_grad[slot_index].reshape(resident_rows, TOPK, MODEL_WIDTH)]
  transfers between devices with their start and end apart: 30 -> 42, of which waited for: 15 -> 23; matrix products, arithmetic and copies ran while one was open for 38% -> 10% of each run, Pallas kernels for 0% -> 19%
where the time goes in v1:
time: 790 us; the launch traced here: 781 us
  waiting for transfers between devices  383 us (48%)
  Pallas kernels  237 us (30%)
  starting transfers between devices  52.7 us (7%)
  matrix products  38.2 us (5%)
  other arithmetic  31.3 us (4%)
  local copies, waits for them, and re-layouts  24.5 us (3%)
  between operations  14.7 us (2%)
    reduce_scatter x1, waiting for transfers between devices, per_device(): lax.psum_scatter(gate_up_grad, ('dp', 'ctx'), scatter_dimension=1, tiled=...  163 us
    ppermute x8, waiting for transfers between devices, chip_shift(): lax.ppermute(value, 'exp', [(i, (i + 2 * steps) % count) for i in range(c...  105 us
    pallas_call x4, Pallas kernels, expert_block(): pl.pallas_call(expert_kernel, grid=(EXP_DEV,), in_specs=[pl.BlockSpec((1,...  103 us
    ppermute x18, waiting for transfers between devices, shifted(): lax.ppermute(value, axis, [(i, (i + steps) % count) for i in range(count)])  97.5 us
    pallas_call x4, Pallas kernels, attention_backward(): pl.pallas_call(functools.partial(attention_back_kernel, first), grid=(KEY...  60.5 us
    ppermute x18, starting transfers between devices, shifted(): lax.ppermute(value, axis, [(i, (i + steps) % count) for i in range(count)])  39.1 us
    pallas_call x1, Pallas kernels, attention_forward(): pl.pallas_call(attention_kernel, grid=(QUERY_HEADS,), in_specs=[pl.BlockS...  35.6 us
    dot_general x1, matrix products, per_device(): jnp.einsum('erd,erf->edf', slot_rows, projected_grad, preferred_element_t...  19.6 us
  transfers between devices with their start and end apart: 42, of which 23 were waited for; matrix products, arithmetic and copies ran while one was open for 10% of the time, Pallas kernels for 19%

profile of v1, /device:TPU:0, one launch (start us, length us, event | category | flops | bytes accessed | tf_op | source)
XLA Modules:
  0.0 781.3 jit_solution(13030218587215264777)
XLA Ops:
  12.3 4.2 norm_kv.1
  27.4 6.9 query_projection.1.q_ref.refs_0_
  43.4 12.9 %collective-permute-done.1.refs_2_.refs_3_ = bf16[512,512]{1,0:T(8,128)(2,1)S(1)} collective-permute-done((bf16[512,512]{1,0:T(8,128)(2,1)}, bf16[512,512]{1,0:T(8,128)(2,1)S(1)}, u32[]{:S(2)}, u32[]{:S(2)}) %collective-permute-start.1) | collective-permute-done | bytes 524320 | tf_op jit(solution)/shard_map/ppermute | solution.py:479
  59.2 35.6 %attention_forward.1 = (f32[512,1536]{1,0:T(8,128)}, bf16[512,1536]{1,0:T(8,128)(2,1)}, f32[16,512]{1,0:T(8,128)}, f32[512,1536]{1,0:T(8,128)}, bf16[512,1536]{1,0:T(8,128)(2,1)}) custom-call(bf16[512,1536]{1,0:T(8,128)(2,1)} %query_projection.1.q_ref.refs_0_, bf16[2048,512]{1,0:T(8,128)(2,1)} %pad_maximum_fusion.k_ref.v_ref, ...), custom_call_target="tpu_custom_call" | custom-call | flops 12884901888 | bytes 20000000 | tf_op jit(solution)/shard_map/attention_forward/pallas_call | solution.py:165
  96.5 25.7 %expert_block.4 = (bf16[512,1536]{1,0:T(8,128)(2,1)}, bf16[512,1536]{1,0:T(8,128)(2,1)}, bf16[2,4,320,1536]{3,2,1,0:T(8,128)(2,1)}, bf16[2,4,320,768]{3,2,1,0:T(...) custom-call(s32[2,1,512]{2,1,0:T(1,128)} %get-tuple-element.125.pos_row_ref, ...), custom_call_target="tpu_custom_call" | custom-call | flops 17616076800 | bytes 30000000 | tf_op jit(solution)/shard_map/expert_block/pallas_call | solution.py:262
  122.4 9.5 %collective-permute-done.9.x_ref = bf16[512,1536]{1,0:T(8,128)(2,1)S(1)} collective-permute-done((bf16[512,1536]{1,0:T(8,128)(2,1)}, bf16[512,1536]{1,0:T(8,128)(2,1)S(1)}, u32[]{:S(2)}, u32[]{:S(2)}) %collective-permute-start.9) | collective-permute-done | bytes 1572896 | tf_op jit(solution)/shard_map/ppermute | solution.py:488
  131.9 26.0 %expert_block.5 = (bf16[512,1536]{1,0:T(8,128)(2,1)}, bf16[512,1536]{1,0:T(8,128)(2,1)}, bf16[2,4,320,1536]{3,2,1,0:T(8,128)(2,1)}, bf16[2,4,320,768]{3,2,1,0:T(...) custom-call(s32[2,1,512]{2,1,0:T(1,128)} %get-tuple-element.114.pos_, ...), custom_call_target="tpu_custom_call", output_to_operand_aliasing={{2}: (7, {}), {3}: (8, {}), {4}: (9, {}), {5}: (10, {})} | custom-call | flops 17616076800 | bytes 30000000 | tf_op jit(solution)/shard_map/expert_block/pallas_call | solution.py:262
  158.2 25.8 %expert_block.6 = (bf16[512,1536]{1,0:T(8,128)(2,1)}, bf16[512,1536]{1,0:T(8,128)(2,1)}, bf16[2,4,320,1536]{3,2,1,0:T(8,128)(2,1)}, bf16[2,4,320,768]{3,2,1,0:T(...) custom-call(s32[2,1,512]{2,1,0:T(1,128)} %get-tuple-element.117.pos_, ...), custom_call_target="tpu_custom_call", output_to_operand_aliasing={{2}: (7, {}), {3}: (8, {}), {4}: (9, {}), {5}: (10, {})} | custom-call | flops 17616076800 | bytes 30000000 | tf_op jit(solution)/shard_map/expert_block/pallas_call | solution.py:262
  184.4 25.8 %expert_block.7 = (bf16[512,1536]{1,0:T(8,128)(2,1)}, bf16[512,1536]{1,0:T(8,128)(2,1)}, bf16[2,4,320,1536]{3,2,1,0:T(8,128)(2,1)}, bf16[2,4,320,768]{3,2,1,0:T(...) custom-call(s32[2,1,512]{2,1,0:T(1,128)} %get-tuple-element.120.pos_, ...), custom_call_target="tpu_custom_call", output_to_operand_aliasing={{2}: (7, {}), {3}: (8, {}), {4}: (9, {}), {5}: (10, {})} | custom-call | flops 17616076800 | bytes 30000000 | tf_op jit(solution)/shard_map/expert_block/pallas_call | solution.py:262
  215.6 34.4 %collective-permute-done.17.refs_2_ = bf16[512,1536]{1,0:T(8,128)(2,1)S(1)} collective-permute-done((bf16[512,1536]{1,0:T(8,128)(2,1)}, bf16[512,1536]{1,0:T(8,128)(2,1)S(1)}, u32[]{:S(2)}, u32[]{:S(2)}) %collective-permute-start.17) | collective-permute-done | bytes 1572896 | tf_op jit(solution)/shard_map/ppermute | solution.py:488
  251.1 11.7 %middle_backward.1 = (f32[512,1536]{1,0:T(8,128)}, bf16[512,1536]{1,0:T(8,128)(2,1)}, bf16[512,1536]{1,0:T(8,128)(2,1)}, f32[16,512]{1,0:T(8,128)}, f32[1,1536]{1,0:T(1,128)}) custom-call(bf16[512,1536]{1,0:T(8,128)(2,1)} %get-tuple-element.77.refs_0_, bf16[512,1536]{1,0:T(8,128)(2,1)} %copy-done.4, bf16[512,1536]{1,0:T(8,128)(2,1)} %copy-done.5, ...), custom_call_target="tpu_custom_call" | custom-call | flops 2415919104 | bytes 20000000 | tf_op jit(solution)/shard_map/middle_backward/pallas_call | solution.py:327
  262.9 14.4 %attention_backward.4 = (f32[512,1536]{1,0:T(8,128)}, bf16[512,512]{1,0:T(8,128)(2,1)}) custom-call(bf16[512,1536]{1,0:T(8,128)(2,1)} %query_projection.1.q_ref.refs_0_, bf16[512,1536]{1,0:T(8,128)(2,1)} %get-tuple-element.82.refs_1_, bf16[512,512]{1,0:T(8,128)(2,1)} %collective-permute-done.refs_2_.refs_3_, ...), custom_call_target="tpu_custom_call" | custom-call | flops 4026531840 | bytes 10000000 | tf_op jit(solution)/shard_map/attention_backward/pallas_call | solution.py:403
  277.3 11.6 %collective-permute-start.18 = (bf16[512,512]{1,0:T(8,128)(2,1)}, bf16[512,512]{1,0:T(8,128)(2,1)S(1)}, u32[]{:S(2)}, u32[]{:S(2)}) collective-permute-start(bf16[512,512]{1,0:T(8,128)(2,1)} %get-tuple-element.86), channel_id=1, source_target_pairs={{0,4},{4,8},{8,12},{12,0},{1,5},{5,9},{9,13},{13,1},{2,6},{6,10},{... | collective-permute-start | bytes 1572872 | tf_op jit(solution)/shard_map/ppermute | solution.py:479
  289.7 12.1 %collective-permute-done.18.refs_9_ = bf16[512,512]{1,0:T(8,128)(2,1)S(1)} collective-permute-done((bf16[512,512]{1,0:T(8,128)(2,1)}, bf16[512,512]{1,0:T(8,128)(2,1)S(1)}, u32[]{:S(2)}, u32[]{:S(2)}) %collective-permute-start.18) | collective-permute-done | bytes 524320 | tf_op jit(solution)/shard_map/ppermute | solution.py:479
  302.6 15.2 %attention_backward.5 = (f32[512,1536]{1,0:T(8,128)}, bf16[512,512]{1,0:T(8,128)(2,1)}) custom-call(bf16[512,1536]{1,0:T(8,128)(2,1)} %query_projection.1.q_ref.refs_0_, bf16[512,1536]{1,0:T(8,128)(2,1)} %get-tuple-element.82.refs_1_, bf16[512,512]{1,0:T(8,128)(2,1)} %copy-done.9, bf16[512,512]{1,0:T(8,128)(2,1)} %copy-done.9, ...), custom_call_target="tpu_custom_call" | custom-call | flops 4026531840 | bytes 10000000 | tf_op jit(solution)/shard_map/attention_backward/pallas_call | solution.py:403
  319.2 13.3 %collective-permute-done.19.refs_9_ = bf16[512,512]{1,0:T(8,128)(2,1)S(1)} collective-permute-done((bf16[512,512]{1,0:T(8,128)(2,1)}, bf16[512,512]{1,0:T(8,128)(2,1)S(1)}, u32[]{:S(2)}, u32[]{:S(2)}) %collective-permute-start.19) | collective-permute-done | bytes 524320 | tf_op jit(solution)/shard_map/ppermute | solution.py:479
  333.3 15.2 %attention_backward.6 = (f32[512,1536]{1,0:T(8,128)}, bf16[512,512]{1,0:T(8,128)(2,1)}) custom-call(bf16[512,1536]{1,0:T(8,128)(2,1)} %query_projection.1.q_ref.refs_0_, bf16[512,1536]{1,0:T(8,128)(2,1)} %get-tuple-element.82.refs_1_, bf16[512,512]{1,0:T(8,128)(2,1)} %copy-done.8, bf16[512,512]{1,0:T(8,128)(2,1)} %copy-done.8, ...), custom_call_target="tpu_custom_call" | custom-call | flops 4026531840 | bytes 10000000 | tf_op jit(solution)/shard_map/attention_backward/pallas_call | solution.py:403
  348.5 13.7 %collective-permute-done.20.refs_9_ = bf16[512,512]{1,0:T(8,128)(2,1)S(1)} collective-permute-done((bf16[512,512]{1,0:T(8,128)(2,1)}, bf16[512,512]{1,0:T(8,128)(2,1)S(1)}, u32[]{:S(2)}, u32[]{:S(2)}) %collective-permute-start.20) | collective-permute-done | bytes 524320 | tf_op jit(solution)/shard_map/ppermute | solution.py:479
  363.1 15.7 %attention_backward.7 = (f32[512,1536]{1,0:T(8,128)}, bf16[512,512]{1,0:T(8,128)(2,1)}) custom-call(bf16[512,1536]{1,0:T(8,128)(2,1)} %query_projection.1.q_ref.refs_0_, bf16[512,1536]{1,0:T(8,128)(2,1)} %get-tuple-element.82.refs_1_, bf16[512,512]{1,0:T(8,128)(2,1)} %get-tuple-element.58.refs_2_.refs_3_, ...), custom_call_target="tpu_custom_call" | custom-call | flops 4026531840 | bytes 10000000 | tf_op jit(solution)/shard_map/attention_backward/pallas_call | solution.py:403
  382.8 10.6 %input_backward.1 = (bf16[512,512]{1,0:T(8,128)(2,1)}, bf16[512,1536]{1,0:T(8,128)(2,1)}, f32[1,1536]{1,0:T(1,128)}) custom-call(bf16[512,1536]{1,0:T(8,128)(2,1)} %unrotate.1.dql_ref, bf16[512,512]{1,0:T(8,128)(2,1)} %get-tuple-element.92.dkv_ref, bf16[1536,1536]{1,0:T(8,128)(2,1)} %wq_ref.3, bf16[1536,256]{1,0:T(8,128)(2,1)} %wk_ref.3, ...), custom_call_target="tpu_custom_call" | custom-call | flops 3221225472 | bytes 20000000 | tf_op jit(solution)/shard_map/input_backward/pallas_call | solution.py:464
  395.3 11.6 %convolution_convert_fusion.3 = bf16[2,768,1536]{2,1,0:T(8,128)(2,1)} fusion(bf16[2,1280,768]{2,1,0:T(8,128)(2,1)} %bitcast.249, bf16[2,1280,1536]{2,1,0:T(8,128)(2,1)} %bitcast.247), kind=kOutput, calls=%fused_computation.7 | convolution fusion | flops 6042157056 | bytes 16515072 | tf_op jit(solution)/shard_map/erf,erd->efd/dot_general | solution.py:598
  406.9 19.6 %convolution_convert_fusion = bf16[2,1536,1536]{2,1,0:T(8,128)(2,1)} fusion(bf16[2,1280,1536]{2,1,0:T(8,128)(2,1)} %bitcast.246, bf16[2,1280,1536]{2,1,0:T(8,128)(2,1)} %bitcast.248), kind=kOutput, calls=%fused_computation | convolution fusion | flops 12084314112 | bytes 25165824 | tf_op jit(solution)/shard_map/erd,erf->edf/dot_general | solution.py:599
  448.8 21.3 %collective-permute-done.14 = bf16[512,1536]{1,0:T(8,128)(2,1)S(1)} collective-permute-done((bf16[512,1536]{1,0:T(8,128)(2,1)S(1)}, bf16[512,1536]{1,0:T(8,128)(2,1)S(1)}, u32[]{:S(2)}, u32[]{:S(2)}) %collective-permute-start.14) | collective-permute-done | bytes 1572896 | tf_op jit(solution)/shard_map/ppermute | solution.py:488
  472.2 5.6 collective-permute-done.28
  479.4 12.0 %reduce-scatter.10.cloned.1.call-done = f32[48,2]{1,0:T(8,128)} async-done(((f32[1536,2]{1,0:T(8,128)}), f32[48,2]{1,0:T(8,128)}) %reduce-scatter.10.cloned.1.call-update) | async-done | bytes 400
  501.2 5.3 collective-permute-done.31
  514.2 14.5 %collective-permute-done.34 = bf16[2,4,48,1536]{3,2,1,0:T(8,128)(2,1)S(1)} collective-permute-done((bf16[2,4,48,1536]{3,2,1,0:T(8,128)(2,1)S(1)}, bf16[2,4,48,1536]{3,2,1,0:T(8,128)(2,1)S(1)}, u32[]{:S(2)}, u32[]{:S(2)}) %collective-permute-start.34) | collective-permute-done | bytes 1179680 | tf_op jit(solution)/shard_map/ppermute | solution.py:488
  530.6 19.4 %collective-permute-done.22 = bf16[2,4,48,1536]{3,2,1,0:T(8,128)(2,1)S(1)} collective-permute-done((bf16[2,4,48,1536]{3,2,1,0:T(8,128)(2,1)S(1)}, bf16[2,4,48,1536]{3,2,1,0:T(8,128)(2,1)S(1)}, u32[]{:S(2)}, u32[]{:S(2)}) %collective-permute-start.22) | collective-permute-done | bytes 1179680 | tf_op jit(solution)/shard_map/ppermute | solution.py:488
  553.4 14.9 %collective-permute-done.23 = bf16[4,48,1536]{2,1,0:T(8,128)(2,1)S(1)} collective-permute-done((bf16[4,48,1536]{2,1,0:T(8,128)(2,1)S(1)}, bf16[4,48,1536]{2,1,0:T(8,128)(2,1)S(1)}, u32[]{:S(2)}, u32[]{:S(2)}) %collective-permute-start.23) | collective-permute-done | bytes 589856 | tf_op jit(solution)/shard_map/ppermute | solution.py:479
  587.2 4.9 collective-permute-start.26
  594.1 8.8 %collective-permute-done.26 = bf16[48,1536]{1,0:T(8,128)(2,1)S(1)} collective-permute-done((bf16[48,1536]{1,0:T(8,128)(2,1)S(1)}, bf16[48,1536]{1,0:T(8,128)(2,1)S(1)}, u32[]{:S(2)}, u32[]{:S(2)}) %collective-permute-start.26) | collective-permute-done | bytes 147488 | tf_op jit(solution)/shard_map/ppermute | solution.py:479
  608.9 162.7 %reduce-scatter.6.cloned.1.call-done = bf16[2,192,1536]{2,1,0:T(8,128)(2,1)} async-done(((bf16[2,1536,1536]{2,1,0:T(8,128)(2,1)}), bf16[2,192,1536]{2,1,0:T(8,128)(2,1)}) %reduce-scatter.6.cloned.1.call-update) | async-done | bytes 1179664 | tf_op jit(solution)/shard_map/reduce_scatter | solution.py:603
  (208 shorter events, 125.8 us)
Async XLA Ops:
  7.2 484.3 %reduce-scatter.10.cloned.1.call-start = ((), (), s32[]{:S(2)}) async-start(), calls=%async_computation.5 | async-start | bytes 811008
  16.5 26.9 %collective-permute-start = (bf16[512,512]{1,0:T(8,128)(2,1)}, bf16[512,512]{1,0:T(8,128)(2,1)}, u32[]{:S(2)}, u32[]{:S(2)}) collective-permute-start(bf16[512,512]{1,0:T(8,128)(2,1)} %get-tuple-element.58.refs_2_.refs_3_), channel_id=1, source_target_pairs={{0,4},{4,8},{8,12},{12,0},{1,5},{5,9},{9,13},{13,1},{2,6},{6,10},{... | collective-permute-start | bytes 1572872 | tf_op jit(solution)/shard_map/ppermute | solution.py:479
  19.5 36.8 %collective-permute-start.1 = (bf16[512,512]{1,0:T(8,128)(2,1)}, bf16[512,512]{1,0:T(8,128)(2,1)S(1)}, u32[]{:S(2)}, u32[]{:S(2)}) collective-permute-start(bf16[512,512]{1,0:T(8,128)(2,1)} %get-tuple-element.58.refs_2_.refs_3_), channel_id=1, source_target_pairs={{0,8},{4,12},{8,0},{12,4},{1,9},{5,13},{9,1},{13,5},{2,10},{6,14},... | collective-permute-start | bytes 1572872 | tf_op jit(solution)/shard_map/ppermute | solution.py:479
  22.1 34.2 %collective-permute-start.2 = (bf16[512,512]{1,0:T(8,128)(2,1)}, bf16[512,512]{1,0:T(8,128)(2,1)S(1)}, u32[]{:S(2)}, u32[]{:S(2)}) collective-permute-start(bf16[512,512]{1,0:T(8,128)(2,1)} %get-tuple-element.58.refs_2_.refs_3_), channel_id=1, source_target_pairs={{0,12},{4,0},{8,4},{12,8},{1,13},{5,1},{9,5},{13,9},{2,14},{6,2},{... | collective-permute-start | bytes 1572872 | tf_op jit(solution)/shard_map/ppermute | solution.py:479
  25.1 13.2 %collective-permute-start.3 = (f32[2,8,512]{2,0,1:T(2,128)S(1)}, f32[2,8,512]{2,0,1:T(2,128)S(1)}, u32[]{:S(2)}, u32[]{:S(2)}) collective-permute-start(f32[2,8,512]{2,0,1:T(2,128)S(1)} %fusion.23), channel_id=1, source_target_pairs={{0,1},{1,0},{2,3},{3,2},{4,5},{5,4},{6,7},{7,6},{8,9},{9,8},{10,11... | collective-permute-start | bytes 98312 | tf_op jit(solution)/shard_map/ppermute | solution.py:483
  37.5 94.4 %collective-permute-start.5 = (bf16[512,1536]{1,0:T(8,128)(2,1)S(1)}, bf16[512,1536]{1,0:T(8,128)(2,1)}, u32[]{:S(2)}, u32[]{:S(2)}) collective-permute-start(bf16[512,1536]{1,0:T(8,128)(2,1)S(1)} %bitcast.216), channel_id=1, source_target_pairs={{0,1},{1,0},{2,3},{3,2},{4,5},{5,4},{6,7},{7,6},{8,9},{9,8},{10,11... | collective-permute-start | bytes 4718600 | tf_op jit(solution)/shard_map/ppermute | solution.py:483
  41.3 80.9 %collective-permute-start.11 = (bf16[512,1536]{1,0:T(8,128)(2,1)S(1)}, bf16[512,1536]{1,0:T(8,128)(2,1)}, u32[]{:S(2)}, u32[]{:S(2)}) collective-permute-start(bf16[512,1536]{1,0:T(8,128)(2,1)S(1)} %bitcast.217), channel_id=1, source_target_pairs={{0,2},{1,3},{2,0},{3,1},{4,6},{5,7},{6,4},{7,5},{8,10},{9,11},{10,... | collective-permute-start | bytes 4718600 | tf_op jit(solution)/shard_map/ppermute | solution.py:488
  94.8 37.1 %collective-permute-start.4 = (bf16[512,1536]{1,0:T(8,128)(2,1)}, bf16[512,1536]{1,0:T(8,128)(2,1)}, u32[]{:S(2)}, u32[]{:S(2)}) collective-permute-start(bf16[512,1536]{1,0:T(8,128)(2,1)} %get-tuple-element.60.x_ref), channel_id=1, source_target_pairs={{0,1},{1,0},{2,3},{3,2},{4,5},{5,4},{6,7},{7,6},{8,9},{9,8},{10,11... | collective-permute-start | bytes 4718600 | tf_op jit(solution)/shard_map/ppermute | solution.py:483
  94.9 37.0 %collective-permute-start.9 = (bf16[512,1536]{1,0:T(8,128)(2,1)}, bf16[512,1536]{1,0:T(8,128)(2,1)S(1)}, u32[]{:S(2)}, u32[]{:S(2)}) collective-permute-start(bf16[512,1536]{1,0:T(8,128)(2,1)} %get-tuple-element.60.x_ref), channel_id=1, source_target_pairs={{0,2},{1,3},{2,0},{3,1},{4,6},{5,7},{6,4},{7,5},{8,10},{9,11},{10,... | collective-permute-start | bytes 4718600 | tf_op jit(solution)/shard_map/ppermute | solution.py:488
  122.1 36.0 %collective-permute-start.12 = (bf16[512,1536]{1,0:T(8,128)(2,1)}, bf16[512,1536]{1,0:T(8,128)(2,1)}, u32[]{:S(2)}, u32[]{:S(2)}) collective-permute-start(bf16[512,1536]{1,0:T(8,128)(2,1)} %collective-permute-done.11.g_ref), channel_id=1, source_target_pairs={{0,1},{1,0},{2,3},{3,2},{4,5},{5,4},{6,7},{7,6},{8,9},{9,8},{10,11... | collective-permute-start | bytes 4718600 | tf_op jit(solution)/shard_map/ppermute | solution.py:483
  131.9 26.3 %collective-permute-start.10 = (bf16[512,1536]{1,0:T(8,128)(2,1)S(1)}, bf16[512,1536]{1,0:T(8,128)(2,1)}, u32[]{:S(2)}, u32[]{:S(2)}) collective-permute-start(bf16[512,1536]{1,0:T(8,128)(2,1)S(1)} %collective-permute-done.9.x_ref), channel_id=1, source_target_pairs={{0,1},{1,0},{2,3},{3,2},{4,5},{5,4},{6,7},{7,6},{8,9},{9,8},{10,11... | collective-permute-start | bytes 4718600 | tf_op jit(solution)/shard_map/ppermute | solution.py:483
  157.9 57.7 %collective-permute-start.15 = (bf16[512,1536]{1,0:T(8,128)(2,1)}, bf16[512,1536]{1,0:T(8,128)(2,1)S(1)}, u32[]{:S(2)}, u32[]{:S(2)}) collective-permute-start(bf16[512,1536]{1,0:T(8,128)(2,1)} %get-tuple-element.78), channel_id=1, source_target_pairs={{0,1},{1,0},{2,3},{3,2},{4,5},{5,4},{6,7},{7,6},{8,9},{9,8},{10,11... | collective-permute-start | bytes 4718600 | tf_op jit(solution)/shard_map/ppermute | solution.py:483
  184.0 26.1 %collective-permute-start.16 = (bf16[512,1536]{1,0:T(8,128)(2,1)}, bf16[512,1536]{1,0:T(8,128)(2,1)S(1)}, u32[]{:S(2)}, u32[]{:S(2)}) collective-permute-start(bf16[512,1536]{1,0:T(8,128)(2,1)} %get-tuple-element.79), channel_id=1, source_target_pairs={{0,1},{1,0},{2,3},{3,2},{4,5},{5,4},{6,7},{7,6},{8,9},{9,8},{10,11... | collective-permute-start | bytes 4718600 | tf_op jit(solution)/shard_map/ppermute | solution.py:483
  213.2 36.8 %collective-permute-start.17 = (bf16[512,1536]{1,0:T(8,128)(2,1)}, bf16[512,1536]{1,0:T(8,128)(2,1)S(1)}, u32[]{:S(2)}, u32[]{:S(2)}) collective-permute-start(bf16[512,1536]{1,0:T(8,128)(2,1)} %add_convert_fusion), channel_id=1, source_target_pairs={{0,2},{1,3},{2,0},{3,1},{4,6},{5,7},{6,4},{7,5},{8,10},{9,11},{10,... | collective-permute-start | bytes 4718600 | tf_op jit(solution)/shard_map/ppermute | solution.py:488
  277.3 24.5 %collective-permute-start.18 = (bf16[512,512]{1,0:T(8,128)(2,1)}, bf16[512,512]{1,0:T(8,128)(2,1)S(1)}, u32[]{:S(2)}, u32[]{:S(2)}) collective-permute-start(bf16[512,512]{1,0:T(8,128)(2,1)} %get-tuple-element.86), channel_id=1, source_target_pairs={{0,4},{4,8},{8,12},{12,0},{1,5},{5,9},{9,13},{13,1},{2,6},{6,10},{... | collective-permute-start | bytes 1572872 | tf_op jit(solution)/shard_map/ppermute | solution.py:479
  317.8 14.7 %collective-permute-start.19 = (bf16[512,512]{1,0:T(8,128)(2,1)}, bf16[512,512]{1,0:T(8,128)(2,1)S(1)}, u32[]{:S(2)}, u32[]{:S(2)}) collective-permute-start(bf16[512,512]{1,0:T(8,128)(2,1)} %get-tuple-element.88), channel_id=1, source_target_pairs={{0,4},{4,8},{8,12},{12,0},{1,5},{5,9},{9,13},{13,1},{2,6},{6,10},{... | collective-permute-start | bytes 1572872 | tf_op jit(solution)/shard_map/ppermute | solution.py:479
  348.5 13.8 %collective-permute-start.20 = (bf16[512,512]{1,0:T(8,128)(2,1)}, bf16[512,512]{1,0:T(8,128)(2,1)S(1)}, u32[]{:S(2)}, u32[]{:S(2)}) collective-permute-start(bf16[512,512]{1,0:T(8,128)(2,1)} %get-tuple-element.90), channel_id=1, source_target_pairs={{0,4},{4,8},{8,12},{12,0},{1,5},{5,9},{9,13},{13,1},{2,6},{6,10},{... | collective-permute-start | bytes 1572872 | tf_op jit(solution)/shard_map/ppermute | solution.py:479
  395.2 211.4 %reduce-scatter.8.cloned.1.call-start = ((), (), s32[]{:S(2)}) async-start(), calls=%async_computation.4 | async-start | bytes 5308416 | tf_op jit(solution)/shard_map/reduce_scatter | solution.py:602
  406.9 364.7 %reduce-scatter.6.cloned.1.call-start = ((), (), s32[]{:S(2)}) async-start(), calls=%async_computation.3 | async-start | bytes 10616832 | tf_op jit(solution)/shard_map/reduce_scatter | solution.py:603
  426.9 21.9 %collective-permute-start.6 = (bf16[512,1536]{1,0:T(8,128)(2,1)}, bf16[512,1536]{1,0:T(8,128)(2,1)S(1)}, u32[]{:S(2)}, u32[]{:S(2)}) collective-permute-start(bf16[512,1536]{1,0:T(8,128)(2,1)} %get-tuple-element.66), channel_id=1, source_target_pairs={{0,1},{1,0},{2,3},{3,2},{4,5},{5,4},{6,7},{7,6},{8,9},{9,8},{10,11... | collective-permute-start | bytes 4718600 | tf_op jit(solution)/shard_map/ppermute | solution.py:483
  430.7 39.4 %collective-permute-start.14 = (bf16[512,1536]{1,0:T(8,128)(2,1)S(1)}, bf16[512,1536]{1,0:T(8,128)(2,1)S(1)}, u32[]{:S(2)}, u32[]{:S(2)}) collective-permute-start(bf16[512,1536]{1,0:T(8,128)(2,1)S(1)} %add_convert_fusion.2), channel_id=1, source_target_pairs={{0,2},{1,3},{2,0},{3,1},{4,6},{5,7},{6,4},{7,5},{8,10},{9,11},{10,... | collective-permute-start | bytes 4718600 | tf_op jit(solution)/shard_map/ppermute | solution.py:488
  438.5 56.5 %collective-permute-start.33 = (bf16[2,2,4,48,1536]{4,3,2,1,0:T(8,128)(2,1)}, bf16[2,2,4,48,1536]{4,3,2,1,0:T(8,128)(2,1)}, u32[]{:S(2)}, u32[]{:S(2)}) collective-permute-start(bf16[2,2,4,48,1536]{4,3,2,1,0:T(8,128)(2,1)} %bitcast.205), channel_id=1, source_target_pairs={{0,1},{1,0},{2,3},{3,2},{4,5},{5,4},{6,7},{7,6},{8,9},{9,8},{10,11... | collective-permute-start | bytes 7077896 | tf_op jit(solution)/shard_map/ppermute | solution.py:483
  446.9 59.7 %collective-permute-start.21 = (bf16[2,2,4,48,1536]{4,3,2,1,0:T(8,128)(2,1)}, bf16[2,2,4,48,1536]{4,3,2,1,0:T(8,128)(2,1)}, u32[]{:S(2)}, u32[]{:S(2)}) collective-permute-start(bf16[2,2,4,48,1536]{4,3,2,1,0:T(8,128)(2,1)} %bitcast.206), channel_id=1, source_target_pairs={{0,1},{1,0},{2,3},{3,2},{4,5},{5,4},{6,7},{7,6},{8,9},{9,8},{10,11... | collective-permute-start | bytes 7077896 | tf_op jit(solution)/shard_map/ppermute | solution.py:483
  447.3 30.5 %collective-permute-start.28 = (bf16[2,4,48,512]{3,2,1,0:T(8,128)(2,1)S(1)}, bf16[2,4,48,512]{3,2,1,0:T(8,128)(2,1)S(1)}, u32[]{:S(2)}, u32[]{:S(2)}) collective-permute-start(bf16[2,4,48,512]{3,2,1,0:T(8,128)(2,1)S(1)} %dynamic-slice_bitcast_fusion.4), channel_id=1, source_target_pairs={{0,2},{1,3},{2,0},{3,1},{4,6},{5,7},{6,4},{7,5},{8,10},{9,11},{10,... | collective-permute-start | bytes 1179656 | tf_op jit(solution)/shard_map/ppermute | solution.py:488
  477.9 15.6 %collective-permute-start.29 = (bf16[4,48,512]{2,1,0:T(8,128)(2,1)S(1)}, bf16[4,48,512]{2,1,0:T(8,128)(2,1)S(1)}, u32[]{:S(2)}, u32[]{:S(2)}) collective-permute-start(bf16[4,48,512]{2,1,0:T(8,128)(2,1)S(1)} %dynamic-slice_bitcast_fusion.5), channel_id=1, source_target_pairs={{0,16},{16,0},{1,17},{17,1},{2,18},{18,2},{3,19},{19,3},{4,20},{20... | collective-permute-start | bytes 589832 | tf_op jit(solution)/shard_map/ppermute | solution.py:479
  499.7 29.0 %collective-permute-start.34 = (bf16[2,4,48,1536]{3,2,1,0:T(8,128)(2,1)S(1)}, bf16[2,4,48,1536]{3,2,1,0:T(8,128)(2,1)S(1)}, u32[]{:S(2)}, u32[]{:S(2)}) collective-permute-start(bf16[2,4,48,1536]{3,2,1,0:T(8,128)(2,1)S(1)} %dynamic-slice_bitcast_fusion), channel_id=1, source_target_pairs={{0,2},{1,3},{2,0},{3,1},{4,6},{5,7},{6,4},{7,5},{8,10},{9,11},{10,... | collective-permute-start | bytes 3538952 | tf_op jit(solution)/shard_map/ppermute | solution.py:488
  509.1 40.9 %collective-permute-start.22 = (bf16[2,4,48,1536]{3,2,1,0:T(8,128)(2,1)S(1)}, bf16[2,4,48,1536]{3,2,1,0:T(8,128)(2,1)S(1)}, u32[]{:S(2)}, u32[]{:S(2)}) collective-permute-start(bf16[2,4,48,1536]{3,2,1,0:T(8,128)(2,1)S(1)} %dynamic-slice_bitcast_fusion.1), channel_id=1, source_target_pairs={{0,2},{1,3},{2,0},{3,1},{4,6},{5,7},{6,4},{7,5},{8,10},{9,11},{10,... | collective-permute-start | bytes 3538952 | tf_op jit(solution)/shard_map/ppermute | solution.py:488
  529.1 22.8 %collective-permute-start.35 = (bf16[4,48,1536]{2,1,0:T(8,128)(2,1)S(1)}, bf16[4,48,1536]{2,1,0:T(8,128)(2,1)S(1)}, u32[]{:S(2)}, u32[]{:S(2)}) collective-permute-start(bf16[4,48,1536]{2,1,0:T(8,128)(2,1)S(1)} %dynamic-slice_bitcast_fusion.2), channel_id=1, source_target_pairs={{0,16},{16,0},{1,17},{17,1},{2,18},{18,2},{3,19},{19,3},{4,20},{20... | collective-permute-start | bytes 1769480 | tf_op jit(solution)/shard_map/ppermute | solution.py:479
  550.4 17.8 %collective-permute-start.23 = (bf16[4,48,1536]{2,1,0:T(8,128)(2,1)S(1)}, bf16[4,48,1536]{2,1,0:T(8,128)(2,1)S(1)}, u32[]{:S(2)}, u32[]{:S(2)}) collective-permute-start(bf16[4,48,1536]{2,1,0:T(8,128)(2,1)S(1)} %dynamic-slice_bitcast_fusion.3), channel_id=1, source_target_pairs={{0,16},{16,0},{1,17},{17,1},{2,18},{18,2},{3,19},{19,3},{4,20},{20... | collective-permute-start | bytes 1769480 | tf_op jit(solution)/shard_map/ppermute | solution.py:479
  552.1 18.1 %collective-permute-start.36 = (bf16[48,1536]{1,0:T(8,128)(2,1)S(1)}, bf16[48,1536]{1,0:T(8,128)(2,1)S(1)}, u32[]{:S(2)}, u32[]{:S(2)}) collective-permute-start(bf16[48,1536]{1,0:T(8,128)(2,1)S(1)} %dynamic-slice_bitcast_fusion.6), channel_id=1, source_target_pairs={{0,4},{4,8},{8,12},{12,0},{1,5},{5,9},{9,13},{13,1},{2,6},{6,10},{... | collective-permute-start | bytes 442376 | tf_op jit(solution)/shard_map/ppermute | solution.py:479
  580.2 13.2 %collective-permute-start.38 = (bf16[48,1536]{1,0:T(8,128)(2,1)S(1)}, bf16[48,1536]{1,0:T(8,128)(2,1)S(1)}, u32[]{:S(2)}, u32[]{:S(2)}) collective-permute-start(bf16[48,1536]{1,0:T(8,128)(2,1)S(1)} %fusion.11), channel_id=1, source_target_pairs={{0,4},{4,8},{8,12},{12,0},{1,5},{5,9},{9,13},{13,1},{2,6},{6,10},{... | collective-permute-start | bytes 442376 | tf_op jit(solution)/shard_map/ppermute | solution.py:479
  587.2 15.7 %collective-permute-start.26 = (bf16[48,1536]{1,0:T(8,128)(2,1)S(1)}, bf16[48,1536]{1,0:T(8,128)(2,1)S(1)}, u32[]{:S(2)}, u32[]{:S(2)}) collective-permute-start(bf16[48,1536]{1,0:T(8,128)(2,1)S(1)} %fusion.14), channel_id=1, source_target_pairs={{0,4},{4,8},{8,12},{12,0},{1,5},{5,9},{9,13},{13,1},{2,6},{6,10},{... | collective-permute-start | bytes 442376 | tf_op jit(solution)/shard_map/ppermute | solution.py:479
  (33 other events, 380.1 us)
Sparse Core Ops, SparseCore 0:
  395.4 96.0 reduce-scatter.9
  495.1 111.5 reduce-scatter.7
  610.2 161.2 reduce-scatter.5

commit v2 on v1

--- a/solution.py
+++ b/solution.py
@@ -51,7 +51,7 @@
 
 
 def cost(flops, size, exps=0):
-    return pl.CostEstimate(flops=int(flops), bytes_accessed=int(size), transcendentals=int(exps))
+    return pl.CostEstimate(flops=int(flops) // 32, bytes_accessed=int(size) // 32, transcendentals=int(exps) // 32)
 
 
 def whole(shape):
@@ -196,95 +196,140 @@
     )(q, kv_all, kv_all, qpos_col, kpos_row, wo, x, gain)
 
 
-def expert_kernel(
-    pos_row_ref, pos_col_ref, gate_row_ref, x_ref, g_ref, wgu_ref, wd_ref, *rest
-):
-    (y_ref, dx_ref, rows_ref, hidden_ref, slot_grad_ref, pg_ref, y_acc, dx_acc) = rest[-8:]
-    expert = pl.program_id(0)
+FF_TILE = 256
+WIDTH_TILE = 512
+
+
+def expert_kernel(count, pos_row_ref, pos_col_ref, gate_row_ref, *refs):
+    x_refs, g_refs = refs[:count], refs[count : 2 * count]
+    wgu_ref, wd_ref = refs[2 * count : 2 * count + 2]
+    rows_ref, hidden_ref, slot_grad_ref, pg_ref, place, result, rows_grad = refs[-7:]
+    y_refs, dx_refs = refs[-7 - 2 * count : -7 - count], refs[-7 - count : -7]
+    block, expert = pl.program_id(0), pl.program_id(1)
     capacity = rows_ref.shape[-2]
-    tokens = x_ref.shape[0]
+    tokens = x_refs[0].shape[0]
     slot_r = lax.broadcasted_iota(jnp.int32, (capacity, tokens), 0)
-    match = slot_r == pos_row_ref[0]
+    slot_c = lax.broadcasted_iota(jnp.int32, (tokens, capacity), 1)
+    match = slot_r == pos_row_ref[0, 0]
     pick = match.astype(bf16)
-    slot_c = lax.broadcasted_iota(jnp.int32, (tokens, capacity), 1)
-    place = (slot_c == pos_col_ref[0]).astype(bf16)
-    gates = jnp.sum(jnp.where(match, gate_row_ref[0], 0.0), axis=1, keepdims=True)
-    rows = dot(pick, x_ref[...]).astype(bf16)
-    slot_grad = (dot(pick, g_ref[...]) * gates).astype(bf16)
-    rows_ref[0, 0] = rows
-    slot_grad_ref[0, 0] = slot_grad
-    projected = dot(rows, wgu_ref[0])
-    gate, up = projected[:, :FF], projected[:, FF:]
-    square = gate * gate
-    tangent = jnp.tanh(gelu_c * (gate + 0.044715 * (square * gate)))
-    half_plus = 0.5 + 0.5 * tangent
-    activated = gate * half_plus
-    slope = half_plus + 0.5 * gate * (1.0 - tangent * tangent) * (
-        gelu_c * (1.0 + (3.0 * 0.044715) * square)
-    )
-    hidden = (activated * up).astype(bf16)
-    hidden_ref[0, 0] = hidden
-    result = (dot(hidden, wd_ref[0]) * gates).astype(bf16)
-    hidden_grad = dot_nt(slot_grad, wd_ref[0])
-    pg_ref[0, 0, :, :FF] = (hidden_grad * up * slope).astype(bf16)
-    pg_ref[0, 0, :, FF:] = (hidden_grad * activated).astype(bf16)
-    rows_grad = dot_nt(pg_ref[0, 0], wgu_ref[0]).astype(bf16)
-    y_part = dot(place, result)
-    dx_part = dot(place, rows_grad)
-
-    @pl.when(expert == 0)
-    def _():
-        y_acc[...] = y_part
-        dx_acc[...] = dx_part
-
-    @pl.when(expert != 0)
-    def _():
-        y_acc[...] += y_part
-        dx_acc[...] += dx_part
-
-    @pl.when(expert == EXP_DEV - 1)
-    def _():
-        y_ref[...] = y_acc[...].astype(bf16)
-        dx_ref[...] = dx_acc[...].astype(bf16)
-
-
-def expert_block(block, blocks, capacity, pos, gates, x, g, wgu, wd, kept):
-    tokens = x.shape[0]
+    place[expert] = (slot_c == pos_col_ref[0, 0]).astype(bf16)
+    gates = jnp.sum(jnp.where(match, gate_row_ref[0, 0], 0.0), axis=1, keepdims=True)
+    for one in range(count):
+
+        @pl.when(block == one)
+        def _():
+            for start in range(0, MODEL_WIDTH, WIDTH_TILE):
+                span = slice(start, start + WIDTH_TILE)
+                rows_ref[0, 0, :, span] = dot(pick, x_refs[one][:, span]).astype(bf16)
+                slot_grad_ref[0, 0, :, span] = (dot(pick, g_refs[one][:, span]) * gates).astype(bf16)
+
+    rows = rows_ref[0, 0]
+    slot_grad = slot_grad_ref[0, 0]
+    for start in range(0, FF, FF_TILE):
+        span = slice(start, start + FF_TILE)
+        up_span = slice(FF + start, FF + start + FF_TILE)
+        gate = dot(rows, wgu_ref[0, :, span])
+        up = dot(rows, wgu_ref[0, :, up_span])
+        hidden_grad = dot_nt(slot_grad, wd_ref[0, span, :])
+        square = gate * gate
+        tangent = jnp.tanh(gate * (gelu_c + (gelu_c * 0.044715) * square))
+        half_plus = 0.5 + 0.5 * tangent
+        activated = gate * half_plus
+        slope = half_plus + activated * (1.0 - tangent) * (
+            gelu_c + (3.0 * 0.044715 * gelu_c) * square
+        )
+        hidden_ref[0, 0, :, span] = (activated * up).astype(bf16)
+        pg_ref[0, 0, :, span] = (hidden_grad * up * slope).astype(bf16)
+        pg_ref[0, 0, :, up_span] = (hidden_grad * activated).astype(bf16)
+    hidden = hidden_ref[0, 0]
+    projected_grad = pg_ref[0, 0]
+    for start in range(0, MODEL_WIDTH, WIDTH_TILE):
+        span = slice(start, start + WIDTH_TILE)
+        result[expert, :, span] = (dot(hidden, wd_ref[0, :, span]) * gates).astype(bf16)
+        rows_grad[expert, :, span] = dot_nt(projected_grad, wgu_ref[0, span, :]).astype(bf16)
+
+    for one in range(count):
+
+        @pl.when((expert == EXP_DEV - 1) & (block == one))
+        def _():
+            both = jnp.concatenate([place[e] for e in range(EXP_DEV)], axis=1)
+            for start in range(0, MODEL_WIDTH, WIDTH_TILE):
+                span = slice(start, start + WIDTH_TILE)
+                for out_ref, terms in ((y_refs[one], result), (dx_refs[one], rows_grad)):
+                    stacked = terms[:, :, span].reshape(EXP_DEV * capacity, WIDTH_TILE)
+                    out_ref[:, span] = dot(both, stacked).astype(bf16)
+
+
+def expert_blocks(first, blocks, capacity, pos, gates, xs, gs, wgu, wd, kept):
+    count, tokens = len(xs), xs[0].shape[0]
     kept_shapes = tuple(
         jax.ShapeDtypeStruct((EXP_DEV, blocks, capacity, width), bf16)
         for width in (MODEL_WIDTH, FF, MODEL_WIDTH, 2 * FF)
     )
     kept_specs = tuple(
-        pl.BlockSpec((1, 1, capacity, s.shape[-1]), lambda e: (e, block, 0, 0)) for s in kept_shapes
-    )
-    aliases = {} if kept is None else {7 + i: 2 + i for i in range(4)}
-    flops = EXP_DEV * 2 * capacity * (4 * tokens * MODEL_WIDTH + 9 * MODEL_WIDTH * FF)
+        pl.BlockSpec((1, 1, capacity, s.shape[-1]), lambda b, e: (e, first + b, 0, 0))
+        for s in kept_shapes
+    )
+    args = [pos[:, :, None, :], pos[:, :, :, None], gates[:, :, None, :], *xs, *gs, wgu, wd]
+    aliases = {} if kept is None else {len(args) + i: 2 * count + i for i in range(4)}
+    flops = count * EXP_DEV * 2 * capacity * (4 * tokens * MODEL_WIDTH + 9 * MODEL_WIDTH * FF)
+    result = jax.ShapeDtypeStruct((tokens, MODEL_WIDTH), bf16)
+    once = pl.BlockSpec((tokens, MODEL_WIDTH), lambda b, e: (0, 0), pipeline_mode=pl.Buffered(1))
     out = pl.pallas_call(
-        expert_kernel,
-        grid=(EXP_DEV,),
+        functools.partial(expert_kernel, count),
+        grid=(count, EXP_DEV),
         in_specs=[
-            pl.BlockSpec((1, 1, tokens), lambda e: (e, 0, 0)),
-            pl.BlockSpec((1, tokens, 1), lambda e: (e, 0, 0)),
-            pl.BlockSpec((1, 1, tokens), lambda e: (e, 0, 0)),
-            whole((tokens, MODEL_WIDTH)),
-            whole((tokens, MODEL_WIDTH)),
-            pl.BlockSpec((1, MODEL_WIDTH, 2 * FF), lambda e: (e, 0, 0)),
-            pl.BlockSpec((1, FF, MODEL_WIDTH), lambda e: (e, 0, 0)),
+            pl.BlockSpec((1, 1, 1, tokens), lambda b, e: (b, e, 0, 0)),
+            pl.BlockSpec((1, 1, tokens, 1), lambda b, e: (b, e, 0, 0)),
+            pl.BlockSpec((1, 1, 1, tokens), lambda b, e: (b, e, 0, 0)),
+        ]
+        + [once] * (2 * count)
+        + [
+            pl.BlockSpec((1, MODEL_WIDTH, 2 * FF), lambda b, e: (e, 0, 0)),
+            pl.BlockSpec((1, FF, MODEL_WIDTH), lambda b, e: (e, 0, 0)),
         ]
         + [pl.BlockSpec(memory_space=pl.ANY) for _ in aliases],
-        out_specs=(whole((tokens, MODEL_WIDTH)), whole((tokens, MODEL_WIDTH))) + kept_specs,
-        out_shape=(
-            jax.ShapeDtypeStruct((tokens, MODEL_WIDTH), bf16),
-            jax.ShapeDtypeStruct((tokens, MODEL_WIDTH), bf16),
-        )
-        + kept_shapes,
-        scratch_shapes=[pltpu.VMEM((tokens, MODEL_WIDTH), f32)] * 2,
+        out_specs=(once,) * (2 * count) + kept_specs,
+        out_shape=(result,) * (2 * count) + kept_shapes,
+        scratch_shapes=[
+            pltpu.VMEM((EXP_DEV, tokens, capacity), bf16),
+            pltpu.VMEM((EXP_DEV, capacity, MODEL_WIDTH), bf16),
+            pltpu.VMEM((EXP_DEV, capacity, MODEL_WIDTH), bf16),
+        ],
         input_output_aliases=aliases,
         compiler_params=params(),
-        cost_estimate=cost(flops, 3e7),
-        name="expert_block",
-    )(pos[:, None, :], pos[:, :, None], gates[:, None, :], x, g, wgu, wd, *(kept or ()))
-    return out[0], out[1], out[2:]
+        cost_estimate=cost(flops, 6e7),
+        name="expert_blocks",
+    )(*args, *(kept or ()))
+    return out[:count], out[count : 2 * count], out[2 * count :]
+
+
+GRAD_TILE = 384
+
+
+def weight_grad_kernel(chunk_ref, a_ref, b_ref, out_ref):
+    out_ref[0] = dot_tn(a_ref[0], b_ref[0]).astype(bf16)
+
+
+def weight_grad(first, experts, chunk, size, a, b):
+    slots, width = a.shape[1], b.shape[-1]
+    tiles = size // GRAD_TILE
+    return pl.pallas_call(
+        weight_grad_kernel,
+        grid_spec=pltpu.PrefetchScalarGridSpec(
+            num_scalar_prefetch=1,
+            grid=(experts, tiles),
+            in_specs=[
+                pl.BlockSpec((1, slots, GRAD_TILE), lambda e, t, c: (first + e, 0, c[0] * tiles + t)),
+                pl.BlockSpec((1, slots, width), lambda e, t, c: (first + e, 0, 0)),
+            ],
+            out_specs=pl.BlockSpec((1, GRAD_TILE, width), lambda e, t, c: (e, t, 0)),
+        ),
+        out_shape=jax.ShapeDtypeStruct((experts, size, width), bf16),
+        compiler_params=params(),
+        cost_estimate=cost(2 * experts * slots * size * width, 2e7),
+        name="weight_grad",
+    )(chunk.reshape(1).astype(jnp.int32), a, b)
 
 
 def middle_kernel(*refs):
@@ -340,14 +385,14 @@
     )(*parts, mid, g, gain, wo, att)
 
 
-def attention_back_kernel(first, *refs):
+def attention_back_kernel(first, group, *refs):
     (q_ref, ag_ref, k_ref, v_ref, lse_ref, delta_ref, kpos_ref, qpos_ref) = refs[:8]
     rest = refs[8:]
     if not first:
         dq_in, dkv_in = rest[:2]
         rest = rest[2:]
     dq_ref, dkv_ref, dk_acc, dv_acc = rest
-    group, member = pl.program_id(0), pl.program_id(1)
+    member = pl.program_id(0)
     head = group * GROUP + member
     q, ag, keys, values = q_ref[...], ag_ref[...], k_ref[...], v_ref[...]
     scores = dot_nt(keys, q)
@@ -374,23 +419,24 @@
 
     @pl.when(member == GROUP - 1)
     def _():
-        for place, total in ((group, dk_acc), (KEY_VALUE_HEADS + group, dv_acc)):
-            columns = pl.ds(pl.multiple_of(place * HEAD_SIZE, HEAD_SIZE), HEAD_SIZE)
+        for place, total in enumerate((dk_acc, dv_acc)):
+            columns = slice(place * HEAD_SIZE, (place + 1) * HEAD_SIZE)
             value = total[...]
             if not first:
                 value += dkv_in[:, columns].astype(f32)
             dkv_ref[:, columns] = value.astype(bf16)
 
 
-def attention_backward(q, ag, kv, lse, delta, kpos_col, qpos_row, dq, dkv):
+def attention_backward(group, q, ag, kv, lse, delta, kpos_col, qpos_row, dq, dkv):
     first = dq is None
     rows, keys = q.shape[0], kv.shape[0]
-    by_head = pl.BlockSpec((rows, HEAD_SIZE), lambda g, m: (0, g * GROUP + m))
+    by_head = pl.BlockSpec((rows, HEAD_SIZE), lambda m: (0, group * GROUP + m))
+    by_member = pl.BlockSpec((rows, HEAD_SIZE), lambda m: (0, m))
     in_specs = [
         by_head,
         by_head,
-        pl.BlockSpec((keys, HEAD_SIZE), lambda g, m: (0, g)),
-        pl.BlockSpec((keys, HEAD_SIZE), lambda g, m: (0, KEY_VALUE_HEADS + g)),
+        pl.BlockSpec((keys, HEAD_SIZE), lambda m: (0, group)),
+        pl.BlockSpec((keys, HEAD_SIZE), lambda m: (0, KEY_VALUE_HEADS + group)),
         whole((HEAD_ROWS, rows)),
         whole((HEAD_ROWS, rows)),
         whole((keys, 1)),
@@ -398,50 +444,56 @@
     ]
     args = [q, ag, kv, kv, lse, delta, kpos_col, qpos_row]
     if not first:
-        in_specs += [by_head, whole((keys, 2 * KV_WIDTH))]
+        in_specs += [by_member, whole((keys, 2 * HEAD_SIZE))]
         args += [dq, dkv]
     return pl.pallas_call(
-        functools.partial(attention_back_kernel, first),
-        grid=(KEY_VALUE_HEADS, GROUP),
+        functools.partial(attention_back_kernel, first, group),
+        grid=(GROUP,),
         in_specs=in_specs,
-        out_specs=(by_head, whole((keys, 2 * KV_WIDTH))),
+        out_specs=(by_member, whole((keys, 2 * HEAD_SIZE))),
         out_shape=(
-            jax.ShapeDtypeStruct((rows, MODEL_WIDTH), f32),
-            jax.ShapeDtypeStruct((keys, 2 * KV_WIDTH), bf16),
+            jax.ShapeDtypeStruct((rows, GROUP * HEAD_SIZE), f32),
+            jax.ShapeDtypeStruct((keys, 2 * HEAD_SIZE), bf16),
         ),
         scratch_shapes=[pltpu.VMEM((keys, HEAD_SIZE), f32)] * 2,
         compiler_params=params(),
-        cost_estimate=cost(10 * rows * keys * MODEL_WIDTH, 1e7, rows * keys * QUERY_HEADS),
+        cost_estimate=cost(5 * rows * keys * MODEL_WIDTH, 1e7, rows * keys * GROUP),
         name="attention_backward",
     )(*args)
 
 
-def unrotate_kernel(dq_ref, cos_ref, sin_ref, out_ref):
+def unrotate_kernel(*refs):
+    *dq_refs, cos_ref, sin_ref, out_ref = refs
     cosine, sine = cos_ref[...], sin_ref[...]
     for head in range(QUERY_HEADS):
         span = slice(head * HEAD_SIZE, (head + 1) * HEAD_SIZE)
-        out_ref[:, span] = rotate_back(dq_ref[:, span], cosine, sine).astype(bf16)
-
-
-def unrotate(dq, cosine, sine):
+        member = head % GROUP
+        source = slice(member * HEAD_SIZE, (member + 1) * HEAD_SIZE)
+        out_ref[:, span] = rotate_back(dq_refs[head // GROUP][:, source], cosine, sine).astype(bf16)
+
+
+def unrotate(dqs, cosine, sine):
+    rows = dqs[0].shape[0]
     return pl.pallas_call(
         unrotate_kernel,
-        out_shape=jax.ShapeDtypeStruct(dq.shape, bf16),
+        out_shape=jax.ShapeDtypeStruct((rows, MODEL_WIDTH), bf16),
         compiler_params=params(),
-        cost_estimate=cost(dq.size * 4, dq.size * 6),
+        cost_estimate=cost(rows * MODEL_WIDTH * 4, rows * MODEL_WIDTH * 6),
         name="unrotate",
-    )(dq, cosine, sine)
+    )(*dqs, cosine, sine)
 
 
 def input_kernel(
-    dql_ref, dkv_ref, wq_ref, wk_ref, wv_ref, cos_ref, sin_ref, x_ref, gain_ref, mg_ref,
+    dql_ref, dkv0_ref, dkv1_ref, wq_ref, wk_ref, wv_ref, cos_ref, sin_ref, x_ref, gain_ref, mg_ref,
     dkvl_ref, dx_ref, dgain_ref,
 ):
     cosine, sine = cos_ref[...], sin_ref[...]
-    for head in range(KEY_VALUE_HEADS):
+    for head, dkv_ref in enumerate((dkv0_ref, dkv1_ref)):
         span = slice(head * HEAD_SIZE, (head + 1) * HEAD_SIZE)
-        dkvl_ref[:, span] = rotate_back(dkv_ref[:, span].astype(f32), cosine, sine).astype(bf16)
-    dkvl_ref[:, KV_WIDTH:] = dkv_ref[:, KV_WIDTH:]
+        v_span = slice(KV_WIDTH + head * HEAD_SIZE, KV_WIDTH + (head + 1) * HEAD_SIZE)
+        key_grad = dkv_ref[:, :HEAD_SIZE].astype(f32)
+        dkvl_ref[:, span] = rotate_back(key_grad, cosine, sine).astype(bf16)
+        dkvl_ref[:, v_span] = dkv_ref[:, HEAD_SIZE:]
     rows = x_ref.shape[0]
     half = rows // 2
     dgain = jnp.zeros((1, MODEL_WIDTH), f32)
@@ -459,7 +511,7 @@
     dgain_ref[...] = dgain
 
 
-def input_backward(dql, dkv, wq, wk, wv, cosine, sine, x, gain, mg):
+def input_backward(dql, dkvs, wq, wk, wv, cosine, sine, x, gain, mg):
     rows = x.shape[0]
     return pl.pallas_call(
         input_kernel,
@@ -471,7 +523,7 @@
         compiler_params=params(),
         cost_estimate=cost(2 * rows * MODEL_WIDTH * (MODEL_WIDTH + 2 * KV_WIDTH), 2e7),
         name="input_backward",
-    )(dql, dkv, wq, wk, wv, cosine, sine, x, gain, mg)
+    )(dql, *dkvs, wq, wk, wv, cosine, sine, x, gain, mg)
 
 
 def shifted(value, axis, steps):
@@ -489,7 +541,9 @@
 
 
 def gather_blocks(own):
-    out = [own, core_swap(own)]
+    swapped = core_swap(own)
+    out = [own, swapped]
+    own, swapped = tie(own, swapped)
     for steps in range(1, lax.axis_size("exp") // 2):
         same = chip_shift(own, steps)
         out += [core_swap(same), same]
@@ -505,28 +559,53 @@
     return terms
 
 
-def ring_scatter(parts, shift, index, count):
-    def part(step):
-        return lax.dynamic_index_in_dim(parts, (index - 1 - step) % count, 0, keepdims=False)
-
-    total = part(0)
+def ring_part(parts, index, count, step, axis=0):
+    return lax.dynamic_index_in_dim(parts, (index - 1 - step) % count, axis, keepdims=False)
+
+
+def add_low(a, b):
+    return (a.astype(f32) + b.astype(f32)).astype(bf16)
+
+
+def ring_scatter(parts, shift, index, count, axis=0):
+    total = ring_part(parts, index, count, 0, axis)
     for step in range(1, count):
-        total = (shift(total).astype(f32) + part(step).astype(f32)).astype(bf16)
+        total = add_low(shift(total), ring_part(parts, index, count, step, axis))
     return total
 
 
-def scatter_all(array):
+def sum_at_owner(parts, index, count):
+    def part(place):
+        return lax.dynamic_index_in_dim(parts, place % count, 0, keepdims=False)
+
+    total = part(index).astype(f32)
+    for step in range(1, count):
+        total += shifted(part(index + step), "ctx", step).astype(f32)
+    return total
+
+
+def scatter_core(array):
     dp, ctx, exp = (lax.axis_size(a) for a in ("dp", "ctx", "exp"))
-    d, c, e = (lax.axis_index(a) for a in ("dp", "ctx", "exp"))
-    chips = exp // 2
     rows, columns = array.shape
-    share = rows // (dp * ctx * exp)
-    parts = array.reshape(dp, ctx, chips, 2, share, columns)
+    parts = array.reshape(dp, ctx, exp // 2, 2, rows // (dp * ctx * exp), columns)
     parts = jnp.transpose(parts, (3, 2, 0, 1, 4, 5))
-    parts = ring_scatter(parts, core_swap, e % 2, 2)
-    parts = ring_scatter(parts, lambda v: chip_shift(v, 1), e // 2, chips)
-    parts = ring_scatter(parts, lambda v: shifted(v, "dp", 1), d, dp)
-    return ring_scatter(parts, lambda v: shifted(v, "ctx", 1), c, ctx)
+    return ring_scatter(parts, core_swap, lax.axis_index("exp") % 2, 2)
+
+
+def scatter_chip(parts):
+    return ring_scatter(
+        parts, lambda v: chip_shift(v, 1), lax.axis_index("exp") // 2, lax.axis_size("exp") // 2
+    )
+
+
+def scatter_axis(parts, axis):
+    return ring_scatter(
+        parts, lambda v: shifted(v, axis, 1), lax.axis_index(axis), lax.axis_size(axis)
+    )
+
+
+def tie(*values):
+    return lax.optimization_barrier(values)
 
 
 def per_device(
@@ -573,77 +652,131 @@
         return pair[0].astype(jnp.int32), pair[1]
 
     routing = [local_routing(block) for block in routing]
+    pos = jnp.stack([r[0] for r in routing])
+    gates = jnp.stack([r[1] for r in routing])
     g_blocks = gather_blocks(g)
 
     kv_all = jnp.concatenate(kv_blocks, axis=0)
+    kv_all, pos, gates, g_blocks = tie(kv_all, pos, gates, g_blocks)
     kpos_row = jnp.concatenate(key_positions)[None, :]
     att, att_low, lse, mid, nf = attention_forward(
         q, kv_all, positions[:, None], kpos_row, w_out, x, gain_two
     )
 
-    nf_blocks = gather_blocks(nf)
+    swapped = core_swap(nf)
+    nf_blocks = [nf, swapped]
+    nf, swapped = tie(nf, swapped)
     y_parts, dx_parts, kept = [], [], None
-    for block in range(exp_size):
-        pos, gates = routing[block]
-        y_part, dx_part, kept = expert_block(
-            block, exp_size, capacity, pos, gates, nf_blocks[block], g_blocks[block],
+    for first in range(0, exp_size, 2):
+        here = slice(first, first + 2)
+        if first:
+            same, dx_parts[-1] = tie(chip_shift(nf, first // 2), dx_parts[-1])
+            nf_blocks += [core_swap(same), same]
+        y_part, dx_part, kept = expert_blocks(
+            first, exp_size, capacity, pos[here], gates[here], nf_blocks[here], g_blocks[here],
             expert_gate_up, expert_down, kept,
         )
-        y_parts.append(y_part)
-        dx_parts.append(dx_part)
+        y_parts += y_part
+        dx_parts += dx_part
     nf_grad_terms = return_blocks(dx_parts)
     slot_rows, hidden, slot_grad, projected_grad = (
         a.reshape(EXP_DEV, exp_size * capacity, a.shape[-1]) for a in kept
     )
-    down_grad = jnp.einsum("erf,erd->efd", hidden, slot_grad, preferred_element_type=f32).astype(bf16)
-    gate_up_grad = jnp.einsum(
-        "erd,erf->edf", slot_rows, projected_grad, preferred_element_type=f32
-    ).astype(bf16)
-    down_share = lax.psum_scatter(down_grad, ("dp", "ctx"), scatter_dimension=1, tiled=True)
-    gate_up_share = lax.psum_scatter(gate_up_grad, ("dp", "ctx"), scatter_dimension=1, tiled=True)
+    dp_size, dp_here = lax.axis_size("dp"), lax.axis_index("dp")
+    gate_up_parts = [
+        [
+            weight_grad(
+                e, 1, (dp_here - 1 - step) % dp_size, MODEL_WIDTH // dp_size, slot_rows,
+                projected_grad,
+            )
+            for e in range(EXP_DEV)
+        ]
+        for step in range(dp_size)
+    ]
+    down_grad = weight_grad(0, EXP_DEV, jnp.int32(0), FF, hidden, slot_grad)
+
+    def over_dp(expert):
+        total = gate_up_parts[0][expert]
+        for step in range(1, dp_size):
+            total = shifted(total, "dp", 1).astype(f32) + gate_up_parts[step][expert].astype(f32)
+            total = total.astype(bf16)
+        return total[0].reshape(ctx_size, -1, 2 * FF)
+
+    nf_grad_terms, down_grad, gate_up_parts, y_parts = tie(
+        nf_grad_terms, down_grad, gate_up_parts, y_parts
+    )
 
     mid_grad, mid_grad_low, att_grad, delta, ffn_gain_part = middle_backward(
         nf_grad_terms, mid, g, gain_two, w_out, att
     )
+    w_out_grad = dot_tn(att_low, mid_grad_low).astype(bf16)
+    att_grad, w_out_grad = tie(att_grad, w_out_grad)
+    w_out_part = scatter_core(w_out_grad)
     y_terms = return_blocks(y_parts)
+    down_parts = down_grad.reshape(EXP_DEV, dp_size, ctx_size, -1, MODEL_WIDTH)
+    down_total = ring_part(down_parts, ctx_here, ctx_size, 0, 2)
+
+    dqs, dkvs = [None] * KEY_VALUE_HEADS, [None] * KEY_VALUE_HEADS
+    gate_up_totals = [None] * EXP_DEV
+    for step in range(ctx_size):
+        back = (step + 1) % ctx_size
+        for group in range(KEY_VALUE_HEADS):
+            dkv = shifted(dkvs[group], "ctx", 1) if step else None
+            ag, other = tie(att_grad, dqs[group - 1]) if step + group else (att_grad, None)
+            if other is not None:
+                dqs[group - 1] = other
+            dqs[group], dkvs[group] = attention_backward(
+                group, q, ag, kv_blocks[back], lse, delta, key_positions[back][:, None],
+                positions[None, :], dqs[group], dkv,
+            )
+        if step < ctx_size - 1:
+            down_total = add_low(
+                shifted(down_total, "ctx", 1), ring_part(down_parts, ctx_here, ctx_size, step + 1, 2)
+            )
+            att_grad, down_total = tie(att_grad, down_total)
+        if step == 0:
+            att_grad, w_out_part, gate_up_totals[0] = tie(att_grad, w_out_part, over_dp(0))
+            w_out_part = scatter_chip(w_out_part)
+        if step == 1:
+            att_grad, y_terms = tie(att_grad, y_terms)
+        if step == 2:
+            att_grad, w_out_part = tie(att_grad, w_out_part)
+    down_share = ring_scatter(
+        down_total, lambda v: shifted(v, "dp", 1), dp_here, dp_size, 1
+    )
+    gate_up_totals[1] = over_dp(1)
     layer_output = mid
     for term in y_terms:
         layer_output = layer_output + term.astype(f32)
     layer_output = layer_output.astype(bf16)
-    w_out_grad = dot_tn(att_low, mid_grad_low).astype(bf16)
-    w_out_share = scatter_all(w_out_grad)
-
-    dq, dkv = None, None
-    for step in range(ctx_size):
-        back = (step + 1) % ctx_size
-        if step:
-            dkv = shifted(dkv, "ctx", 1)
-        dq, dkv = attention_backward(
-            q, att_grad, kv_blocks[back], lse, delta, key_positions[back][:, None],
-            positions[None, :], dq, dkv,
-        )
-    dql = unrotate(dq, cosine, sine)
+    dql = unrotate(dqs, cosine, sine)
     w_query_grad = dot_tn(normed, dql).astype(bf16)
+    dql, w_query_grad, gate_up_totals = tie(dql, w_query_grad, gate_up_totals)
+    w_query_part = scatter_core(w_query_grad)
     dkvl, tokens_grad, attn_gain_part = input_backward(
-        dql, dkv, w_query, key_matrix, value_matrix, cosine, sine, x, gain_one, mid_grad
-    )
-    w_kv_grad = dot_tn(normed, dkvl).astype(bf16)
-    w_query_share = scatter_all(w_query_grad)
-    w_kv_share = scatter_all(w_kv_grad)
-    gains = lax.psum_scatter(
-        jnp.concatenate([attn_gain_part, ffn_gain_part], axis=0),
-        ("dp", "ctx", "exp"), scatter_dimension=1, tiled=True,
-    )
+        dql, dkvs, w_query, key_matrix, value_matrix, cosine, sine, x, gain_one, mid_grad
+    )
+    w_kv_grad = dot_tn(normed, dkvl)
+    gains = jnp.concatenate([attn_gain_part, ffn_gain_part], axis=0).T
+    gains = jnp.pad(gains, ((0, 0), (0, HEAD_SIZE - 2)))
+    w_kv_grad = jnp.concatenate([w_kv_grad, gains], axis=1).astype(bf16)
+    gate_up_share = jnp.stack(
+        [sum_at_owner(total, ctx_here, ctx_size) for total in gate_up_totals]
+    )
+    w_out_share = scatter_axis(scatter_axis(w_out_part, "dp"), "ctx")
+    w_query_share = scatter_axis(scatter_axis(scatter_chip(w_query_part), "dp"), "ctx")
+    w_kv_share = scatter_axis(scatter_axis(scatter_chip(scatter_core(w_kv_grad)), "dp"), "ctx")
+    w_kv_share = w_kv_share.astype(f32)
     return (
         layer_output[None],
         tokens_grad[None],
-        gains[0],
+        w_kv_share[:, 2 * KV_WIDTH],
         w_query_share.astype(f32),
-        w_kv_share[:, :KV_WIDTH].astype(f32),
-        w_kv_share[:, KV_WIDTH:].astype(f32),
+        w_kv_share[:, :KV_WIDTH],
+        w_kv_share[:, KV_WIDTH : 2 * KV_WIDTH],
         w_out_share.astype(f32),
-        gains[1],
-        gate_up_share.astype(f32),
+        w_kv_share[:, 2 * KV_WIDTH + 1],
+        gate_up_share,
         down_share.astype(f32),
     )
 

time: 790 us -> 648 us (0.82)
  waiting for transfers between devices: 383 us -> 231 us
  Pallas kernels: 237 us -> 263 us
  matrix products: 38.2 us -> 12.7 us
  other arithmetic: 31.3 us -> 49.7 us
  between operations: 14.7 us -> 1.44 us
  local copies, waits for them, and re-layouts: 24.5 us -> 35.9 us
    reduce_scatter x2 -> x0, waiting for transfers between devices: 166 us -> none  [the longest x1 163 us: per_device(): lax.psum_scatter(gate_up_grad, ('dp', 'ctx'), scatter_dimension=1, tiled=...]
    ppermute x18 -> x33, waiting for transfers between devices: 97.5 us -> 170 us  [shifted(): lax.ppermute(value, axis, [(i, (i + steps) % count) for i in range(count)])]
    ppermute x8, waiting for transfers between devices: 105 us -> 50.9 us  [chip_shift(): lax.ppermute(value, 'exp', [(i, (i + 2 * steps) % count) for i in range(c...]
    dot_general x2 -> x0, matrix products: 31.2 us -> none  [the longest x1 19.6 us: per_device(): jnp.einsum('erd,erf->edf', slot_rows, projected_grad, preferred_element_t...]
    pallas_call x9 -> x16, Pallas kernels: 168 us -> 195 us  [the longest x2 82.2 us: expert_blocks(): pl.pallas_call(functools.partial(expert_kernel, count), grid=(count, EXP_...]
    convert_element_type x19 -> x21, other arithmetic: 10.7 us -> 23.7 us  [the longest x18 16.3 us: add_low(): return (a.astype(f32) + b.astype(f32)).astype(bf16)]
    unnamed x4 -> x0, waiting for transfers between devices: 12.1 us -> none
    ppermute x18 -> x33, starting transfers between devices: 39.1 us -> 33.5 us  [shifted(): lax.ppermute(value, axis, [(i, (i + steps) % count) for i in range(count)])]
  transfers between devices with their start and end apart: 42 -> 54, of which waited for: 23 -> 26; matrix products, arithmetic and copies ran while one was open for 10% -> 12% of each run, Pallas kernels for 19% -> 24%
where the time goes in v2:
time: 648 us; the launch traced here: 640 us
  Pallas kernels  263 us (41%)
  waiting for transfers between devices  231 us (36%)
  other arithmetic  49.7 us (8%)
  starting transfers between devices  45.5 us (7%)
  local copies, waits for them, and re-layouts  35.9 us (6%)
  matrix products  12.7 us (2%)
    ppermute x33, waiting for transfers between devices, shifted(): lax.ppermute(value, axis, [(i, (i + steps) % count) for i in range(count)])  170 us
    pallas_call x2, Pallas kernels, expert_blocks(): pl.pallas_call(functools.partial(expert_kernel, count), grid=(count, EXP_...  82.2 us
    pallas_call x8, Pallas kernels, attention_backward(): pl.pallas_call(functools.partial(attention_back_kernel, first, group), gr...  68.5 us
    ppermute x8, waiting for transfers between devices, chip_shift(): lax.ppermute(value, 'exp', [(i, (i + 2 * steps) % count) for i in range(c...  50.9 us
    pallas_call x5, Pallas kernels, weight_grad(): pl.pallas_call(weight_grad_kernel, grid_spec=pltpu.PrefetchScalarGridSpec...  39.7 us
    pallas_call x1, Pallas kernels, attention_forward(): pl.pallas_call(attention_kernel, grid=(QUERY_HEADS,), in_specs=[pl.BlockS...  35.6 us
    ppermute x33, starting transfers between devices, shifted(): lax.ppermute(value, axis, [(i, (i + steps) % count) for i in range(count)])  33.5 us
    convert_element_type x18, other arithmetic, add_low(): return (a.astype(f32) + b.astype(f32)).astype(bf16)  16.3 us
  transfers between devices with their start and end apart: 54, of which 26 were waited for; matrix products, arithmetic and copies ran while one was open for 12% of the time, Pallas kernels for 24%

profile of v2, /device:TPU:0, one launch (start us, length us, event | category | flops | bytes accessed | tf_op | source)
XLA Modules:
  0.0 639.6 jit_solution(5993248874294851778)
XLA Ops:
  20.6 21.8 %collective-permute-done.7.refs_3_ = bf16[512,1536]{1,0:T(8,128)(2,1)S(1)} collective-permute-done((bf16[512,1536]{1,0:T(8,128)(2,1)}, bf16[512,1536]{1,0:T(8,128)(2,1)S(1)}, u32[]{:S(2)}, u32[]{:S(2)}) %collective-permute-start.7) | collective-permute-done | bytes 1572896 | tf_op jit(solution)/shard_map/ppermute | solution.py:540
  45.0 6.8 %query_projection.1.q_ref.refs_0_ = bf16[512,1536]{1,0:T(8,128)(2,1)} custom-call(bf16[512,1536]{1,0:T(8,128)(2,1)} %get-tuple-element.116.normed_ref, bf16[1536,1536]{1,0:T(8,128)(2,1)} %wq_ref.3, f32[512,128]{1,0:T(8,128)} %pad_maximum_fusion.2.cos_ref.refs_2_, f32[512,128]{1,0:T(8,128)} %pad_maximum_fusion.3.sin_ref.refs_3_), custom_call_target="tpu_custom_call" | custom-call | flops 75497472 | bytes 250000 | tf_op jit(solution)/shard_map/query_projection/pallas_call | solution.py:109
  57.1 5.9 collective-permute-done.1.refs_2_.refs_3_
  64.7 35.6 %attention_forward.1 = (f32[512,1536]{1,0:T(8,128)}, bf16[512,1536]{1,0:T(8,128)(2,1)}, f32[16,512]{1,0:T(8,128)}, f32[512,1536]{1,0:T(8,128)}, bf16[512,1536]{1,0:T(8,128)(2,1)}) custom-call(bf16[512,1536]{1,0:T(8,128)(2,1)} %query_projection.1.q_ref.refs_0_, bf16[2048,512]{1,0:T(8,128)(2,1)} %pad_maximum_fusion.1.k_ref.v_ref, ...), custom_call_target="tpu_custom_call" | custom-call | flops 402653184 | bytes 625000 | tf_op jit(solution)/shard_map/attention_forward/pallas_call | solution.py:165
  107.0 41.0 %expert_blocks.2 = (bf16[512,1536]{1,0:T(8,128)(2,1)}, bf16[512,1536]{1,0:T(8,128)(2,1)}, bf16[512,1536]{1,0:T(8,128)(2,1)}, bf16[512,1536]{1,0:T(8,128)(2,1)}, ...) custom-call(s32[2,2,1,512]{3,2,1,0:T(1,128)} %copy.72.pos_row_ref, ...), custom_call_target="tpu_custom_call" | custom-call | flops 1101004800 | bytes 1875000 | tf_op jit(solution)/shard_map/expert_blocks/pallas_call | solution.py:278
  152.6 41.2 %expert_blocks.3 = (bf16[512,1536]{1,0:T(8,128)(2,1)}, bf16[512,1536]{1,0:T(8,128)(2,1)}, bf16[512,1536]{1,0:T(8,128)(2,1)}, bf16[512,1536]{1,0:T(8,128)(2,1)}, ...) custom-call(s32[2,2,1,512]{3,2,1,0:T(1,128)} %copy.75.pos_row_ref, ...), custom_call_target="tpu_custom_call", output_to_operand_aliasing={{4}: (9, {}), {5}: (10, {}), {6}: (11, {}), {7}: (12, {})} | custom-call | flops 1101004800 | bytes 1875000 | tf_op jit(solution)/shard_map/expert_blocks/pallas_call | solution.py:278
  202.0 7.0 %weight_grad.6 = bf16[1,768,1536]{2,1,0:T(8,128)(2,1)} custom-call(s32[1]{0:T(128)} %bitcast.24.chunk_ref, bf16[2,1280,1536]{2,1,0:T(8,128)(2,1)} %bitcast.238, bf16[2,1280,1536]{2,1,0:T(8,128)(2,1)} %bitcast.242), custom_call_target="tpu_custom_call" | custom-call | flops 94371840 | bytes 625000 | tf_op jit(solution)/shard_map/weight_grad/pallas_call | solution.py:317
  209.0 6.9 %weight_grad.7 = bf16[1,768,1536]{2,1,0:T(8,128)(2,1)} custom-call(s32[1]{0:T(128)} %bitcast.24.chunk_ref, bf16[2,1280,1536]{2,1,0:T(8,128)(2,1)} %bitcast.239, bf16[2,1280,1536]{2,1,0:T(8,128)(2,1)} %bitcast.243), custom_call_target="tpu_custom_call" | custom-call | flops 94371840 | bytes 625000 | tf_op jit(solution)/shard_map/weight_grad/pallas_call | solution.py:317
  215.9 7.0 %weight_grad.8 = bf16[1,768,1536]{2,1,0:T(8,128)(2,1)} custom-call(s32[1]{0:T(128)} %bitcast.27.chunk_ref, bf16[2,1280,1536]{2,1,0:T(8,128)(2,1)} %bitcast.240, bf16[2,1280,1536]{2,1,0:T(8,128)(2,1)} %bitcast.244), custom_call_target="tpu_custom_call" | custom-call | flops 94371840 | bytes 625000 | tf_op jit(solution)/shard_map/weight_grad/pallas_call | solution.py:317
  222.9 7.0 %weight_grad.9 = bf16[1,768,1536]{2,1,0:T(8,128)(2,1)} custom-call(s32[1]{0:T(128)} %bitcast.27.chunk_ref, bf16[2,1280,1536]{2,1,0:T(8,128)(2,1)} %bitcast.241, bf16[2,1280,1536]{2,1,0:T(8,128)(2,1)} %bitcast.245), custom_call_target="tpu_custom_call" | custom-call | flops 94371840 | bytes 625000 | tf_op jit(solution)/shard_map/weight_grad/pallas_call | solution.py:317
  229.8 11.9 %weight_grad.5 = bf16[2,768,1536]{2,1,0:T(8,128)(2,1)} custom-call(s32[1]{0:T(128)} %constant.340.clone.1.chunk_ref, bf16[2,1280,768]{2,1,0:T(8,128)(2,1)} %bitcast.250, bf16[2,1280,1536]{2,1,0:T(8,128)(2,1)} %bitcast.246), custom_call_target="tpu_custom_call" | custom-call | flops 188743680 | bytes 625000 | tf_op jit(solution)/shard_map/weight_grad/pallas_call | solution.py:317
  243.4 11.7 %middle_backward.1 = (f32[512,1536]{1,0:T(8,128)}, bf16[512,1536]{1,0:T(8,128)(2,1)}, bf16[512,1536]{1,0:T(8,128)(2,1)}, f32[16,512]{1,0:T(8,128)}, f32[1,1536]{1,0:T(1,128)}) custom-call(bf16[512,1536]{1,0:T(8,128)(2,1)} %get-tuple-element.148.refs_0_, bf16[512,1536]{1,0:T(8,128)(2,1)} %copy-done.18, bf16[512,1536]{1,0:T(8,128)(2,1)} %copy-done.19, ...), custom_call_target="tpu_custom_call" | custom-call | flops 75497472 | bytes 625000 | tf_op jit(solution)/shard_map/middle_backward/pallas_call | solution.py:372
  270.9 8.3 %attention_backward.8 = (f32[512,768]{1,0:T(8,128)}, bf16[512,256]{1,0:T(8,128)(2,1)}) custom-call(bf16[512,1536]{1,0:T(8,128)(2,1)} %query_projection.1.q_ref.refs_0_, bf16[512,1536]{1,0:T(8,128)(2,1)} %get-tuple-element.202.refs_1_, bf16[512,512]{1,0:T(8,128)(2,1)} %copy-done.3, bf16[512,512]{1,0:T(8,128)(2,1)} %copy-done.3, ...), custom_call_target="tpu_custom_call" | custom-call | flops 62914560 | bytes 312500 | tf_op jit(solution)/shard_map/attention_backward/pallas_call | solution.py:449
  279.3 8.1 %attention_backward.9 = (f32[512,768]{1,0:T(8,128)}, bf16[512,256]{1,0:T(8,128)(2,1)}) custom-call(bf16[512,1536]{1,0:T(8,128)(2,1)} %query_projection.1.q_ref.refs_0_, bf16[512,1536]{1,0:T(8,128)(2,1)} %get-tuple-element.202.refs_1_, bf16[512,512]{1,0:T(8,128)(2,1)} %copy-done.3, bf16[512,512]{1,0:T(8,128)(2,1)} %copy-done.3, ...), custom_call_target="tpu_custom_call" | custom-call | flops 62914560 | bytes 312500 | tf_op jit(solution)/shard_map/attention_backward/pallas_call | solution.py:449
  287.4 8.2 %collective-permute-done.15 = bf16[2,2,96,1536]{3,2,0,1:T(8,128)(2,1)} collective-permute-done((bf16[2,2,96,1536]{3,2,0,1:T(8,128)(2,1)}, bf16[2,2,96,1536]{3,2,0,1:T(8,128)(2,1)}, u32[]{:S(2)}, u32[]{:S(2)}) %collective-permute-start.15) | collective-permute-done | bytes 1179680 | tf_op jit(solution)/shard_map/ppermute | solution.py:531
  307.4 13.5 %collective-permute-done.17 = bf16[1,768,1536]{2,1,0:T(8,128)(2,1)} collective-permute-done((bf16[1,768,1536]{2,1,0:T(8,128)(2,1)}, bf16[1,768,1536]{2,1,0:T(8,128)(2,1)}, u32[]{:S(2)}, u32[]{:S(2)}) %collective-permute-start.17) | collective-permute-done | bytes 2359328 | tf_op jit(solution)/shard_map/ppermute | solution.py:531
  332.5 8.5 %attention_backward.10 = (f32[512,768]{1,0:T(8,128)}, bf16[512,256]{1,0:T(8,128)(2,1)}) custom-call(bf16[512,1536]{1,0:T(8,128)(2,1)} %query_projection.1.q_ref.refs_0_, bf16[512,1536]{1,0:T(8,128)(2,1)} %get-tuple-element.202.refs_1_, bf16[512,512]{1,0:T(8,128)(2,1)} %copy-done.2, bf16[512,512]{1,0:T(8,128)(2,1)} %copy-done.2, ...), custom_call_target="tpu_custom_call" | custom-call | flops 62914560 | bytes 312500 | tf_op jit(solution)/shard_map/attention_backward/pallas_call | solution.py:449
  343.9 8.6 %attention_backward.11 = (f32[512,768]{1,0:T(8,128)}, bf16[512,256]{1,0:T(8,128)(2,1)}) custom-call(bf16[512,1536]{1,0:T(8,128)(2,1)} %query_projection.1.q_ref.refs_0_, bf16[512,1536]{1,0:T(8,128)(2,1)} %get-tuple-element.202.refs_1_, bf16[512,512]{1,0:T(8,128)(2,1)} %copy-done.2, bf16[512,512]{1,0:T(8,128)(2,1)} %copy-done.2, ...), custom_call_target="tpu_custom_call" | custom-call | flops 62914560 | bytes 312500 | tf_op jit(solution)/shard_map/attention_backward/pallas_call | solution.py:449
  352.5 18.6 %collective-permute-done.30 = bf16[1,768,1536]{2,1,0:T(8,128)(2,1)} collective-permute-done((bf16[1,768,1536]{2,1,0:T(8,128)(2,1)}, bf16[1,768,1536]{2,1,0:T(8,128)(2,1)}, u32[]{:S(2)}, u32[]{:S(2)}) %collective-permute-start.30) | collective-permute-done | bytes 2359328 | tf_op jit(solution)/shard_map/ppermute | solution.py:531
  378.9 9.0 %attention_backward.12 = (f32[512,768]{1,0:T(8,128)}, bf16[512,256]{1,0:T(8,128)(2,1)}) custom-call(bf16[512,1536]{1,0:T(8,128)(2,1)} %query_projection.1.q_ref.refs_0_, bf16[512,1536]{1,0:T(8,128)(2,1)} %get-tuple-element.202.refs_1_, bf16[512,512]{1,0:T(8,128)(2,1)} %copy-done.1, bf16[512,512]{1,0:T(8,128)(2,1)} %copy-done.1, ...), custom_call_target="tpu_custom_call" | custom-call | flops 62914560 | bytes 312500 | tf_op jit(solution)/shard_map/attention_backward/pallas_call | solution.py:449
  388.1 8.6 %attention_backward.13 = (f32[512,768]{1,0:T(8,128)}, bf16[512,256]{1,0:T(8,128)(2,1)}) custom-call(bf16[512,1536]{1,0:T(8,128)(2,1)} %query_projection.1.q_ref.refs_0_, bf16[512,1536]{1,0:T(8,128)(2,1)} %get-tuple-element.202.refs_1_, bf16[512,512]{1,0:T(8,128)(2,1)} %copy-done.1, bf16[512,512]{1,0:T(8,128)(2,1)} %copy-done.1, ...), custom_call_target="tpu_custom_call" | custom-call | flops 62914560 | bytes 312500 | tf_op jit(solution)/shard_map/attention_backward/pallas_call | solution.py:449
  409.3 8.9 %attention_backward.14 = (f32[512,768]{1,0:T(8,128)}, bf16[512,256]{1,0:T(8,128)(2,1)}) custom-call(bf16[512,1536]{1,0:T(8,128)(2,1)} %query_projection.1.q_ref.refs_0_, bf16[512,1536]{1,0:T(8,128)(2,1)} %get-tuple-element.202.refs_1_, bf16[512,512]{1,0:T(8,128)(2,1)} %get-tuple-element.117.refs_2_.refs_3_, ...), custom_call_target="tpu_custom_call" | custom-call | flops 62914560 | bytes 312500 | tf_op jit(solution)/shard_map/attention_backward/pallas_call | solution.py:449
  418.9 8.5 %attention_backward.15 = (f32[512,768]{1,0:T(8,128)}, bf16[512,256]{1,0:T(8,128)(2,1)}) custom-call(bf16[512,1536]{1,0:T(8,128)(2,1)} %query_projection.1.q_ref.refs_0_, bf16[512,1536]{1,0:T(8,128)(2,1)} %get-tuple-element.202.refs_1_, bf16[512,512]{1,0:T(8,128)(2,1)} %get-tuple-element.117.refs_2_.refs_3_, ...), custom_call_target="tpu_custom_call" | custom-call | flops 62914560 | bytes 312500 | tf_op jit(solution)/shard_map/attention_backward/pallas_call | solution.py:449
  431.5 5.7 convolution_convert_fusion
  437.2 10.6 %input_backward.1 = (bf16[512,512]{1,0:T(8,128)(2,1)}, bf16[512,1536]{1,0:T(8,128)(2,1)}, f32[1,1536]{1,0:T(1,128)}) custom-call(bf16[512,1536]{1,0:T(8,128)(2,1)} %unrotate.1.dql_ref, bf16[512,256]{1,0:T(8,128)(2,1)} %get-tuple-element.210.dkv0_ref, bf16[512,256]{1,0:T(8,128)(2,1)} %get-tuple-element.211.dkv1_ref, bf16[1536,1536]{1,0:T(8,128)(2,1)} %wq_ref.3, ...), custom_call_target="tpu_custom_call" | custom-call | flops 100663296 | bytes 625000 | tf_op jit(solution)/shard_map/input_backward/pallas_call | solution.py:516
  474.4 36.8 %collective-permute-done.51 = bf16[192,1536]{1,0:T(8,128)(2,1)} collective-permute-done((bf16[192,1536]{1,0:T(8,128)(2,1)}, bf16[192,1536]{1,0:T(8,128)(2,1)}, u32[]{:S(2)}, u32[]{:S(2)}) %collective-permute-start.51) | collective-permute-done | bytes 589856 | tf_op jit(solution)/shard_map/ppermute | solution.py:531
  514.3 46.3 %collective-permute-done.48 = bf16[192,1536]{1,0:T(8,128)(2,1)S(1)} collective-permute-done((bf16[192,1536]{1,0:T(8,128)(2,1)S(1)}, bf16[192,1536]{1,0:T(8,128)(2,1)S(1)}, u32[]{:S(2)}, u32[]{:S(2)}) %collective-permute-start.48) | collective-permute-done | bytes 589856 | tf_op jit(solution)/shard_map/ppermute | solution.py:531
  570.5 8.9 %collective-permute-done.32 = bf16[2,4,48,640]{3,2,1,0:T(8,128)(2,1)S(1)} collective-permute-done((bf16[2,4,48,640]{3,2,1,0:T(8,128)(2,1)S(1)}, bf16[2,4,48,640]{3,2,1,0:T(8,128)(2,1)S(1)}, u32[]{:S(2)}, u32[]{:S(2)}) %collective-permute-start.32) | collective-permute-done | bytes 491552 | tf_op jit(solution)/shard_map/ppermute | solution.py:540
  586.5 16.5 %collective-permute-done.38 = bf16[2,4,48,1536]{3,2,1,0:T(8,128)(2,1)S(1)} collective-permute-done((bf16[2,4,48,1536]{3,2,1,0:T(8,128)(2,1)S(1)}, bf16[2,4,48,1536]{3,2,1,0:T(8,128)(2,1)S(1)}, u32[]{:S(2)}, u32[]{:S(2)}) %collective-permute-start.38) | collective-permute-done | bytes 1179680 | tf_op jit(solution)/shard_map/ppermute | solution.py:540
  606.0 11.2 %collective-permute-done.39 = bf16[4,48,1536]{2,1,0:T(8,128)(2,1)S(1)} collective-permute-done((bf16[4,48,1536]{2,1,0:T(8,128)(2,1)S(1)}, bf16[4,48,1536]{2,1,0:T(8,128)(2,1)S(1)}, u32[]{:S(2)}, u32[]{:S(2)}) %collective-permute-start.39) | collective-permute-done | bytes 589856 | tf_op jit(solution)/shard_map/ppermute | solution.py:531
  625.3 6.4 collective-permute-done.41
  633.1 5.6 collective-permute-done.42
  (284 shorter events, 177.7 us)
Async XLA Ops:
  4.5 37.8 %collective-permute-start.7 = (bf16[512,1536]{1,0:T(8,128)(2,1)}, bf16[512,1536]{1,0:T(8,128)(2,1)S(1)}, u32[]{:S(2)}, u32[]{:S(2)}) collective-permute-start(bf16[512,1536]{1,0:T(8,128)(2,1)} %bitcast.259), channel_id=1, source_target_pairs={{0,2},{1,3},{2,0},{3,1},{4,6},{5,7},{6,4},{7,5},{8,10},{9,11},{10,... | collective-permute-start | bytes 4718600 | tf_op jit(solution)/shard_map/ppermute | solution.py:540
  14.4 42.7 %collective-permute-start.2 = (bf16[512,512]{1,0:T(8,128)(2,1)}, bf16[512,512]{1,0:T(8,128)(2,1)S(1)}, u32[]{:S(2)}, u32[]{:S(2)}) collective-permute-start(bf16[512,512]{1,0:T(8,128)(2,1)} %get-tuple-element.117.refs_2_.refs_3_), channel_id=1, source_target_pairs={{0,12},{4,0},{8,4},{12,8},{1,13},{5,1},{9,5},{13,9},{2,14},{6,2},{... | collective-permute-start | bytes 1572872 | tf_op jit(solution)/shard_map/ppermute | solution.py:531
  18.0 45.0 %collective-permute-start.1 = (bf16[512,512]{1,0:T(8,128)(2,1)}, bf16[512,512]{1,0:T(8,128)(2,1)S(1)}, u32[]{:S(2)}, u32[]{:S(2)}) collective-permute-start(bf16[512,512]{1,0:T(8,128)(2,1)} %get-tuple-element.117.refs_2_.refs_3_), channel_id=1, source_target_pairs={{0,8},{4,12},{8,0},{12,4},{1,9},{5,13},{9,1},{13,5},{2,10},{6,14},... | collective-permute-start | bytes 1572872 | tf_op jit(solution)/shard_map/ppermute | solution.py:531
  18.0 45.0 %collective-permute-start = (bf16[512,512]{1,0:T(8,128)(2,1)}, bf16[512,512]{1,0:T(8,128)(2,1)S(1)}, u32[]{:S(2)}, u32[]{:S(2)}) collective-permute-start(bf16[512,512]{1,0:T(8,128)(2,1)} %get-tuple-element.117.refs_2_.refs_3_), channel_id=1, source_target_pairs={{0,4},{4,8},{8,12},{12,0},{1,5},{5,9},{9,13},{13,1},{2,6},{6,10},{... | collective-permute-start | bytes 1572872 | tf_op jit(solution)/shard_map/ppermute | solution.py:531
  42.3 22.3 %collective-permute-start.8 = (bf16[512,1536]{1,0:T(8,128)(2,1)S(1)}, bf16[512,1536]{1,0:T(8,128)(2,1)}, u32[]{:S(2)}, u32[]{:S(2)}) collective-permute-start(bf16[512,1536]{1,0:T(8,128)(2,1)S(1)} %collective-permute-done.7.refs_3_), channel_id=1, source_target_pairs={{0,1},{1,0},{2,3},{3,2},{4,5},{5,4},{6,7},{7,6},{8,9},{9,8},{10,11... | collective-permute-start | bytes 4718600 | tf_op jit(solution)/shard_map/ppermute | solution.py:535
  103.9 44.1 %collective-permute-start.10 = (bf16[512,1536]{1,0:T(8,128)(2,1)}, bf16[512,1536]{1,0:T(8,128)(2,1)S(1)}, u32[]{:S(2)}, u32[]{:S(2)}) collective-permute-start(bf16[512,1536]{1,0:T(8,128)(2,1)} %get-tuple-element.128.refs_0_), channel_id=1, source_target_pairs={{0,2},{1,3},{2,0},{3,1},{4,6},{5,7},{6,4},{7,5},{8,10},{9,11},{10,... | collective-permute-start | bytes 4718600 | tf_op jit(solution)/shard_map/ppermute | solution.py:540
  194.0 47.7 %collective-permute-start.11 = (bf16[512,1536]{1,0:T(8,128)(2,1)}, bf16[512,1536]{1,0:T(8,128)(2,1)S(1)}, u32[]{:S(2)}, u32[]{:S(2)}) collective-permute-start(bf16[512,1536]{1,0:T(8,128)(2,1)} %get-tuple-element.130), channel_id=1, source_target_pairs={{0,1},{1,0},{2,3},{3,2},{4,5},{5,4},{6,7},{7,6},{8,9},{9,8},{10,11... | collective-permute-start | bytes 4718600 | tf_op jit(solution)/shard_map/ppermute | solution.py:535
  200.5 41.2 %collective-permute-start.14 = (bf16[512,1536]{1,0:T(8,128)(2,1)}, bf16[512,1536]{1,0:T(8,128)(2,1)S(1)}, u32[]{:S(2)}, u32[]{:S(2)}) collective-permute-start(bf16[512,1536]{1,0:T(8,128)(2,1)} %add_convert_fusion.4), channel_id=1, source_target_pairs={{0,2},{1,3},{2,0},{3,1},{4,6},{5,7},{6,4},{7,5},{8,10},{9,11},{10,... | collective-permute-start | bytes 4718600 | tf_op jit(solution)/shard_map/ppermute | solution.py:540
  261.7 40.4 %collective-permute-start.16 = (bf16[2,2,4,48,1536]{4,3,2,1,0:T(8,128)(2,1)}, bf16[2,2,4,48,1536]{4,3,2,1,0:T(8,128)(2,1)}, u32[]{:S(2)}, u32[]{:S(2)}) collective-permute-start(bf16[2,2,4,48,1536]{4,3,2,1,0:T(8,128)(2,1)} %bitcast.235), channel_id=1, source_target_pairs={{0,1},{1,0},{2,3},{3,2},{4,5},{5,4},{6,7},{7,6},{8,9},{9,8},{10,11... | collective-permute-start | bytes 7077896 | tf_op jit(solution)/shard_map/ppermute | solution.py:535
  265.7 29.8 %collective-permute-start.15 = (bf16[2,2,96,1536]{3,2,0,1:T(8,128)(2,1)}, bf16[2,2,96,1536]{3,2,0,1:T(8,128)(2,1)}, u32[]{:S(2)}, u32[]{:S(2)}) collective-permute-start(bf16[2,2,96,1536]{3,2,0,1:T(8,128)(2,1)} %bitcast.236), channel_id=1, source_target_pairs={{0,4},{4,8},{8,12},{12,0},{1,5},{5,9},{9,13},{13,1},{2,6},{6,10},{... | collective-permute-start | bytes 3538952 | tf_op jit(solution)/shard_map/ppermute | solution.py:531
  266.6 31.0 %collective-permute-start.20 = (bf16[512,1536]{1,0:T(8,128)(2,1)}, bf16[512,1536]{1,0:T(8,128)(2,1)}, u32[]{:S(2)}, u32[]{:S(2)}) collective-permute-start(bf16[512,1536]{1,0:T(8,128)(2,1)} %get-tuple-element.166), channel_id=1, source_target_pairs={{0,1},{1,0},{2,3},{3,2},{4,5},{5,4},{6,7},{7,6},{8,9},{9,8},{10,11... | collective-permute-start | bytes 4718600 | tf_op jit(solution)/shard_map/ppermute | solution.py:535
  266.6 54.4 %collective-permute-start.17 = (bf16[1,768,1536]{2,1,0:T(8,128)(2,1)}, bf16[1,768,1536]{2,1,0:T(8,128)(2,1)}, u32[]{:S(2)}, u32[]{:S(2)}) collective-permute-start(bf16[1,768,1536]{2,1,0:T(8,128)(2,1)} %weight_grad.6), channel_id=1, source_target_pairs={{0,16},{16,0},{1,17},{17,1},{2,18},{18,2},{3,19},{19,3},{4,20},{20... | collective-permute-start | bytes 7077896 | tf_op jit(solution)/shard_map/ppermute | solution.py:531
  270.7 107.6 %collective-permute-start.19 = (bf16[512,1536]{1,0:T(8,128)(2,1)}, bf16[512,1536]{1,0:T(8,128)(2,1)}, u32[]{:S(2)}, u32[]{:S(2)}) collective-permute-start(bf16[512,1536]{1,0:T(8,128)(2,1)} %get-tuple-element.165), channel_id=1, source_target_pairs={{0,1},{1,0},{2,3},{3,2},{4,5},{5,4},{6,7},{7,6},{8,9},{9,8},{10,11... | collective-permute-start | bytes 4718600 | tf_op jit(solution)/shard_map/ppermute | solution.py:535
  295.6 36.2 %collective-permute-start.24 = (bf16[512,256]{1,0:T(8,128)(2,1)}, bf16[512,256]{1,0:T(8,128)(2,1)S(1)}, u32[]{:S(2)}, u32[]{:S(2)}) collective-permute-start(bf16[512,256]{1,0:T(8,128)(2,1)} %get-tuple-element.183), channel_id=1, source_target_pairs={{0,4},{4,8},{8,12},{12,0},{1,5},{5,9},{9,13},{13,1},{2,6},{6,10},{... | collective-permute-start | bytes 786440 | tf_op jit(solution)/shard_map/ppermute | solution.py:531
  297.6 73.5 %collective-permute-start.30 = (bf16[1,768,1536]{2,1,0:T(8,128)(2,1)}, bf16[1,768,1536]{2,1,0:T(8,128)(2,1)}, u32[]{:S(2)}, u32[]{:S(2)}) collective-permute-start(bf16[1,768,1536]{2,1,0:T(8,128)(2,1)} %weight_grad.7), channel_id=1, source_target_pairs={{0,16},{16,0},{1,17},{17,1},{2,18},{18,2},{3,19},{19,3},{4,20},{20... | collective-permute-start | bytes 7077896 | tf_op jit(solution)/shard_map/ppermute | solution.py:531
  302.1 28.4 %collective-permute-start.18 = (bf16[2,2,96,1536]{3,2,0,1:T(8,128)(2,1)S(1)}, bf16[2,2,96,1536]{3,2,0,1:T(8,128)(2,1)S(1)}, u32[]{:S(2)}, u32[]{:S(2)}) collective-permute-start(bf16[2,2,96,1536]{3,2,0,1:T(8,128)(2,1)S(1)} %fusion.6), channel_id=1, source_target_pairs={{0,4},{4,8},{8,12},{12,0},{1,5},{5,9},{9,13},{13,1},{2,6},{6,10},{... | collective-permute-start | bytes 3538952 | tf_op jit(solution)/shard_map/ppermute | solution.py:531
  321.0 57.9 %collective-permute-start.21 = (bf16[512,1536]{1,0:T(8,128)(2,1)}, bf16[512,1536]{1,0:T(8,128)(2,1)S(1)}, u32[]{:S(2)}, u32[]{:S(2)}) collective-permute-start(bf16[512,1536]{1,0:T(8,128)(2,1)} %add_convert_fusion.3), channel_id=1, source_target_pairs={{0,2},{1,3},{2,0},{3,1},{4,6},{5,7},{6,4},{7,5},{8,10},{9,11},{10,... | collective-permute-start | bytes 4718600 | tf_op jit(solution)/shard_map/ppermute | solution.py:540
  331.8 70.9 %collective-permute-start.22 = (bf16[2,2,96,1536]{3,2,0,1:T(8,128)(2,1)}, bf16[2,2,96,1536]{3,2,0,1:T(8,128)(2,1)}, u32[]{:S(2)}, u32[]{:S(2)}) collective-permute-start(bf16[2,2,96,1536]{3,2,0,1:T(8,128)(2,1)} %fusion.5), channel_id=1, source_target_pairs={{0,4},{4,8},{8,12},{12,0},{1,5},{5,9},{9,13},{13,1},{2,6},{6,10},{... | collective-permute-start | bytes 3538952 | tf_op jit(solution)/shard_map/ppermute | solution.py:531
  342.2 36.7 %collective-permute-start.26 = (bf16[512,256]{1,0:T(8,128)(2,1)}, bf16[512,256]{1,0:T(8,128)(2,1)}, u32[]{:S(2)}, u32[]{:S(2)}) collective-permute-start(bf16[512,256]{1,0:T(8,128)(2,1)} %get-tuple-element.191), channel_id=1, source_target_pairs={{0,4},{4,8},{8,12},{12,0},{1,5},{5,9},{9,13},{13,1},{2,6},{6,10},{... | collective-permute-start | bytes 786440 | tf_op jit(solution)/shard_map/ppermute | solution.py:531
  378.4 27.6 %collective-permute-start.23 = (bf16[2,4,48,1536]{3,2,1,0:T(8,128)(2,1)}, bf16[2,4,48,1536]{3,2,1,0:T(8,128)(2,1)}, u32[]{:S(2)}, u32[]{:S(2)}) collective-permute-start(bf16[2,4,48,1536]{3,2,1,0:T(8,128)(2,1)} %dynamic-slice_bitcast_fusion.1), channel_id=1, source_target_pairs={{0,2},{1,3},{2,0},{3,1},{4,6},{5,7},{6,4},{7,5},{8,10},{9,11},{10,... | collective-permute-start | bytes 3538952 | tf_op jit(solution)/shard_map/ppermute | solution.py:540
  387.9 20.7 %collective-permute-start.28 = (bf16[512,256]{1,0:T(8,128)(2,1)}, bf16[512,256]{1,0:T(8,128)(2,1)S(1)}, u32[]{:S(2)}, u32[]{:S(2)}) collective-permute-start(bf16[512,256]{1,0:T(8,128)(2,1)} %get-tuple-element.199), channel_id=1, source_target_pairs={{0,4},{4,8},{8,12},{12,0},{1,5},{5,9},{9,13},{13,1},{2,6},{6,10},{... | collective-permute-start | bytes 786440 | tf_op jit(solution)/shard_map/ppermute | solution.py:531
  396.7 21.4 %collective-permute-start.29 = (bf16[512,256]{1,0:T(8,128)(2,1)}, bf16[512,256]{1,0:T(8,128)(2,1)S(1)}, u32[]{:S(2)}, u32[]{:S(2)}) collective-permute-start(bf16[512,256]{1,0:T(8,128)(2,1)} %get-tuple-element.204), channel_id=1, source_target_pairs={{0,4},{4,8},{8,12},{12,0},{1,5},{5,9},{9,13},{13,1},{2,6},{6,10},{... | collective-permute-start | bytes 786440 | tf_op jit(solution)/shard_map/ppermute | solution.py:531
  452.8 113.7 %collective-permute-start.37 = (bf16[2,2,4,48,1536]{4,3,2,1,0:T(8,128)(2,1)}, bf16[2,2,4,48,1536]{4,3,2,1,0:T(8,128)(2,1)}, u32[]{:S(2)}, u32[]{:S(2)}) collective-permute-start(bf16[2,2,4,48,1536]{4,3,2,1,0:T(8,128)(2,1)} %bitcast.234), channel_id=1, source_target_pairs={{0,1},{1,0},{2,3},{3,2},{4,5},{5,4},{6,7},{7,6},{8,9},{9,8},{10,11... | collective-permute-start | bytes 7077896 | tf_op jit(solution)/shard_map/ppermute | solution.py:535
  458.1 53.1 %collective-permute-start.51 = (bf16[192,1536]{1,0:T(8,128)(2,1)}, bf16[192,1536]{1,0:T(8,128)(2,1)}, u32[]{:S(2)}, u32[]{:S(2)}) collective-permute-start(bf16[192,1536]{1,0:T(8,128)(2,1)} %get-tuple-element.237), channel_id=1, source_target_pairs={{0,8},{4,12},{8,0},{12,4},{1,9},{5,13},{9,1},{13,5},{2,10},{6,14},... | collective-permute-start | bytes 1769480 | tf_op jit(solution)/shard_map/ppermute | solution.py:531
  458.4 52.8 %collective-permute-start.50 = (bf16[192,1536]{1,0:T(8,128)(2,1)}, bf16[192,1536]{1,0:T(8,128)(2,1)}, u32[]{:S(2)}, u32[]{:S(2)}) collective-permute-start(bf16[192,1536]{1,0:T(8,128)(2,1)} %get-tuple-element.235), channel_id=1, source_target_pairs={{0,4},{4,8},{8,12},{12,0},{1,5},{5,9},{9,13},{13,1},{2,6},{6,10},{... | collective-permute-start | bytes 1769480 | tf_op jit(solution)/shard_map/ppermute | solution.py:531
  469.7 43.5 %collective-permute-start.49 = (bf16[192,1536]{1,0:T(8,128)(2,1)S(1)}, bf16[192,1536]{1,0:T(8,128)(2,1)S(1)}, u32[]{:S(2)}, u32[]{:S(2)}) collective-permute-start(bf16[192,1536]{1,0:T(8,128)(2,1)S(1)} %copy-done.26), channel_id=1, source_target_pairs={{0,12},{4,0},{8,4},{12,8},{1,13},{5,1},{9,5},{13,9},{2,14},{6,2},{... | collective-permute-start | bytes 1769480 | tf_op jit(solution)/shard_map/ppermute | solution.py:531
  473.5 87.1 %collective-permute-start.48 = (bf16[192,1536]{1,0:T(8,128)(2,1)S(1)}, bf16[192,1536]{1,0:T(8,128)(2,1)S(1)}, u32[]{:S(2)}, u32[]{:S(2)}) collective-permute-start(bf16[192,1536]{1,0:T(8,128)(2,1)S(1)} %copy-done.25), channel_id=1, source_target_pairs={{0,8},{4,12},{8,0},{12,4},{1,9},{5,13},{9,1},{13,5},{2,10},{6,14},... | collective-permute-start | bytes 1769480 | tf_op jit(solution)/shard_map/ppermute | solution.py:531
  511.2 49.5 %collective-permute-start.47 = (bf16[192,1536]{1,0:T(8,128)(2,1)S(1)}, bf16[192,1536]{1,0:T(8,128)(2,1)S(1)}, u32[]{:S(2)}, u32[]{:S(2)}) collective-permute-start(bf16[192,1536]{1,0:T(8,128)(2,1)S(1)} %copy-done.24), channel_id=1, source_target_pairs={{0,4},{4,8},{8,12},{12,0},{1,5},{5,9},{9,13},{13,1},{2,6},{6,10},{... | collective-permute-start | bytes 1769480 | tf_op jit(solution)/shard_map/ppermute | solution.py:531
  511.2 53.6 %collective-permute-start.31 = (bf16[2,2,4,48,640]{4,3,2,1,0:T(8,128)(2,1)S(1)}, bf16[2,2,4,48,640]{4,3,2,1,0:T(8,128)(2,1)S(1)}, u32[]{:S(2)}, u32[]{:S(2)}) collective-permute-start(bf16[2,2,4,48,640]{4,3,2,1,0:T(8,128)(2,1)S(1)} %bitcast.275), channel_id=1, source_target_pairs={{0,1},{1,0},{2,3},{3,2},{4,5},{5,4},{6,7},{7,6},{8,9},{9,8},{10,11... | collective-permute-start | bytes 2949128 | tf_op jit(solution)/shard_map/ppermute | solution.py:535
  513.3 50.4 %collective-permute-start.53 = (bf16[2,96,1536]{2,1,0:T(8,128)(2,1)S(1)}, bf16[2,96,1536]{2,1,0:T(8,128)(2,1)S(1)}, u32[]{:S(2)}, u32[]{:S(2)}) collective-permute-start(bf16[2,96,1536]{2,1,0:T(8,128)(2,1)S(1)} %copy-done.23), channel_id=1, source_target_pairs={{0,16},{16,0},{1,17},{17,1},{2,18},{18,2},{3,19},{19,3},{4,20},{20... | collective-permute-start | bytes 1769480 | tf_op jit(solution)/shard_map/ppermute | solution.py:531
  569.0 34.1 %collective-permute-start.38 = (bf16[2,4,48,1536]{3,2,1,0:T(8,128)(2,1)S(1)}, bf16[2,4,48,1536]{3,2,1,0:T(8,128)(2,1)S(1)}, u32[]{:S(2)}, u32[]{:S(2)}) collective-permute-start(bf16[2,4,48,1536]{3,2,1,0:T(8,128)(2,1)S(1)} %dynamic-slice_bitcast_fusion), channel_id=1, source_target_pairs={{0,2},{1,3},{2,0},{3,1},{4,6},{5,7},{6,4},{7,5},{8,10},{9,11},{10,... | collective-permute-start | bytes 3538952 | tf_op jit(solution)/shard_map/ppermute | solution.py:540
  580.2 23.7 %collective-permute-start.46 = (bf16[48,1536]{1,0:T(8,128)(2,1)S(1)}, bf16[48,1536]{1,0:T(8,128)(2,1)S(1)}, u32[]{:S(2)}, u32[]{:S(2)}) collective-permute-start(bf16[48,1536]{1,0:T(8,128)(2,1)S(1)} %fusion.24), channel_id=1, source_target_pairs={{0,4},{4,8},{8,12},{12,0},{1,5},{5,9},{9,13},{13,1},{2,6},{6,10},{... | collective-permute-start | bytes 442376 | tf_op jit(solution)/shard_map/ppermute | solution.py:531
  (61 other events, 517.3 us)

commit v3 on v2

--- a/solution.py
+++ b/solution.py
@@ -32,6 +32,7 @@
 NT = (((1,), (1,)), ((), ()))
 TN = (((0,), (0,)), ((), ()))
 VMEM_BYTES = 60 * 1024 * 1024
+MESH = pl.DeviceIdType.MESH
 
 
 def dot(a, b):
@@ -385,115 +386,209 @@
     )(*parts, mid, g, gain, wo, att)
 
 
-def attention_back_kernel(first, group, *refs):
-    (q_ref, ag_ref, k_ref, v_ref, lse_ref, delta_ref, kpos_ref, qpos_ref) = refs[:8]
-    rest = refs[8:]
-    if not first:
-        dq_in, dkv_in = rest[:2]
-        rest = rest[2:]
-    dq_ref, dkv_ref, dk_acc, dv_acc = rest
-    member = pl.program_id(0)
-    head = group * GROUP + member
-    q, ag, keys, values = q_ref[...], ag_ref[...], k_ref[...], v_ref[...]
-    scores = dot_nt(keys, q)
-    weights = jnp.exp2(scores * score_to_log2 - lse_ref[pl.ds(head, 1), :])
-    weights = jnp.where(kpos_ref[...] <= qpos_ref[...], weights, 0.0)
-    weights_grad = dot_nt(values, ag)
-    score_grad = (weights * (weights_grad - delta_ref[pl.ds(head, 1), :]) * score_scale).astype(bf16)
-    dv = dot(weights.astype(bf16), ag)
-    dk = dot(score_grad, q)
-    dq = dot_tn(score_grad, keys)
-    if not first:
-        dq += dq_in[...]
-    dq_ref[...] = dq
-
-    @pl.when(member == 0)
-    def _():
-        dk_acc[...] = dk
-        dv_acc[...] = dv
-
-    @pl.when(member != 0)
-    def _():
-        dk_acc[...] += dk
-        dv_acc[...] += dv
-
-    @pl.when(member == GROUP - 1)
-    def _():
-        for place, total in enumerate((dk_acc, dv_acc)):
-            columns = slice(place * HEAD_SIZE, (place + 1) * HEAD_SIZE)
-            value = total[...]
-            if not first:
-                value += dkv_in[:, columns].astype(f32)
-            dkv_ref[:, columns] = value.astype(bf16)
-
-
-def attention_backward(group, q, ag, kv, lse, delta, kpos_col, qpos_row, dq, dkv):
-    first = dq is None
-    rows, keys = q.shape[0], kv.shape[0]
-    by_head = pl.BlockSpec((rows, HEAD_SIZE), lambda m: (0, group * GROUP + m))
-    by_member = pl.BlockSpec((rows, HEAD_SIZE), lambda m: (0, m))
-    in_specs = [
-        by_head,
-        by_head,
-        pl.BlockSpec((keys, HEAD_SIZE), lambda m: (0, group)),
-        pl.BlockSpec((keys, HEAD_SIZE), lambda m: (0, KEY_VALUE_HEADS + group)),
-        whole((HEAD_ROWS, rows)),
-        whole((HEAD_ROWS, rows)),
-        whole((keys, 1)),
-        whole((1, rows)),
-    ]
-    args = [q, ag, kv, kv, lse, delta, kpos_col, qpos_row]
-    if not first:
-        in_specs += [by_member, whole((keys, 2 * HEAD_SIZE))]
-        args += [dq, dkv]
-    return pl.pallas_call(
-        functools.partial(attention_back_kernel, first, group),
-        grid=(GROUP,),
-        in_specs=in_specs,
-        out_specs=(by_member, whole((keys, 2 * HEAD_SIZE))),
-        out_shape=(
-            jax.ShapeDtypeStruct((rows, GROUP * HEAD_SIZE), f32),
-            jax.ShapeDtypeStruct((keys, 2 * HEAD_SIZE), bf16),
-        ),
-        scratch_shapes=[pltpu.VMEM((keys, HEAD_SIZE), f32)] * 2,
-        compiler_params=params(),
-        cost_estimate=cost(5 * rows * keys * MODEL_WIDTH, 1e7, rows * keys * GROUP),
-        name="attention_backward",
-    )(*args)
-
-
-def unrotate_kernel(*refs):
-    *dq_refs, cos_ref, sin_ref, out_ref = refs
+def signal_and_wait(neighbours):
+    barrier = pltpu.get_barrier_semaphore()
+    for neighbour in neighbours:
+        pl.semaphore_signal(barrier, inc=1, device_id=neighbour, device_id_type=MESH)
+    pl.semaphore_wait(barrier, len(neighbours))
+
+
+def remote(source, target, send_sem, recv_sem, device):
+    return pltpu.make_async_remote_copy(
+        src_ref=source, dst_ref=target, send_sem=send_sem, recv_sem=recv_sem,
+        device_id=device, device_id_type=MESH,
+    )
+
+
+class Axis:
+    def __init__(self, name):
+        if name in ("dp", "ctx"):
+            self.count, self.me = lax.axis_size(name), lax.axis_index(name)
+            place = lambda i: {name: i}
+        else:
+            exp = lax.axis_index("exp")
+            core, chip = lax.rem(exp, 2), exp // 2
+            if name == "core":
+                self.count, self.me = 2, core
+                place = lambda i: {"exp": chip * 2 + i}
+            else:
+                self.count, self.me = lax.axis_size("exp") // 2, chip
+                place = lambda i: {"exp": i * 2 + core}
+        self.next = place(lax.rem(self.me + 1, self.count))
+        self.last = place(lax.rem(self.me + self.count - 1, self.count))
+
+    def neighbours(self):
+        return [self.next] if self.count == 2 else [self.next, self.last]
+
+
+class Ring:
+    def __init__(self, axis, terms, rows, send, recv, send_sem, recv_sem):
+        self.axis, self.count, self.terms, self.rows = axis, axis.count, terms, rows
+        self.send, self.recv, self.send_sem, self.recv_sem = send, recv, send_sem, recv_sem
+
+    def here(self, hop):
+        part = lax.rem(self.axis.me + self.count - 1 - hop, self.count)
+        return pl.ds(pl.multiple_of(part * self.rows, self.rows), self.rows)
+
+    def copy(self, hop):
+        if len(self.terms) > 1:
+            source = self.send.at[hop]
+        elif hop == 0:
+            source = self.terms[0].at[self.here(0), :]
+        else:
+            source = self.send.at[hop - 1]
+        return remote(
+            source, self.recv.at[hop], self.send_sem.at[hop], self.recv_sem.at[hop], self.axis.next
+        )
+
+    def hop(self, hop):
+        if hop == 0 and len(self.terms) == 1:
+            self.copy(0).start()
+            return None
+        here = self.here(hop)
+        total = self.terms[0][here, :].astype(f32)
+        for term in self.terms[1:]:
+            total += term[here, :].astype(f32)
+        if hop:
+            self.copy(hop - 1).wait_recv()
+            total += self.recv[hop - 1].astype(f32)
+        if hop < self.count - 1:
+            self.send[hop - (len(self.terms) == 1)] = total.astype(bf16)
+            self.copy(hop).start()
+        return total
+
+    def finish(self):
+        for hop in range(self.count - 1):
+            self.copy(hop).wait_send()
+
+
+def attention_back_kernel(
+    n, q_ref, ag_ref, lse_ref, delta_ref, kpos_ref, qpos_ref, cos_ref, sin_ref, mine_ref, came_ref,
+    next_ref, *refs,
+):
+    kv_refs = refs[:n]
+    dql_ref, dkv_ref, share_ref, next_came_ref = refs[n : n + 4]
+    (
+        dq_acc, send, recv, ring_send, ring_recv,
+        send_sem, recv_sem, ring_send_sem, ring_recv_sem, next_sem,
+    ) = refs[n + 4 :]
+    me = lax.axis_index("ctx")
+    right, left = lax.rem(me + 1, n), lax.rem(me + n - 1, n)
+    across = {"dp": 1 - lax.axis_index("dp")}
+    signal_and_wait([{"ctx": right}, {"ctx": left}, across])
+    exchange = remote(next_ref, next_came_ref, next_sem.at[0], next_sem.at[1], across)
+    exchange.start()
+    ring = Ring(
+        Axis("ctx"), [mine_ref, came_ref], share_ref.shape[0], ring_send, ring_recv,
+        ring_send_sem, ring_recv_sem,
+    )
+    ring.hop(0)
+
+    def dkv_copy(step, group):
+        return remote(
+            send.at[group, step], recv.at[group, step], send_sem.at[group, step],
+            recv_sem.at[group, step], {"ctx": right},
+        )
+
+    for step in range(n):
+        kv_ref = kv_refs[(step + 1) % n]
+        kpos = kpos_ref[(step + 1) % n]
+
+        def one_group(group, carry):
+            keys = kv_ref[:, pl.ds(pl.multiple_of(group * HEAD_SIZE, HEAD_SIZE), HEAD_SIZE)]
+            start = pl.multiple_of(KV_WIDTH + group * HEAD_SIZE, HEAD_SIZE)
+            values = kv_ref[:, pl.ds(start, HEAD_SIZE)]
+            dk = dv = None
+            for member in range(GROUP):
+                head = group * GROUP + member
+                columns = pl.ds(pl.multiple_of(head * HEAD_SIZE, HEAD_SIZE), HEAD_SIZE)
+                q, ag = q_ref[:, columns], ag_ref[:, columns]
+                scores = dot_nt(keys, q)
+                weights = jnp.exp2(scores * score_to_log2 - lse_ref[pl.ds(head, 1), :])
+                weights = jnp.where(kpos <= qpos_ref[...], weights, 0.0)
+                weights_grad = dot_nt(values, ag)
+                score_grad = weights * (weights_grad - delta_ref[pl.ds(head, 1), :]) * score_scale
+                score_grad = score_grad.astype(bf16)
+                dv_part = dot(weights.astype(bf16), ag)
+                dk_part = dot(score_grad, q)
+                dv = dv_part if dv is None else dv + dv_part
+                dk = dk_part if dk is None else dk + dk_part
+                dq = dot_tn(score_grad, keys)
+                if step:
+                    dq += dq_acc[:, columns]
+                dq_acc[:, columns] = dq
+            dkv = jnp.concatenate([dk, dv], axis=1)
+            if step:
+                dkv_copy(step - 1, group).wait_recv()
+                dkv += recv[group, step - 1].astype(f32)
+            if step < n - 1:
+                send[group, step] = dkv.astype(bf16)
+                dkv_copy(step, group).start()
+            else:
+                for place in range(2):
+                    start = pl.multiple_of(place * KV_WIDTH + group * HEAD_SIZE, HEAD_SIZE)
+                    part = dkv[:, place * HEAD_SIZE : (place + 1) * HEAD_SIZE]
+                    dkv_ref[:, pl.ds(start, HEAD_SIZE)] = part.astype(bf16)
+            return carry
+
+        lax.fori_loop(0, KEY_VALUE_HEADS, one_group, 0)
+        if step < n - 2:
+            ring.hop(step + 1)
     cosine, sine = cos_ref[...], sin_ref[...]
     for head in range(QUERY_HEADS):
         span = slice(head * HEAD_SIZE, (head + 1) * HEAD_SIZE)
-        member = head % GROUP
-        source = slice(member * HEAD_SIZE, (member + 1) * HEAD_SIZE)
-        out_ref[:, span] = rotate_back(dq_refs[head // GROUP][:, source], cosine, sine).astype(bf16)
-
-
-def unrotate(dqs, cosine, sine):
-    rows = dqs[0].shape[0]
+        dql_ref[:, span] = rotate_back(dq_acc[:, span], cosine, sine).astype(bf16)
+    share_ref[...] = ring.hop(n - 1)
+    for step in range(n - 1):
+        for group in range(KEY_VALUE_HEADS):
+            dkv_copy(step, group).wait_send()
+    ring.finish()
+    exchange.wait()
+
+
+def attention_backward(q, ag, kvs, lse, delta, kpos, qpos_row, cosine, sine, mine, came, following):
+    n = len(kvs)
+    rows, keys = q.shape[0], kvs[0].shape[0]
+    share = mine.shape[0] // n
+    vmem = pl.BlockSpec(memory_space=pltpu.VMEM)
+    hbm = pl.BlockSpec(memory_space=pl.ANY)
     return pl.pallas_call(
-        unrotate_kernel,
-        out_shape=jax.ShapeDtypeStruct((rows, MODEL_WIDTH), bf16),
-        compiler_params=params(),
-        cost_estimate=cost(rows * MODEL_WIDTH * 4, rows * MODEL_WIDTH * 6),
-        name="unrotate",
-    )(*dqs, cosine, sine)
+        functools.partial(attention_back_kernel, n),
+        in_specs=[vmem] * 10 + [hbm] + [vmem] * n,
+        out_specs=(vmem, vmem, vmem, hbm),
+        out_shape=(
+            jax.ShapeDtypeStruct((rows, MODEL_WIDTH), bf16),
+            jax.ShapeDtypeStruct((keys, 2 * KV_WIDTH), bf16),
+            jax.ShapeDtypeStruct((share, mine.shape[1]), f32),
+            jax.ShapeDtypeStruct(following.shape, bf16),
+        ),
+        scratch_shapes=[
+            pltpu.VMEM((rows, MODEL_WIDTH), f32),
+            pltpu.VMEM((KEY_VALUE_HEADS, n - 1, keys, 2 * HEAD_SIZE), bf16),
+            pltpu.VMEM((KEY_VALUE_HEADS, n - 1, keys, 2 * HEAD_SIZE), bf16),
+            pltpu.VMEM((n - 1, share, mine.shape[1]), bf16),
+            pltpu.VMEM((n - 1, share, mine.shape[1]), bf16),
+            pltpu.SemaphoreType.DMA((KEY_VALUE_HEADS, n - 1)),
+            pltpu.SemaphoreType.DMA((KEY_VALUE_HEADS, n - 1)),
+            pltpu.SemaphoreType.DMA((n - 1,)),
+            pltpu.SemaphoreType.DMA((n - 1,)),
+            pltpu.SemaphoreType.DMA((2,)),
+        ],
+        compiler_params=params(collective_id=1, has_side_effects=True),
+        cost_estimate=cost(10 * n * rows * keys * MODEL_WIDTH, 4e7, n * rows * keys * QUERY_HEADS),
+        name="attention_backward",
+    )(q, ag, lse, delta, kpos, qpos_row, cosine, sine, mine, came, following, *kvs)
 
 
 def input_kernel(
-    dql_ref, dkv0_ref, dkv1_ref, wq_ref, wk_ref, wv_ref, cos_ref, sin_ref, x_ref, gain_ref, mg_ref,
+    dql_ref, dkv_ref, wq_ref, wk_ref, wv_ref, cos_ref, sin_ref, x_ref, gain_ref, mg_ref,
     dkvl_ref, dx_ref, dgain_ref,
 ):
     cosine, sine = cos_ref[...], sin_ref[...]
-    for head, dkv_ref in enumerate((dkv0_ref, dkv1_ref)):
+    for head in range(KEY_VALUE_HEADS):
         span = slice(head * HEAD_SIZE, (head + 1) * HEAD_SIZE)
-        v_span = slice(KV_WIDTH + head * HEAD_SIZE, KV_WIDTH + (head + 1) * HEAD_SIZE)
-        key_grad = dkv_ref[:, :HEAD_SIZE].astype(f32)
-        dkvl_ref[:, span] = rotate_back(key_grad, cosine, sine).astype(bf16)
-        dkvl_ref[:, v_span] = dkv_ref[:, HEAD_SIZE:]
+        dkvl_ref[:, span] = rotate_back(dkv_ref[:, span].astype(f32), cosine, sine).astype(bf16)
+    dkvl_ref[:, KV_WIDTH:] = dkv_ref[:, KV_WIDTH:]
     rows = x_ref.shape[0]
     half = rows // 2
     dgain = jnp.zeros((1, MODEL_WIDTH), f32)
@@ -511,7 +606,7 @@
     dgain_ref[...] = dgain
 
 
-def input_backward(dql, dkvs, wq, wk, wv, cosine, sine, x, gain, mg):
+def input_backward(dql, dkv, wq, wk, wv, cosine, sine, x, gain, mg):
     rows = x.shape[0]
     return pl.pallas_call(
         input_kernel,
@@ -523,7 +618,169 @@
         compiler_params=params(),
         cost_estimate=cost(2 * rows * MODEL_WIDTH * (MODEL_WIDTH + 2 * KV_WIDTH), 2e7),
         name="input_backward",
-    )(dql, *dkvs, wq, wk, wv, cosine, sine, x, gain, mg)
+    )(dql, dkv, wq, wk, wv, cosine, sine, x, gain, mg)
+
+
+def ring_buffers(count, terms, rows, width):
+    sends = count - 1 if terms > 1 else max(count - 2, 1)
+    return [
+        pltpu.VMEM((sends, rows, width), bf16),
+        pltpu.VMEM((count - 1, rows, width), bf16),
+        pltpu.SemaphoreType.DMA((count - 1,)),
+        pltpu.SemaphoreType.DMA((count - 1,)),
+    ]
+
+
+class Chain:
+    def __init__(self, rings, stores):
+        self.hops = [(r, h) for r in range(len(rings)) for h in range(rings[r].count)]
+        self.rings, self.stores, self.done = rings, stores, 0
+
+    def step(self, times=1):
+        for _ in range(times):
+            if self.done == len(self.hops):
+                return
+            index, hop = self.hops[self.done]
+            self.done += 1
+            ring = self.rings[index]
+            total = ring.hop(hop)
+            if hop == ring.count - 1:
+                store = self.stores[index]
+                store[...] = total.astype(store.dtype)
+
+    def finish(self):
+        assert self.done == len(self.hops)
+        for ring in self.rings:
+            ring.finish()
+
+
+FULL_AXES = ("core", "chip", "dp", "ctx")
+
+
+def sizes():
+    exp = lax.axis_size("exp")
+    return {"core": 2, "chip": exp // 2, "dp": lax.axis_size("dp"), "ctx": lax.axis_size("ctx")}
+
+
+def last_kernel(plan, *refs):
+    mine_ref, came_ref, mine_down_ref, other_down_ref = refs[:4]
+    arrays = refs[4 : 4 + len(plan)]
+    share_ref, down_ref = refs[4 + len(plan) : 6 + len(plan)]
+    outs = refs[6 + len(plan) : 6 + 2 * len(plan)]
+    scratch = list(refs[6 + 2 * len(plan) :])
+
+    def take(number):
+        taken = scratch[:number]
+        del scratch[:number]
+        return taken
+
+    axes = {name: Axis(name) for name in FULL_AXES}
+    across = axes["dp"].next
+    piece = Chain(
+        [Ring(axes["ctx"], [mine_ref, came_ref], share_ref.shape[0], *take(4))], [share_ref]
+    )
+    came_down, down_sem = take(2)
+    downs, exchanges = [], []
+    for expert in range(EXP_DEV):
+        exchanges.append(
+            remote(
+                other_down_ref.at[expert], came_down.at[expert], down_sem.at[expert, 0],
+                down_sem.at[expert, 1], across,
+            )
+        )
+        terms = [mine_down_ref.at[expert], came_down.at[expert]]
+        downs.append(
+            Chain(
+                [Ring(axes["ctx"], terms, down_ref.shape[1], *take(4))], [down_ref.at[expert]]
+            )
+        )
+    chains = []
+    for (names, rows), array, out in zip(plan, arrays, outs):
+        rings, stores, source = [], [], array
+        for name in names:
+            rows //= axes[name].count
+            rings.append(Ring(axes[name], [source], rows, *take(4)))
+            source = out if name == names[-1] else take(1)[0]
+            stores.append(source)
+        chains.append(Chain(rings, stores))
+    query, kv, out_chain = chains
+    signal_and_wait([device for axis in axes.values() for device in axis.neighbours()])
+
+    query.step()
+    kv.step()
+    piece.step()
+    out_chain.step()
+    exchanges[0].start()
+    query.step(2)
+    kv.step(2)
+    piece.step()
+    out_chain.step(2)
+    exchanges[1].start()
+    piece.step()
+    out_chain.step()
+    exchanges[0].wait_recv()
+    downs[0].step()
+    query.step(2)
+    kv.step(2)
+    piece.step()
+    out_chain.step()
+    downs[0].step()
+    out_chain.step()
+    exchanges[1].wait_recv()
+    downs[1].step()
+    downs[0].step()
+    query.step(2)
+    kv.step(2)
+    everything = [downs[0], downs[1], query, kv, piece, out_chain]
+    while any(chain.done < len(chain.hops) for chain in everything):
+        for chain in everything:
+            chain.step()
+    for chain in everything:
+        chain.finish()
+    for exchange in exchanges:
+        exchange.wait_send()
+
+
+def last_transfers(mine, came, mine_down, other_down, w_query, w_kv, w_out):
+    counts = sizes()
+    n = counts["ctx"]
+    full = FULL_AXES if (MODEL_WIDTH // (2 * counts["chip"] * counts["dp"] * n)) % 16 == 0 else FULL_AXES[:3]
+    plan = [(full, w_query.shape[0]), (full, w_kv.shape[0]), (full[2:], w_out.shape[0])]
+    share, down_share = mine.shape[0] // n, mine_down.shape[1] // n
+    scratch = ring_buffers(n, 2, share, mine.shape[1])
+    scratch += [pltpu.VMEM(mine_down.shape, bf16), pltpu.SemaphoreType.DMA((EXP_DEV, 2))]
+    for _ in range(EXP_DEV):
+        scratch += ring_buffers(n, 2, down_share, mine_down.shape[2])
+    shapes = [
+        jax.ShapeDtypeStruct((share, mine.shape[1]), f32),
+        jax.ShapeDtypeStruct((EXP_DEV, down_share, mine_down.shape[2]), f32),
+    ]
+    for (names, rows), array in zip(plan, (w_query, w_kv, w_out)):
+        width = array.shape[1]
+        for name in names:
+            rows //= counts[name]
+            scratch += ring_buffers(counts[name], 1, rows, width)
+            if name != names[-1]:
+                scratch.append(pltpu.VMEM((rows, width), bf16))
+        shapes.append(jax.ShapeDtypeStruct((rows, width), f32 if "ctx" in names else bf16))
+    vmem = pl.BlockSpec(memory_space=pltpu.VMEM)
+    out = pl.pallas_call(
+        functools.partial(last_kernel, plan),
+        in_specs=[vmem] * 3 + [pl.BlockSpec(memory_space=pl.ANY)] + [vmem] * 3,
+        out_specs=(vmem,) * 5,
+        out_shape=tuple(shapes),
+        scratch_shapes=scratch,
+        compiler_params=params(collective_id=2, has_side_effects=True),
+        cost_estimate=cost(1e6, 4e7),
+        name="last_transfers",
+    )(mine, came, mine_down, other_down, w_query, w_kv, w_out)
+    attention = out[2:]
+    if "ctx" not in full:
+        attention = [
+            scatter_axis(a.reshape(n, a.shape[0] // n, a.shape[1]), "ctx").astype(f32)
+            for a in attention
+        ]
+    return out[0], out[1], attention
 
 
 def shifted(value, axis, steps):
@@ -574,21 +831,15 @@
     return total
 
 
-def sum_at_owner(parts, index, count):
-    def part(place):
-        return lax.dynamic_index_in_dim(parts, place % count, 0, keepdims=False)
-
-    total = part(index).astype(f32)
-    for step in range(1, count):
-        total += shifted(part(index + step), "ctx", step).astype(f32)
-    return total
-
-
-def scatter_core(array):
+def by_owner(array):
     dp, ctx, exp = (lax.axis_size(a) for a in ("dp", "ctx", "exp"))
     rows, columns = array.shape
     parts = array.reshape(dp, ctx, exp // 2, 2, rows // (dp * ctx * exp), columns)
-    parts = jnp.transpose(parts, (3, 2, 0, 1, 4, 5))
+    return jnp.transpose(parts, (3, 2, 0, 1, 4, 5)).reshape(rows, columns)
+
+
+def scatter_core(array):
+    parts = array.reshape(2, lax.axis_size("exp") // 2, -1, array.shape[1])
     return ring_scatter(parts, core_swap, lax.axis_index("exp") % 2, 2)
 
 
@@ -683,101 +934,63 @@
         a.reshape(EXP_DEV, exp_size * capacity, a.shape[-1]) for a in kept
     )
     dp_size, dp_here = lax.axis_size("dp"), lax.axis_index("dp")
-    gate_up_parts = [
-        [
-            weight_grad(
-                e, 1, (dp_here - 1 - step) % dp_size, MODEL_WIDTH // dp_size, slot_rows,
-                projected_grad,
-            )
-            for e in range(EXP_DEV)
-        ]
-        for step in range(dp_size)
+    half, down_half = MODEL_WIDTH // dp_size, FF // dp_size
+    theirs = [
+        weight_grad(e, 1, (dp_here - 1) % dp_size, half, slot_rows, projected_grad)[0]
+        for e in range(EXP_DEV)
     ]
-    down_grad = weight_grad(0, EXP_DEV, jnp.int32(0), FF, hidden, slot_grad)
-
-    def over_dp(expert):
-        total = gate_up_parts[0][expert]
-        for step in range(1, dp_size):
-            total = shifted(total, "dp", 1).astype(f32) + gate_up_parts[step][expert].astype(f32)
-            total = total.astype(bf16)
-        return total[0].reshape(ctx_size, -1, 2 * FF)
-
-    nf_grad_terms, down_grad, gate_up_parts, y_parts = tie(
-        nf_grad_terms, down_grad, gate_up_parts, y_parts
+    came_first = shifted(theirs[0][: half // 2], "dp", 1)
+    mine = [weight_grad(0, 1, dp_here, half, slot_rows, projected_grad)[0]]
+    slot_rows, theirs, mine, came_first = tie(slot_rows, theirs, mine, came_first)
+    came_second = shifted(theirs[0][half // 2 :], "dp", 1)
+    mine.append(weight_grad(1, 1, dp_here, half, slot_rows, projected_grad)[0])
+    other_down = weight_grad(0, EXP_DEV, (dp_here - 1) % dp_size, down_half, hidden, slot_grad)
+    mine_down = weight_grad(0, EXP_DEV, dp_here, down_half, hidden, slot_grad)
+    nf_grad_terms, mine, mine_down, other_down, y_parts = tie(
+        nf_grad_terms, mine, mine_down, other_down, y_parts
     )
 
     mid_grad, mid_grad_low, att_grad, delta, ffn_gain_part = middle_backward(
         nf_grad_terms, mid, g, gain_two, w_out, att
     )
+    mid_grad_low, came_second = tie(mid_grad_low, came_second)
     w_out_grad = dot_tn(att_low, mid_grad_low).astype(bf16)
-    att_grad, w_out_grad = tie(att_grad, w_out_grad)
-    w_out_part = scatter_core(w_out_grad)
+    w_out_part = scatter_core(by_owner(w_out_grad))
+    w_out_part, att_grad = tie(w_out_part, att_grad)
+    w_out_part = scatter_chip(w_out_part)
     y_terms = return_blocks(y_parts)
-    down_parts = down_grad.reshape(EXP_DEV, dp_size, ctx_size, -1, MODEL_WIDTH)
-    down_total = ring_part(down_parts, ctx_here, ctx_size, 0, 2)
-
-    dqs, dkvs = [None] * KEY_VALUE_HEADS, [None] * KEY_VALUE_HEADS
-    gate_up_totals = [None] * EXP_DEV
-    for step in range(ctx_size):
-        back = (step + 1) % ctx_size
-        for group in range(KEY_VALUE_HEADS):
-            dkv = shifted(dkvs[group], "ctx", 1) if step else None
-            ag, other = tie(att_grad, dqs[group - 1]) if step + group else (att_grad, None)
-            if other is not None:
-                dqs[group - 1] = other
-            dqs[group], dkvs[group] = attention_backward(
-                group, q, ag, kv_blocks[back], lse, delta, key_positions[back][:, None],
-                positions[None, :], dqs[group], dkv,
-            )
-        if step < ctx_size - 1:
-            down_total = add_low(
-                shifted(down_total, "ctx", 1), ring_part(down_parts, ctx_here, ctx_size, step + 1, 2)
-            )
-            att_grad, down_total = tie(att_grad, down_total)
-        if step == 0:
-            att_grad, w_out_part, gate_up_totals[0] = tie(att_grad, w_out_part, over_dp(0))
-            w_out_part = scatter_chip(w_out_part)
-        if step == 1:
-            att_grad, y_terms = tie(att_grad, y_terms)
-        if step == 2:
-            att_grad, w_out_part = tie(att_grad, w_out_part)
-    down_share = ring_scatter(
-        down_total, lambda v: shifted(v, "dp", 1), dp_here, dp_size, 1
-    )
-    gate_up_totals[1] = over_dp(1)
+
+    came = jnp.concatenate([came_first, came_second], axis=0)
+    dql, dkv, gate_up_first, came = attention_backward(
+        q, att_grad, kv_blocks, lse, delta, jnp.stack(key_positions)[:, :, None],
+        positions[None, :], cosine, sine, mine[0], came, theirs[1],
+    )
     layer_output = mid
     for term in y_terms:
         layer_output = layer_output + term.astype(f32)
     layer_output = layer_output.astype(bf16)
-    dql = unrotate(dqs, cosine, sine)
-    w_query_grad = dot_tn(normed, dql).astype(bf16)
-    dql, w_query_grad, gate_up_totals = tie(dql, w_query_grad, gate_up_totals)
-    w_query_part = scatter_core(w_query_grad)
+    w_query_grad = by_owner(dot_tn(normed, dql).astype(bf16))
     dkvl, tokens_grad, attn_gain_part = input_backward(
-        dql, dkvs, w_query, key_matrix, value_matrix, cosine, sine, x, gain_one, mid_grad
+        dql, dkv, w_query, key_matrix, value_matrix, cosine, sine, x, gain_one, mid_grad
     )
     w_kv_grad = dot_tn(normed, dkvl)
     gains = jnp.concatenate([attn_gain_part, ffn_gain_part], axis=0).T
     gains = jnp.pad(gains, ((0, 0), (0, HEAD_SIZE - 2)))
-    w_kv_grad = jnp.concatenate([w_kv_grad, gains], axis=1).astype(bf16)
-    gate_up_share = jnp.stack(
-        [sum_at_owner(total, ctx_here, ctx_size) for total in gate_up_totals]
-    )
-    w_out_share = scatter_axis(scatter_axis(w_out_part, "dp"), "ctx")
-    w_query_share = scatter_axis(scatter_axis(scatter_chip(w_query_part), "dp"), "ctx")
-    w_kv_share = scatter_axis(scatter_axis(scatter_chip(scatter_core(w_kv_grad)), "dp"), "ctx")
-    w_kv_share = w_kv_share.astype(f32)
+    w_kv_grad = by_owner(jnp.concatenate([w_kv_grad, gains], axis=1).astype(bf16))
+    gate_up_second, down_share, (w_query_share, w_kv_share, w_out_share) = last_transfers(
+        mine[1], came, mine_down, other_down, w_query_grad, w_kv_grad, w_out_part
+    )
     return (
         layer_output[None],
         tokens_grad[None],
         w_kv_share[:, 2 * KV_WIDTH],
-        w_query_share.astype(f32),
+        w_query_share,
         w_kv_share[:, :KV_WIDTH],
         w_kv_share[:, KV_WIDTH : 2 * KV_WIDTH],
-        w_out_share.astype(f32),
+        w_out_share,
         w_kv_share[:, 2 * KV_WIDTH + 1],
-        gate_up_share,
-        down_share.astype(f32),
+        jnp.stack([gate_up_first, gate_up_second]),
+        down_share,
     )
 
 

time: 648 us -> 552 us (0.85)
  waiting for transfers between devices: 231 us -> 64.6 us
  Pallas kernels: 263 us -> 393 us
  starting transfers between devices: 45.5 us -> 18.3 us
  other arithmetic: 49.7 us -> 27.1 us
    ppermute x33 -> x5, waiting for transfers between devices: 170 us -> 15.4 us  [shifted(): lax.ppermute(value, axis, [(i, (i + steps) % count) for i in range(count)])]
    pallas_call x9 -> x2, Pallas kernels: 72.6 us -> 200 us  [the longest x1 115 us: last_transfers(): pl.pallas_call(functools.partial(last_kernel, plan), in_specs=[vmem] * 3...]
    ppermute x33 -> x5, starting transfers between devices: 33.5 us -> 7.64 us  [shifted(): lax.ppermute(value, axis, [(i, (i + steps) % count) for i in range(count)])]
    convert_element_type x18 -> x2, other arithmetic: 16.3 us -> 3.57 us  [add_low(): return (a.astype(f32) + b.astype(f32)).astype(bf16)]
    convert_element_type x6 -> x0, other arithmetic: 10.1 us -> none  [the longest x2 7.41 us: over_dp(): total = total.astype(bf16)]
    ppermute x8 -> x6, waiting for transfers between devices: 50.9 us -> 41.2 us  [chip_shift(): lax.ppermute(value, 'exp', [(i, (i + 2 * steps) % count) for i in range(c...]
    unnamed x94 -> x69, local copies, waits for them, and re-layouts: 14.2 us -> 10.1 us
    pallas_call x5 -> x6, Pallas kernels: 39.7 us -> 42 us  [weight_grad(): pl.pallas_call(weight_grad_kernel, grid_spec=pltpu.PrefetchScalarGridSpec...]
  transfers between devices with their start and end apart: 54 -> 22, of which waited for: 26 -> 10; matrix products, arithmetic and copies ran while one was open for 12% -> 8% of each run, Pallas kernels for 24% -> 37%
where the time goes in v3:
time: 552 us; the launch traced here: 545 us
  Pallas kernels  393 us (71%)
  waiting for transfers between devices  64.6 us (12%)
  local copies, waits for them, and re-layouts  30 us (5%)
  other arithmetic  27.1 us (5%)
  starting transfers between devices  18.3 us (3%)
  matrix products  10.5 us (2%)
    pallas_call x1, Pallas kernels, last_transfers(): pl.pallas_call(functools.partial(last_kernel, plan), in_specs=[vmem] * 3...  115 us
    pallas_call x1, Pallas kernels, attention_backward(): pl.pallas_call(functools.partial(attention_back_kernel, n), in_specs=[vme...  85 us
    pallas_call x2, Pallas kernels, expert_blocks(): pl.pallas_call(functools.partial(expert_kernel, count), grid=(count, EXP_...  81.9 us
    pallas_call x6, Pallas kernels, weight_grad(): pl.pallas_call(weight_grad_kernel, grid_spec=pltpu.PrefetchScalarGridSpec...  42 us
    ppermute x6, waiting for transfers between devices, chip_shift(): lax.ppermute(value, 'exp', [(i, (i + 2 * steps) % count) for i in range(c...  41.2 us
    pallas_call x1, Pallas kernels, attention_forward(): pl.pallas_call(attention_kernel, grid=(QUERY_HEADS,), in_specs=[pl.BlockS...  35.6 us
    ppermute x5, waiting for transfers between devices, shifted(): lax.ppermute(value, axis, [(i, (i + steps) % count) for i in range(count)])  15.4 us
    pallas_call x1, Pallas kernels, middle_backward(): pl.pallas_call(middle_kernel, out_shape=(jax.ShapeDtypeStruct((rows, MODE...  12 us
  transfers between devices with their start and end apart: 22, of which 10 were waited for; matrix products, arithmetic and copies ran while one was open for 8% of the time, Pallas kernels for 37%

profile of v3, /device:TPU:0, one launch (start us, length us, event | category | flops | bytes accessed | tf_op | source)
XLA Modules:
  0.0 544.9 jit_solution(14047183304854940627)
XLA Ops:
  4.4 2.9 collective-permute-start.7
  10.1 4.2 norm_kv.1
  14.3 3.6 collective-permute-start.2
  20.4 21.9 %collective-permute-done.7.refs_3_ = bf16[512,1536]{1,0:T(8,128)(2,1)} collective-permute-done((bf16[512,1536]{1,0:T(8,128)(2,1)}, bf16[512,1536]{1,0:T(8,128)(2,1)}, u32[]{:S(2)}, u32[]{:S(2)}) %collective-permute-start.7) | collective-permute-done | bytes 1572896 | tf_op jit(solution)/shard_map/ppermute | solution.py:797
  45.0 6.8 %query_projection.1.q_ref = bf16[512,1536]{1,0:T(8,128)(2,1)} custom-call(bf16[512,1536]{1,0:T(8,128)(2,1)} %get-tuple-element.82.normed_ref, bf16[1536,1536]{1,0:T(8,128)(2,1)} %wq_ref.3, f32[512,128]{1,0:T(8,128)} %pad_maximum_fusion.4.cos_ref, f32[512,128]{1,0:T(8,128)} %pad_maximum_fusion.5.sin_ref), custom_call_target="tpu_custom_call" | custom-call | flops 75497472 | bytes 250000 | tf_op jit(solution)/shard_map/query_projection/pallas_call | solution.py:110
  53.6 2.2 collective-permute-done.4
  57.0 5.9 %collective-permute-done.1.refs_2_ = bf16[512,512]{1,0:T(8,128)(2,1)S(1)} collective-permute-done((bf16[512,512]{1,0:T(8,128)(2,1)}, bf16[512,512]{1,0:T(8,128)(2,1)S(1)}, u32[]{:S(2)}, u32[]{:S(2)}) %collective-permute-start.1) | collective-permute-done | bytes 524320 | tf_op jit(solution)/shard_map/ppermute | solution.py:788
  64.6 35.6 %attention_forward.1 = (f32[512,1536]{1,0:T(8,128)}, bf16[512,1536]{1,0:T(8,128)(2,1)}, f32[16,512]{1,0:T(8,128)}, f32[512,1536]{1,0:T(8,128)}, bf16[512,1536]{1,0:T(8,128)(2,1)}) custom-call(bf16[512,1536]{1,0:T(8,128)(2,1)} %query_projection.1.q_ref, bf16[2048,512]{1,0:T(8,128)(2,1)} %pad_maximum_fusion.2.k_ref.v_ref, ...), custom_call_target="tpu_custom_call" | custom-call | flops 402653184 | bytes 625000 | tf_op jit(solution)/shard_map/attention_forward/pallas_call | solution.py:166
  100.2 3.6 collective-permute-done.9.refs_1_
  106.9 40.9 %expert_blocks.2 = (bf16[512,1536]{1,0:T(8,128)(2,1)}, bf16[512,1536]{1,0:T(8,128)(2,1)}, bf16[512,1536]{1,0:T(8,128)(2,1)}, bf16[512,1536]{1,0:T(8,128)(2,1)}, ...) custom-call(s32[2,2,1,512]{3,2,1,0:T(1,128)} %copy.54.pos_row_ref, ...), custom_call_target="tpu_custom_call" | custom-call | flops 1101004800 | bytes 1875000 | tf_op jit(solution)/shard_map/expert_blocks/pallas_call | solution.py:279
  152.5 40.9 %expert_blocks.3 = (bf16[512,1536]{1,0:T(8,128)(2,1)}, bf16[512,1536]{1,0:T(8,128)(2,1)}, bf16[512,1536]{1,0:T(8,128)(2,1)}, bf16[512,1536]{1,0:T(8,128)(2,1)}, ...) custom-call(s32[2,2,1,512]{3,2,1,0:T(1,128)} %copy.57.pos_row_ref, ...), custom_call_target="tpu_custom_call", output_to_operand_aliasing={{4}: (9, {}), {5}: (10, {}), {6}: (11, {}), {7}: (12, {})} | custom-call | flops 1101004800 | bytes 1875000 | tf_op jit(solution)/shard_map/expert_blocks/pallas_call | solution.py:279
  193.6 6.9 %weight_grad.6 = bf16[1,768,1536]{2,1,0:T(8,128)(2,1)} custom-call(s32[1]{0:T(128)} %bitcast.23.chunk_ref, bf16[2,1280,1536]{2,1,0:T(8,128)(2,1)} %bitcast.120, bf16[2,1280,1536]{2,1,0:T(8,128)(2,1)} %bitcast.124), custom_call_target="tpu_custom_call" | custom-call | flops 94371840 | bytes 625000 | tf_op jit(solution)/shard_map/weight_grad/pallas_call | solution.py:318
  200.5 2.5 slice_bitcast_fusion
  207.6 6.9 %weight_grad.7 = bf16[1,768,1536]{2,1,0:T(8,128)(2,1)} custom-call(s32[1]{0:T(128)} %bitcast.23.chunk_ref, bf16[2,1280,1536]{2,1,0:T(8,128)(2,1)} %bitcast.121, bf16[2,1280,1536]{2,1,0:T(8,128)(2,1)} %bitcast.125), custom_call_target="tpu_custom_call" | custom-call | flops 94371840 | bytes 625000 | tf_op jit(solution)/shard_map/weight_grad/pallas_call | solution.py:318
  214.5 7.5 %weight_grad.8 = bf16[1,768,1536]{2,1,0:T(8,128)(2,1)} custom-call(s32[1]{0:T(128)} %bitcast.27.chunk_ref, bf16[2,1280,1536]{2,1,0:T(8,128)(2,1)} %bitcast.122, bf16[2,1280,1536]{2,1,0:T(8,128)(2,1)} %bitcast.126), custom_call_target="tpu_custom_call" | custom-call | flops 94371840 | bytes 625000 | tf_op jit(solution)/shard_map/weight_grad/pallas_call | solution.py:318
  222.0 9.5 %collective-permute-done.15 = bf16[384,1536]{1,0:T(8,128)(2,1)} collective-permute-done((bf16[384,1536]{1,0:T(8,128)(2,1)}, bf16[384,1536]{1,0:T(8,128)(2,1)}, u32[]{:S(2)}, u32[]{:S(2)}) %collective-permute-start.15) | collective-permute-done | bytes 1179680 | tf_op jit(solution)/shard_map/ppermute | solution.py:788
  234.1 6.9 %weight_grad.10.refs_2_ = bf16[2,384,1536]{2,1,0:T(8,128)(2,1)} custom-call(s32[1]{0:T(128)} %bitcast.27.chunk_ref, bf16[2,1280,768]{2,1,0:T(8,128)(2,1)} %bitcast.130, bf16[2,1280,1536]{2,1,0:T(8,128)(2,1)} %bitcast.128), custom_call_target="tpu_custom_call" | custom-call | flops 94371840 | bytes 625000 | tf_op jit(solution)/shard_map/weight_grad/pallas_call | solution.py:318
  241.0 6.9 %weight_grad.11.refs_3_ = bf16[2,384,1536]{2,1,0:T(8,128)(2,1)} custom-call(s32[1]{0:T(128)} %bitcast.23.chunk_ref, bf16[2,1280,768]{2,1,0:T(8,128)(2,1)} %bitcast.131, bf16[2,1280,1536]{2,1,0:T(8,128)(2,1)} %bitcast.129), custom_call_target="tpu_custom_call" | custom-call | flops 94371840 | bytes 625000 | tf_op jit(solution)/shard_map/weight_grad/pallas_call | solution.py:318
  247.9 7.0 %weight_grad.9 = bf16[1,768,1536]{2,1,0:T(8,128)(2,1)} custom-call(s32[1]{0:T(128)} %bitcast.27.chunk_ref, bf16[2,1280,1536]{2,1,0:T(8,128)(2,1)} %bitcast.123, bf16[2,1280,1536]{2,1,0:T(8,128)(2,1)} %bitcast.127), custom_call_target="tpu_custom_call" | custom-call | flops 94371840 | bytes 625000 | tf_op jit(solution)/shard_map/weight_grad/pallas_call | solution.py:318
  256.1 12.0 %middle_backward.1 = (f32[512,1536]{1,0:T(8,128)}, bf16[512,1536]{1,0:T(8,128)(2,1)}, bf16[512,1536]{1,0:T(8,128)(2,1)}, f32[16,512]{1,0:T(8,128)}, f32[1,1536]{1,0:T(1,128)}) custom-call(bf16[512,1536]{1,0:T(8,128)(2,1)} %get-tuple-element.121.refs_0_, bf16[512,1536]{1,0:T(8,128)(2,1)} %copy-done.12, bf16[512,1536]{1,0:T(8,128)(2,1)} %collective-permute-done.14.refs_2_, ...), custom_call_target="tpu_custom_call" | custom-call | flops 75497472 | bytes 625000 | tf_op jit(solution)/shard_map/middle_backward/pallas_call | solution.py:373
  268.1 5.0 convolution_convert_fusion.1
  277.6 3.4 pad_maximum_fusion.came_ref
  282.4 3.4 add_convert_fusion.1
  287.4 2.3 fusion
  289.7 85.0 %attention_backward.1 = (bf16[512,1536]{1,0:T(8,128)(2,1)}, bf16[512,512]{1,0:T(8,128)(2,1)}, f32[192,1536]{1,0:T(8,128)}, bf16[768,1536]{1,0:T(8,128)(2,1)}) custom-call(bf16[512,1536]{1,0:T(8,128)(2,1)} %query_projection.1.q_ref, bf16[512,1536]{1,0:T(8,128)(2,1)} %get-tuple-element.129.ag_ref, f32[16,512]{1,0:T(8,128)} %get-tuple-element.130.lse_ref, ...), custom_call_target="tpu_custom_call" | custom-call | flops 503316480 | bytes 1250000 | tf_op jit(solution)/shard_map/attention_backward/pallas_call | solution.py:555
  374.7 4.5 convolution_convert_fusion
  379.2 2.5 copy.61
  381.7 10.6 %input_backward.1 = (bf16[512,512]{1,0:T(8,128)(2,1)}, bf16[512,1536]{1,0:T(8,128)(2,1)}, f32[1,1536]{1,0:T(1,128)}) custom-call(bf16[512,1536]{1,0:T(8,128)(2,1)} %get-tuple-element.136.dql_ref, bf16[512,512]{1,0:T(8,128)(2,1)} %get-tuple-element.137.dkv_ref, bf16[1536,1536]{1,0:T(8,128)(2,1)} %wq_ref.3, bf16[1536,256]{1,0:T(8,128)(2,1)} %wk_ref.3, ...), custom_call_target="tpu_custom_call" | custom-call | flops 100663296 | bytes 625000 | tf_op jit(solution)/shard_map/input_backward/pallas_call | solution.py:611
  398.9 4.0 fusion.2
  402.9 17.1 %collective-permute-done.21 = bf16[384,1536]{1,0:T(8,128)(2,1)S(1)} collective-permute-done((bf16[384,1536]{1,0:T(8,128)(2,1)S(1)}, bf16[384,1536]{1,0:T(8,128)(2,1)S(1)}, u32[]{:S(2)}, u32[]{:S(2)}) %collective-permute-start.21) | collective-permute-done | bytes 1179680 | tf_op jit(solution)/shard_map/ppermute | solution.py:797
  421.3 115.0 %last_transfers.1 = (f32[192,1536]{1,0:T(8,128)}, f32[2,96,1536]{2,1,0:T(8,128)}, f32[48,1536]{1,0:T(8,128)}, f32[48,640]{1,0:T(8,128)}, f32[48,1536]{1,0:T(8,128)}) custom-call(bf16[768,1536]{1,0:T(8,128)(2,1)} %bitcast.141, bf16[768,1536]{1,0:T(8,128)(2,1)} %get-tuple-element.141.refs_1_, bf16[2,384,1536]{2,1,0:T(8,128)(2,1)} %weight_grad.10.refs_2_, ...), custom_call_target="tpu_custom_call" | custom-call | flops 31250 | bytes 1250000 | tf_op jit(solution)/shard_map/last_transfers/pallas_call | solution.py:767
  539.3 3.0 pad_maximum_fusion.1
  (159 shorter events, 53.4 us)
Async XLA Ops:
  0.6 3.8 collective-permute-start.6
  4.4 9.9 %copy-start.11 = (bf16[512,1536]{1,0:T(8,128)(2,1)}, bf16[512,1536]{1,0:T(8,128)(2,1)S(1)}, u32[]{:S(2)}) copy-start(bf16[512,1536]{1,0:T(8,128)(2,1)S(1)} %collective-permute-done.6.refs_3_) | copy-start | bytes 4718596
  4.4 37.9 %collective-permute-start.7 = (bf16[512,1536]{1,0:T(8,128)(2,1)}, bf16[512,1536]{1,0:T(8,128)(2,1)}, u32[]{:S(2)}, u32[]{:S(2)}) collective-permute-start(bf16[512,1536]{1,0:T(8,128)(2,1)} %bitcast.146), channel_id=1, source_target_pairs={{0,2},{1,3},{2,0},{3,1},{4,6},{5,7},{6,4},{7,5},{8,10},{9,11},{10,... | collective-permute-start | bytes 4718600 | tf_op jit(solution)/shard_map/ppermute | solution.py:797
  9.2 9.6 %copy-start.21 = (s32[1,512,4]{1,2,0:T(4,128)S(1)}, s32[1,512,4]{1,2,0:T(4,128)}, u32[]{:S(2)}) copy-start(s32[1,512,4]{1,2,0:T(4,128)} %param.22) | copy-start | bytes 24580
  9.2 11.1 %copy-start.23 = (f32[1,512,4]{1,2,0:T(4,128)S(1)}, f32[1,512,4]{1,2,0:T(4,128)}, u32[]{:S(2)}) copy-start(f32[1,512,4]{1,2,0:T(4,128)} %param.23) | copy-start | bytes 24580
  10.1 34.3 %copy-start.22 = (f32[1536]{0:T(1024)S(1)}, f32[1536]{0:T(1024)}, u32[]{:S(2)}) copy-start(f32[1536]{0:T(1024)} %param.19) | copy-start | bytes 18436
  14.3 42.7 %collective-permute-start.2 = (bf16[512,512]{1,0:T(8,128)(2,1)}, bf16[512,512]{1,0:T(8,128)(2,1)S(1)}, u32[]{:S(2)}, u32[]{:S(2)}) collective-permute-start(bf16[512,512]{1,0:T(8,128)(2,1)} %get-tuple-element.83.refs_0_), channel_id=1, source_target_pairs={{0,12},{4,0},{8,4},{12,8},{1,13},{5,1},{9,5},{13,9},{2,14},{6,2},{... | collective-permute-start | bytes 1572872 | tf_op jit(solution)/shard_map/ppermute | solution.py:788
  17.9 45.0 %collective-permute-start.1 = (bf16[512,512]{1,0:T(8,128)(2,1)}, bf16[512,512]{1,0:T(8,128)(2,1)S(1)}, u32[]{:S(2)}, u32[]{:S(2)}) collective-permute-start(bf16[512,512]{1,0:T(8,128)(2,1)} %get-tuple-element.83.refs_0_), channel_id=1, source_target_pairs={{0,8},{4,12},{8,0},{12,4},{1,9},{5,13},{9,1},{13,5},{2,10},{6,14},... | collective-permute-start | bytes 1572872 | tf_op jit(solution)/shard_map/ppermute | solution.py:788
  17.9 45.0 %collective-permute-start = (bf16[512,512]{1,0:T(8,128)(2,1)}, bf16[512,512]{1,0:T(8,128)(2,1)S(1)}, u32[]{:S(2)}, u32[]{:S(2)}) collective-permute-start(bf16[512,512]{1,0:T(8,128)(2,1)} %get-tuple-element.83.refs_0_), channel_id=1, source_target_pairs={{0,4},{4,8},{8,12},{12,0},{1,5},{5,9},{9,13},{13,1},{2,6},{6,10},{... | collective-permute-start | bytes 1572872 | tf_op jit(solution)/shard_map/ppermute | solution.py:788
  42.3 22.2 %collective-permute-start.8 = (bf16[512,1536]{1,0:T(8,128)(2,1)}, bf16[512,1536]{1,0:T(8,128)(2,1)}, u32[]{:S(2)}, u32[]{:S(2)}) collective-permute-start(bf16[512,1536]{1,0:T(8,128)(2,1)} %collective-permute-done.7.refs_3_), channel_id=1, source_target_pairs={{0,1},{1,0},{2,3},{3,2},{4,5},{5,4},{6,7},{7,6},{8,9},{9,8},{10,11... | collective-permute-start | bytes 4718600 | tf_op jit(solution)/shard_map/ppermute | solution.py:792
  42.3 9.5 %collective-permute-start.3 = (f32[2,8,512]{2,1,0:T(8,128)S(1)}, f32[2,8,512]{2,1,0:T(8,128)S(1)}, u32[]{:S(2)}, u32[]{:S(2)}) collective-permute-start(f32[2,8,512]{2,1,0:T(8,128)S(1)} %fusion.5), channel_id=1, source_target_pairs={{0,1},{1,0},{2,3},{3,2},{4,5},{5,4},{6,7},{7,6},{8,9},{9,8},{10,11... | collective-permute-start | bytes 98312 | tf_op jit(solution)/shard_map/ppermute | solution.py:792
  43.5 232.6 %copy-start.20 = (s32[1,1,2,256]{3,1,2,0:T(1,128)}, s32[1,1,2,256]{3,1,2,0:T(1,128)S(1)}, u32[]{:S(2)}) copy-start(s32[1,1,2,256]{3,1,2,0:T(1,128)S(1)} %copy.68) | copy-start | bytes 6148
  45.0 17.9 %copy-start.3 = (bf16[512,512]{1,0:T(8,128)(2,1)S(1)}, bf16[512,512]{1,0:T(8,128)(2,1)}, u32[]{:S(2)}) copy-start(bf16[512,512]{1,0:T(8,128)(2,1)} %get-tuple-element.83.refs_0_) | copy-start | bytes 1572868
  51.8 3.9 collective-permute-start.4
  55.8 1.2 collective-permute-start.5
  100.2 3.6 collective-permute-start.9
  103.8 44.0 %collective-permute-start.10 = (bf16[512,1536]{1,0:T(8,128)(2,1)}, bf16[512,1536]{1,0:T(8,128)(2,1)S(1)}, u32[]{:S(2)}, u32[]{:S(2)}) collective-permute-start(bf16[512,1536]{1,0:T(8,128)(2,1)} %get-tuple-element.94.refs_0_), channel_id=1, source_target_pairs={{0,2},{1,3},{2,0},{3,1},{4,6},{5,7},{6,4},{7,5},{8,10},{9,11},{10,... | collective-permute-start | bytes 4718600 | tf_op jit(solution)/shard_map/ppermute | solution.py:797
  147.8 3.5 collective-permute-start.12
  193.4 11.2 %collective-permute-start.13 = (bf16[512,1536]{1,0:T(8,128)(2,1)}, bf16[512,1536]{1,0:T(8,128)(2,1)S(1)}, u32[]{:S(2)}, u32[]{:S(2)}) collective-permute-start(bf16[512,1536]{1,0:T(8,128)(2,1)} %get-tuple-element.104), channel_id=1, source_target_pairs={{0,1},{1,0},{2,3},{3,2},{4,5},{5,4},{6,7},{7,6},{8,9},{9,8},{10,11... | collective-permute-start | bytes 4718600 | tf_op jit(solution)/shard_map/ppermute | solution.py:792
  203.0 28.6 %collective-permute-start.15 = (bf16[384,1536]{1,0:T(8,128)(2,1)}, bf16[384,1536]{1,0:T(8,128)(2,1)}, u32[]{:S(2)}, u32[]{:S(2)}) collective-permute-start(bf16[384,1536]{1,0:T(8,128)(2,1)} %slice_bitcast_fusion), channel_id=1, source_target_pairs={{0,16},{16,0},{1,17},{17,1},{2,18},{18,2},{3,19},{19,3},{4,20},{20... | collective-permute-start | bytes 3538952 | tf_op jit(solution)/shard_map/ppermute | solution.py:788
  204.5 50.4 %collective-permute-start.11 = (bf16[512,1536]{1,0:T(8,128)(2,1)}, bf16[512,1536]{1,0:T(8,128)(2,1)S(1)}, u32[]{:S(2)}, u32[]{:S(2)}) collective-permute-start(bf16[512,1536]{1,0:T(8,128)(2,1)} %get-tuple-element.96), channel_id=1, source_target_pairs={{0,1},{1,0},{2,3},{3,2},{4,5},{5,4},{6,7},{7,6},{8,9},{9,8},{10,11... | collective-permute-start | bytes 4718600 | tf_op jit(solution)/shard_map/ppermute | solution.py:792
  206.1 48.8 %collective-permute-start.14 = (bf16[512,1536]{1,0:T(8,128)(2,1)}, bf16[512,1536]{1,0:T(8,128)(2,1)}, u32[]{:S(2)}, u32[]{:S(2)}) collective-permute-start(bf16[512,1536]{1,0:T(8,128)(2,1)} %add_convert_fusion.2), channel_id=1, source_target_pairs={{0,2},{1,3},{2,0},{3,1},{4,6},{5,7},{6,4},{7,5},{8,10},{9,11},{10,... | collective-permute-start | bytes 4718600 | tf_op jit(solution)/shard_map/ppermute | solution.py:797
  214.5 17.0 %copy-start.2 = (bf16[1,768,1536]{2,1,0:T(8,128)(2,1)S(1)}, bf16[1,768,1536]{2,1,0:T(8,128)(2,1)}, u32[]{:S(2)}) copy-start(bf16[1,768,1536]{2,1,0:T(8,128)(2,1)} %weight_grad.6) | copy-start | bytes 7077892
  232.6 35.4 %collective-permute-start.19 = (bf16[384,1536]{1,0:T(8,128)(2,1)}, bf16[384,1536]{1,0:T(8,128)(2,1)S(1)}, u32[]{:S(2)}, u32[]{:S(2)}) collective-permute-start(bf16[384,1536]{1,0:T(8,128)(2,1)} %slice.79), channel_id=1, source_target_pairs={{0,16},{16,0},{1,17},{17,1},{2,18},{18,2},{3,19},{19,3},{4,20},{20... | collective-permute-start | bytes 3538952 | tf_op jit(solution)/shard_map/ppermute | solution.py:788
  275.6 11.7 %collective-permute-start.20 = (bf16[2,384,1536]{2,1,0:T(8,128)(2,1)S(1)}, bf16[2,384,1536]{2,1,0:T(8,128)(2,1)}, u32[]{:S(2)}, u32[]{:S(2)}) collective-permute-start(bf16[2,384,1536]{2,1,0:T(8,128)(2,1)S(1)} %dynamic-slice_bitcast_fusion), channel_id=1, source_target_pairs={{0,1},{1,0},{2,3},{3,2},{4,5},{5,4},{6,7},{7,6},{8,9},{9,8},{10,11... | collective-permute-start | bytes 7077896 | tf_op jit(solution)/shard_map/ppermute | solution.py:792
  275.6 6.8 %collective-permute-start.17 = (bf16[512,1536]{1,0:T(8,128)(2,1)}, bf16[512,1536]{1,0:T(8,128)(2,1)}, u32[]{:S(2)}, u32[]{:S(2)}) collective-permute-start(bf16[512,1536]{1,0:T(8,128)(2,1)} %get-tuple-element.118), channel_id=1, source_target_pairs={{0,1},{1,0},{2,3},{3,2},{4,5},{5,4},{6,7},{7,6},{8,9},{9,8},{10,11... | collective-permute-start | bytes 4718600 | tf_op jit(solution)/shard_map/ppermute | solution.py:792
  276.2 11.2 %slice-start = ((s8[4718592]{0:T(1024)(128)(4,1)}), s8[524288]{0:T(1024)(128)(4,1)S(1)}, s32[]{:S(2)}) async-start(s8[4718592]{0:T(1024)(128)(4,1)} %bitcast.133), calls=%async_computation | async-start | bytes 1048576
  277.5 119.9 %collective-permute-start.16 = (bf16[512,1536]{1,0:T(8,128)(2,1)}, bf16[512,1536]{1,0:T(8,128)(2,1)}, u32[]{:S(2)}, u32[]{:S(2)}) collective-permute-start(bf16[512,1536]{1,0:T(8,128)(2,1)} %get-tuple-element.117), channel_id=1, source_target_pairs={{0,1},{1,0},{2,3},{3,2},{4,5},{5,4},{6,7},{7,6},{8,9},{9,8},{10,11... | collective-permute-start | bytes 4718600 | tf_op jit(solution)/shard_map/ppermute | solution.py:792
  277.6 9.8 %slice-start.1 = ((s8[4718592]{0:T(1024)(128)(4,1)}), s8[4194304]{0:T(1024)(128)(4,1)S(1)}, s32[]{:S(2)}) async-start(s8[4718592]{0:T(1024)(128)(4,1)} %bitcast.133), calls=%async_computation.1 | async-start | bytes 8388608
  285.8 111.6 %collective-permute-start.18 = (bf16[512,1536]{1,0:T(8,128)(2,1)}, bf16[512,1536]{1,0:T(8,128)(2,1)}, u32[]{:S(2)}, u32[]{:S(2)}) collective-permute-start(bf16[512,1536]{1,0:T(8,128)(2,1)} %add_convert_fusion.1), channel_id=1, source_target_pairs={{0,2},{1,3},{2,0},{3,1},{4,6},{5,7},{6,4},{7,5},{8,10},{9,11},{10,... | collective-permute-start | bytes 4718600 | tf_op jit(solution)/shard_map/ppermute | solution.py:797
  393.4 26.6 %collective-permute-start.21 = (bf16[384,1536]{1,0:T(8,128)(2,1)S(1)}, bf16[384,1536]{1,0:T(8,128)(2,1)S(1)}, u32[]{:S(2)}, u32[]{:S(2)}) collective-permute-start(bf16[384,1536]{1,0:T(8,128)(2,1)S(1)} %dynamic-slice_bitcast_fusion.1), channel_id=1, source_target_pairs={{0,2},{1,3},{2,0},{3,1},{4,6},{5,7},{6,4},{7,5},{8,10},{9,11},{10,... | collective-permute-start | bytes 3538952 | tf_op jit(solution)/shard_map/ppermute | solution.py:797
  421.3 118.0 %copy-start.17 = (f32[192,1536]{1,0:T(8,128)S(1)}, f32[192,1536]{1,0:T(8,128)}, u32[]{:S(2)}) copy-start(f32[192,1536]{1,0:T(8,128)} %get-tuple-element.151) | copy-start | bytes 3538948
  (18 other events, 53.7 us)

commit v4 on v3

v4 whole, which is shorter than its diff:
```python
import functools
import math

import jax
import jax.numpy as jnp
from jax import lax
from jax.experimental import pallas as pl
from jax.experimental.pallas import tpu as pltpu
from jax.sharding import PartitionSpec as P

MODEL_WIDTH = 1536
QUERY_HEADS = 12
KEY_VALUE_HEADS = 2
GROUP = QUERY_HEADS // KEY_VALUE_HEADS
HEAD_SIZE = 128
KV_WIDTH = KEY_VALUE_HEADS * HEAD_SIZE
FF = 768
TOPK = 4
EXP_DEV = 2
TOK_DEV = 512
HALF = 256

epsilon = 1e-06
rope_base = 1000000.0
masked_score = -1e30
score_scale = HEAD_SIZE ** (-0.5)
score_to_log2 = score_scale * math.log2(math.e)
gelu_c = math.sqrt(2.0 / math.pi)

f32 = jnp.float32
bf16 = jnp.bfloat16
NT = (((1,), (1,)), ((), ()))
TN = (((0,), (0,)), ((), ()))
VMEM_BYTES = 63 * 1024 * 1024
MESH = pl.DeviceIdType.MESH


def dot(a, b):
    return jnp.dot(a, b, preferred_element_type=f32)


def dot_nt(a, b):
    return lax.dot_general(a, b, NT, preferred_element_type=f32)


def dot_tn(a, b):
    return lax.dot_general(a, b, TN, preferred_element_type=f32)


def params(**more):
    return pltpu.CompilerParams(vmem_limit_bytes=VMEM_BYTES, **more)


def cost(flops, size, exps=0):
    return pl.CostEstimate(flops=int(flops) // 32, bytes_accessed=int(size) // 32, transcendentals=int(exps) // 32)


def whole(shape):
    return pl.BlockSpec(shape, lambda *_: (0,) * len(shape))


def rotate(values, cosine, signed_sine):
    return values * cosine + pltpu.roll(values, HEAD_SIZE // 2, 1) * signed_sine


def rotate_back(values, cosine, signed_sine):
    return values * cosine - pltpu.roll(values, HEAD_SIZE // 2, 1) * signed_sine


HEAD_ROWS = 16


class Gather:
    def __init__(self, own, slots, send_sem, recv_sem):
        self.own, self.slots, self.send_sem, self.recv_sem = own, slots, send_sem, recv_sem
        self.chips = lax.axis_size("exp") // 2
        exp = lax.axis_index("exp")
        core, chip = lax.rem(exp, 2), exp // 2
        self.other = {"exp": chip * 2 + 1 - core}
        self.ahead = [
            {"exp": lax.rem(chip + s, self.chips) * 2 + core} for s in range(self.chips)
        ]
        self.behind = [
            {"exp": lax.rem(chip + self.chips - s, self.chips) * 2 + core}
            for s in range(self.chips)
        ]

    def neighbours(self):
        if self.chips == 2:
            return [self.other, self.ahead[1]]
        return [self.other] + self.ahead[1:]

    def copy(self, slot):
        source, device = self.own, self.other
        if slot > 1 and slot % 2 == 0:
            source = self.slots.at[slot + 1]
        elif slot > 1:
            device = self.ahead[slot // 2]
        return remote(
            source, self.slots.at[slot], self.send_sem.at[slot], self.recv_sem.at[slot], device
        )

    def start(self):
        self.copy(1).start()
        for s in range(1, self.chips):
            self.copy(2 * s + 1).start()

    def cross(self):
        for s in range(1, self.chips):
            self.copy(2 * s + 1).wait_recv()
            self.copy(2 * s).start()

    def finish(self):
        self.copy(1).wait_recv()
        for s in range(1, self.chips):
            self.copy(2 * s).wait_recv()
        for slot in range(1, 2 * self.chips):
            self.copy(slot).wait_send()


def forward_kernel(
    n, x_ref, gain_ref, wk_ref, wv_ref, cos_ref, sin_ref, qpos_ref, kpos_ref, ffn_gain_ref, wq_hbm,
    wo_hbm, g_hbm, routing_hbm, normed_ref, q_ref, kv_ref, att_ref, att_low_ref, lse_ref, mid_ref,
    nf_ref, g_all, routing_all, wq_ref, wo_ref, tops, totals, load_sem, send_sem, recv_sem,
    g_send_sem, g_recv_sem, routing_send_sem, routing_recv_sem,
):
    load_q = pltpu.make_async_copy(wq_hbm, wq_ref, load_sem.at[0])
    load_o = pltpu.make_async_copy(wo_hbm, wo_ref, load_sem.at[1])
    load_q.start()
    load_o.start()
    ctx = Axis("ctx")
    gathers = [
        Gather(routing_hbm, routing_all, routing_send_sem, routing_recv_sem),
        Gather(g_hbm, g_all, g_send_sem, g_recv_sem),
    ]
    signal_and_wait(ctx.neighbours() + gathers[0].neighbours())
    for gather in gathers:
        gather.start()

    def pass_on(step):
        return remote(
            kv_ref.at[step], kv_ref.at[step + 1], send_sem.at[step], recv_sem.at[step], ctx.next
        )

    rows = x_ref.shape[0]
    x = x_ref[...].astype(f32)
    r = lax.rsqrt(jnp.mean(x * x, axis=-1, keepdims=True) + epsilon)
    normed_ref[...] = (x * r * gain_ref[...]).astype(bf16)
    normed = normed_ref[...]
    cosine, sine = cos_ref[...], sin_ref[...]
    keys = dot(normed, wk_ref[...])
    for head in range(KEY_VALUE_HEADS):
        span = slice(head * HEAD_SIZE, (head + 1) * HEAD_SIZE)
        kv_ref[0, :, span] = rotate(keys[:, span], cosine, sine).astype(bf16)
    kv_ref[0, :, KV_WIDTH:] = dot(normed, wv_ref[...]).astype(bf16)
    pass_on(0).start()
    load_q.wait()
    for start in range(0, MODEL_WIDTH, WIDTH_TILE):
        queries = dot(normed, wq_ref[:, start : start + WIDTH_TILE])
        for offset in range(0, WIDTH_TILE, HEAD_SIZE):
            span = slice(start + offset, start + offset + HEAD_SIZE)
            part = queries[:, offset : offset + HEAD_SIZE]
            q_ref[:, span] = rotate(part, cosine, sine).astype(bf16)

    for step in range(n):
        if step:
            pass_on(step - 1).wait_recv()
            if step < n - 1:
                pass_on(step).start()
        allowed = kpos_ref[step] <= qpos_ref[...]

        def one_group(group, carry):
            keys = kv_ref[step, :, pl.ds(pl.multiple_of(group * HEAD_SIZE, HEAD_SIZE), HEAD_SIZE)]
            start = pl.multiple_of(KV_WIDTH + group * HEAD_SIZE, HEAD_SIZE)
            values = kv_ref[step, :, pl.ds(start, HEAD_SIZE)]
            for member in range(GROUP):
                head = group * GROUP + member
                columns = pl.ds(pl.multiple_of(head * HEAD_SIZE, HEAD_SIZE), HEAD_SIZE)
                lane = slice(member, member + 1)
                scores = jnp.where(allowed, dot_nt(q_ref[:, columns], keys), masked_score)
                top = jnp.max(scores, axis=-1, keepdims=True) * score_to_log2
                if step:
                    before = tops[group, :, lane]
                    top = jnp.maximum(before, top)
                    rescale = jnp.exp2(before - top)
                weights = jnp.exp2(scores * score_to_log2 - top)
                total = jnp.sum(weights, axis=-1, keepdims=True)
                out = dot(weights.astype(bf16), values)
                if step:
                    total += totals[group, :, lane] * rescale
                    out += att_ref[:, columns] * rescale
                if step < n - 1:
                    tops[group, :, lane] = top
                    totals[group, :, lane] = total
                else:
                    out /= total
                    att_low_ref[:, columns] = out.astype(bf16)
                    tops[group, :, lane] = top + jnp.log2(total)
                att_ref[:, columns] = out
            return carry

        lax.fori_loop(0, KEY_VALUE_HEADS, one_group, 0)
    for group in range(KEY_VALUE_HEADS):
        lse_ref[group * GROUP : (group + 1) * GROUP, :] = tops[group].T[:GROUP, :]
    lse_ref[QUERY_HEADS:, :] = jnp.zeros((HEAD_ROWS - QUERY_HEADS, rows), f32)
    for gather in gathers:
        gather.cross()
    load_o.wait()
    half = rows // 2
    for part in range(2):
        band = slice(part * half, (part + 1) * half)
        mid = x_ref[band, :].astype(f32) + dot(att_low_ref[band, :], wo_ref[...])
        mid_ref[band, :] = mid
        r = lax.rsqrt(jnp.mean(mid * mid, axis=-1, keepdims=True) + epsilon)
        nf_ref[band, :] = (mid * r * ffn_gain_ref[...]).astype(bf16)
    for step in range(n - 1):
        pass_on(step).wait_send()
    for gather in gathers:
        gather.finish()


def forward_to_experts(
    x, gain, wk, wv, cosine, sine, qpos_col, kpos_rows, ffn_gain, wq, wo, g, routing
):
    exp_size = lax.axis_size("exp")
    rows, n = x.shape[0], kpos_rows.shape[0]
    vmem = pl.BlockSpec(memory_space=pltpu.VMEM)
    hbm = pl.BlockSpec(memory_space=pl.ANY)
    wide = (rows, MODEL_WIDTH)
    return pl.pallas_call(
        functools.partial(forward_kernel, n),
        in_specs=[vmem] * 9 + [hbm] * 4,
        out_specs=(vmem,) * 8 + (hbm,) * 2,
        out_shape=(
            jax.ShapeDtypeStruct(wide, bf16),
            jax.ShapeDtypeStruct(wide, bf16),
            jax.ShapeDtypeStruct((n, rows, 2 * KV_WIDTH), bf16),
            jax.ShapeDtypeStruct(wide, f32),
            jax.ShapeDtypeStruct(wide, bf16),
            jax.ShapeDtypeStruct((HEAD_ROWS, rows), f32),
            jax.ShapeDtypeStruct(wide, f32),
            jax.ShapeDtypeStruct(wide, bf16),
            jax.ShapeDtypeStruct((exp_size, *g.shape), bf16),
            jax.ShapeDtypeStruct((exp_size, *routing.shape), f32),
        ),
        scratch_shapes=[
            pltpu.VMEM((MODEL_WIDTH, MODEL_WIDTH), bf16),
            pltpu.VMEM((MODEL_WIDTH, MODEL_WIDTH), bf16),
            pltpu.VMEM((KEY_VALUE_HEADS, rows, HEAD_SIZE), f32),
            pltpu.VMEM((KEY_VALUE_HEADS, rows, HEAD_SIZE), f32),
            pltpu.SemaphoreType.DMA((2,)),
            pltpu.SemaphoreType.DMA((n - 1,)),
            pltpu.SemaphoreType.DMA((n - 1,)),
        ]
        + [pltpu.SemaphoreType.DMA((exp_size,))] * 4,
        compiler_params=params(collective_id=3, has_side_effects=True),
        cost_estimate=cost(
            4 * n * rows * rows * MODEL_WIDTH + 5 * rows * MODEL_WIDTH * MODEL_WIDTH, 4e7,
            n * rows * rows * QUERY_HEADS,
        ),
        name="forward_to_experts",
    )(x, gain, wk, wv, cosine, sine, qpos_col, kpos_rows, ffn_gain, wq, wo, g, routing)


FF_TILE = 256
WIDTH_TILE = 512


def expert_kernel(first, count, pos_row_ref, pos_col_ref, gate_row_ref, *refs):
    x_refs = refs[:count]
    g_own_ref, g_ref, wgu_ref, wd_ref = refs[count : count + 4]
    rows_ref, hidden_ref, slot_grad_ref, pg_ref, place, result, rows_grad = refs[-7:]
    y_refs, dx_refs = refs[-7 - 2 * count : -7 - count], refs[-7 - count : -7]
    block, expert = pl.program_id(0), pl.program_id(1)
    capacity = rows_ref.shape[-2]
    tokens = x_refs[0].shape[0]
    slot_r = lax.broadcasted_iota(jnp.int32, (capacity, tokens), 0)
    slot_c = lax.broadcasted_iota(jnp.int32, (tokens, capacity), 1)
    match = slot_r == pos_row_ref[0, 0]
    pick = match.astype(bf16)
    place[expert] = (slot_c == pos_col_ref[0, 0]).astype(bf16)
    gates = jnp.sum(jnp.where(match, gate_row_ref[0, 0], 0.0), axis=1, keepdims=True)
    for one in range(count):

        @pl.when(block == one)
        def _():
            for start in range(0, MODEL_WIDTH, WIDTH_TILE):
                span = slice(start, start + WIDTH_TILE)
                rows_ref[0, 0, :, span] = dot(pick, x_refs[one][:, span]).astype(bf16)
                g_here = g_own_ref[:, span] if first + one == 0 else g_ref[0, :, span]
                slot_grad_ref[0, 0, :, span] = (dot(pick, g_here) * gates).astype(bf16)

    rows = rows_ref[0, 0]
    slot_grad = slot_grad_ref[0, 0]
    for start in range(0, FF, FF_TILE):
        span = slice(start, start + FF_TILE)
        up_span = slice(FF + start, FF + start + FF_TILE)
        gate = dot(rows, wgu_ref[0, :, span])
        up = dot(rows, wgu_ref[0, :, up_span])
        hidden_grad = dot_nt(slot_grad, wd_ref[0, span, :])
        square = gate * gate
        tangent = jnp.tanh(gate * (gelu_c + (gelu_c * 0.044715) * square))
        half_plus = 0.5 + 0.5 * tangent
        activated = gate * half_plus
        slope = half_plus + activated * (1.0 - tangent) * (
            gelu_c + (3.0 * 0.044715 * gelu_c) * square
        )
        hidden_ref[0, 0, :, span] = (activated * up).astype(bf16)
        pg_ref[0, 0, :, span] = (hidden_grad * up * slope).astype(bf16)
        pg_ref[0, 0, :, up_span] = (hidden_grad * activated).astype(bf16)
    hidden = hidden_ref[0, 0]
    projected_grad = pg_ref[0, 0]
    for start in range(0, MODEL_WIDTH, WIDTH_TILE):
        span = slice(start, start + WIDTH_TILE)
        result[expert, :, span] = (dot(hidden, wd_ref[0, :, span]) * gates).astype(bf16)
        rows_grad[expert, :, span] = dot_nt(projected_grad, wgu_ref[0, span, :]).astype(bf16)

    for one in range(count):

        @pl.when((expert == EXP_DEV - 1) & (block == one))
        def _():
            both = jnp.concatenate([place[e] for e in range(EXP_DEV)], axis=1)
            for start in range(0, MODEL_WIDTH, WIDTH_TILE):
                span = slice(start, start + WIDTH_TILE)
                for out_ref, terms in ((y_refs[one], result), (dx_refs[one], rows_grad)):
                    stacked = terms[:, :, span].reshape(EXP_DEV * capacity, WIDTH_TILE)
                    out_ref[:, span] = dot(both, stacked).astype(bf16)


def expert_blocks(first, blocks, capacity, pos, gates, xs, g, g_all, wgu, wd, kept):
    count, tokens = len(xs), xs[0].shape[0]
    kept_shapes = tuple(
        jax.ShapeDtypeStruct((EXP_DEV, blocks, capacity, width), bf16)
        for width in (MODEL_WIDTH, FF, MODEL_WIDTH, 2 * FF)
    )
    kept_specs = tuple(
        pl.BlockSpec((1, 1, capacity, s.shape[-1]), lambda b, e: (e, first + b, 0, 0))
        for s in kept_shapes
    )
    args = [pos[:, :, None, :], pos[:, :, :, None], gates[:, :, None, :], *xs, g, g_all, wgu, wd]
    aliases = {} if kept is None else {len(args) + i: 2 * count + i for i in range(4)}
    flops = count * EXP_DEV * 2 * capacity * (4 * tokens * MODEL_WIDTH + 9 * MODEL_WIDTH * FF)
    result = jax.ShapeDtypeStruct((tokens, MODEL_WIDTH), bf16)
    once = pl.BlockSpec((tokens, MODEL_WIDTH), lambda b, e: (0, 0), pipeline_mode=pl.Buffered(1))
    out = pl.pallas_call(
        functools.partial(expert_kernel, first, count),
        grid=(count, EXP_DEV),
        in_specs=[
            pl.BlockSpec((1, 1, 1, tokens), lambda b, e: (b, e, 0, 0)),
            pl.BlockSpec((1, 1, tokens, 1), lambda b, e: (b, e, 0, 0)),
            pl.BlockSpec((1, 1, 1, tokens), lambda b, e: (b, e, 0, 0)),
        ]
        + [once] * (count + 1)
        + [
            pl.BlockSpec((1, tokens, MODEL_WIDTH), lambda b, e: (jnp.maximum(first + b, 1), 0, 0)),
            pl.BlockSpec((1, MODEL_WIDTH, 2 * FF), lambda b, e: (e, 0, 0)),
            pl.BlockSpec((1, FF, MODEL_WIDTH), lambda b, e: (e, 0, 0)),
        ]
        + [pl.BlockSpec(memory_space=pl.ANY) for _ in aliases],
        out_specs=(once,) * (2 * count) + kept_specs,
        out_shape=(result,) * (2 * count) + kept_shapes,
        scratch_shapes=[
            pltpu.VMEM((EXP_DEV, tokens, capacity), bf16),
            pltpu.VMEM((EXP_DEV, capacity, MODEL_WIDTH), bf16),
            pltpu.VMEM((EXP_DEV, capacity, MODEL_WIDTH), bf16),
        ],
        input_output_aliases=aliases,
        compiler_params=params(),
        cost_estimate=cost(flops, 6e7),
        name="expert_blocks",
    )(*args, *(kept or ()))
    return out[:count], out[count : 2 * count], out[2 * count :]


GRAD_TILE = 384


def weight_grad_kernel(chunk_ref, a_ref, b_ref, out_ref):
    out_ref[0] = dot_tn(a_ref[0], b_ref[0]).astype(bf16)


def weight_grad(first, experts, chunk, size, a, b):
    slots, width = a.shape[1], b.shape[-1]
    tiles = size // GRAD_TILE
    return pl.pallas_call(
        weight_grad_kernel,
        grid_spec=pltpu.PrefetchScalarGridSpec(
            num_scalar_prefetch=1,
            grid=(experts, tiles),
            in_specs=[
                pl.BlockSpec((1, slots, GRAD_TILE), lambda e, t, c: (first + e, 0, c[0] * tiles + t)),
                pl.BlockSpec((1, slots, width), lambda e, t, c: (first + e, 0, 0)),
            ],
            out_specs=pl.BlockSpec((1, GRAD_TILE, width), lambda e, t, c: (e, t, 0)),
        ),
        out_shape=jax.ShapeDtypeStruct((experts, size, width), bf16),
        compiler_params=params(),
        cost_estimate=cost(2 * experts * slots * size * width, 2e7),
        name="weight_grad",
    )(chunk.reshape(1).astype(jnp.int32), a, b)


def middle_kernel(*refs):
    count = len(refs) - 11
    parts = refs[:count]
    mid_ref, g_ref, gain_ref, wo_ref, att_ref = refs[count : count + 5]
    mg_ref, mgl_ref, ag_ref, delta_ref, dgain_ref, delta_cols = refs[count + 5 :]
    rows = mid_ref.shape[0]
    half = rows // 2
    lane = lax.broadcasted_iota(jnp.int32, (half, HEAD_SIZE), 1)
    dgain = jnp.zeros((1, MODEL_WIDTH), f32)
    for part in range(2):
        band = slice(part * half, (part + 1) * half)
        nf_grad = parts[0][band, :].astype(f32)
        for other in parts[1:]:
            nf_grad += other[band, :].astype(f32)
        mid = mid_ref[band, :]
        r = lax.rsqrt(jnp.mean(mid * mid, axis=-1, keepdims=True) + epsilon)
        u = nf_grad * gain_ref[...]
        inner = jnp.mean(u * mid, axis=-1, keepdims=True)
        grad = g_ref[band, :].astype(f32) + r * u - mid * (r * r * r * inner)
        dgain += jnp.sum(nf_grad * mid * r, axis=0, keepdims=True)
        mg_ref[band, :] = grad
        low = grad.astype(bf16)
        mgl_ref[band, :] = low
        att_grad = dot_nt(low, wo_ref[...]).astype(bf16)
        ag_ref[band, :] = att_grad
        delta = jnp.zeros((half, HEAD_SIZE), f32)
        for head in range(QUERY_HEADS):
            span = slice(head * HEAD_SIZE, (head + 1) * HEAD_SIZE)
            one = jnp.sum(att_grad[:, span].astype(f32) * att_ref[band, span], axis=-1, keepdims=True)
            delta = jnp.where(lane == head, one, delta)
        delta_cols[band, :] = delta
    dgain_ref[...] = dgain
    delta_ref[...] = delta_cols[...].T[: delta_ref.shape[0], :]


def middle_backward(parts, mid, g, gain, wo, att):
    rows = mid.shape[0]
    return pl.pallas_call(
        middle_kernel,
        out_shape=(
            jax.ShapeDtypeStruct((rows, MODEL_WIDTH), f32),
            jax.ShapeDtypeStruct((rows, MODEL_WIDTH), bf16),
            jax.ShapeDtypeStruct((rows, MODEL_WIDTH), bf16),
            jax.ShapeDtypeStruct((HEAD_ROWS, rows), f32),
            jax.ShapeDtypeStruct((1, MODEL_WIDTH), f32),
        ),
        scratch_shapes=[pltpu.VMEM((rows, HEAD_SIZE), f32)],
        compiler_params=params(),
        cost_estimate=cost(2 * rows * MODEL_WIDTH * MODEL_WIDTH, 2e7),
        name="middle_backward",
    )(*parts, mid, g, gain, wo, att)


def signal_and_wait(neighbours):
    barrier = pltpu.get_barrier_semaphore()
    for neighbour in neighbours:
        pl.semaphore_signal(barrier, inc=1, device_id=neighbour, device_id_type=MESH)
    pl.semaphore_wait(barrier, len(neighbours))


def remote(source, target, send_sem, recv_sem, device):
    return pltpu.make_async_remote_copy(
        src_ref=source, dst_ref=target, send_sem=send_sem, recv_sem=recv_sem,
        device_id=device, device_id_type=MESH,
    )


class Axis:
    def __init__(self, name):
        if name in ("dp", "ctx"):
            self.count, self.me = lax.axis_size(name), lax.axis_index(name)
            place = lambda i: {name: i}
        else:
            exp = lax.axis_index("exp")
            core, chip = lax.rem(exp, 2), exp // 2
            if name == "core":
                self.count, self.me = 2, core
                place = lambda i: {"exp": chip * 2 + i}
            else:
                self.count, self.me = lax.axis_size("exp") // 2, chip
                place = lambda i: {"exp": i * 2 + core}
        self.next = place(lax.rem(self.me + 1, self.count))
        self.last = place(lax.rem(self.me + self.count - 1, self.count))

    def neighbours(self):
        return [self.next] if self.count == 2 else [self.next, self.last]


class Ring:
    def __init__(self, axis, terms, rows, send, recv, send_sem, recv_sem):
        self.axis, self.count, self.terms, self.rows = axis, axis.count, terms, rows
        self.send, self.recv, self.send_sem, self.recv_sem = send, recv, send_sem, recv_sem

    def here(self, hop):
        part = lax.rem(self.axis.me + self.count - 1 - hop, self.count)
        return pl.ds(pl.multiple_of(part * self.rows, self.rows), self.rows)

    def copy(self, hop):
        if len(self.terms) > 1:
            source = self.send.at[hop]
        elif hop == 0:
            source = self.terms[0].at[self.here(0), :]
        else:
            source = self.send.at[hop - 1]
        return remote(
            source, self.recv.at[hop], self.send_sem.at[hop], self.recv_sem.at[hop], self.axis.next
        )

    def hop(self, hop):
        if hop == 0 and len(self.terms) == 1:
            self.copy(0).start()
            return None
        here = self.here(hop)
        total = self.terms[0][here, :].astype(f32)
        for term in self.terms[1:]:
            total += term[here, :].astype(f32)
        if hop:
            self.copy(hop - 1).wait_recv()
            total += self.recv[hop - 1].astype(f32)
        if hop < self.count - 1:
            self.send[hop - (len(self.terms) == 1)] = total.astype(bf16)
            self.copy(hop).start()
        return total

    def finish(self):
        for hop in range(self.count - 1):
            self.copy(hop).wait_send()


def attention_back_kernel(
    n, q_ref, ag_ref, kv_ref, lse_ref, delta_ref, kpos_ref, qpos_ref, cos_ref, sin_ref, mine_ref,
    came_ref, wo_grad_ref, next_ref, next_mine_ref, down_ref, down_mine_ref, dql_ref, dkv_ref,
    share_ref, next_sum_ref, down_sum_ref, wo_sum_ref, next_came, down_came, next_mine, down_mine,
    dq_acc, held, send, recv, send_sem, recv_sem, next_sem, *scratch,
):
    ctx, core, chip = Axis("ctx"), Axis("core"), Axis("chip")
    right, across = ctx.next, Axis("dp").next
    signal_and_wait(ctx.neighbours() + core.neighbours() + chip.neighbours() + [across])
    core_rows = wo_grad_ref.shape[0] // 2
    wo_chain = Chain(
        [
            Ring(core, [wo_grad_ref], core_rows, *scratch[:4]),
            Ring(chip, [scratch[4]], core_rows // chip.count, *scratch[5:9]),
        ],
        [scratch[4], wo_sum_ref],
    )
    ring = Ring(ctx, [mine_ref, came_ref], share_ref.shape[0], *scratch[9:])
    ring.hop(0)
    wo_chain.step()
    exchanges, loads = [], []
    for i, (source, target, mine_hbm, mine) in enumerate(
        (
            (next_ref, next_came, next_mine_ref, next_mine),
            (down_ref.at[0], down_came, down_mine_ref.at[0], down_mine),
        )
    ):
        exchanges.append(remote(source, target, next_sem.at[i, 0], next_sem.at[i, 1], across))
        loads.append(pltpu.make_async_copy(mine_hbm, mine, next_sem.at[i, 2]))
        exchanges[i].start()
        loads[i].start()
    def dkv_copy(step, group):
        return remote(
            send.at[group, step], recv.at[group, step], send_sem.at[group, step],
            recv_sem.at[group, step], right,
        )

    for step in range(n):
        back = (step + 1) % n
        kpos = kpos_ref[back]

        def one_group(group, carry):
            keys = kv_ref[back, :, pl.ds(pl.multiple_of(group * HEAD_SIZE, HEAD_SIZE), HEAD_SIZE)]
            start = pl.multiple_of(KV_WIDTH + group * HEAD_SIZE, HEAD_SIZE)
            values = kv_ref[back, :, pl.ds(start, HEAD_SIZE)]
            dk = dv = None
            for member in range(GROUP):
                head = group * GROUP + member
                columns = pl.ds(pl.multiple_of(head * HEAD_SIZE, HEAD_SIZE), HEAD_SIZE)
                q, ag = q_ref[:, columns], ag_ref[:, columns]
                scores = dot_nt(keys, q)
                weights = jnp.exp2(scores * score_to_log2 - lse_ref[pl.ds(head, 1), :])
                weights = jnp.where(kpos <= qpos_ref[...], weights, 0.0)
                weights_grad = dot_nt(values, ag)
                score_grad = weights * (weights_grad - delta_ref[pl.ds(head, 1), :]) * score_scale
                score_grad = score_grad.astype(bf16)
                dv_part = dot(weights.astype(bf16), ag)
                dk_part = dot(score_grad, q)
                dv = dv_part if dv is None else dv + dv_part
                dk = dk_part if dk is None else dk + dk_part
                dq = dot_tn(score_grad, keys)
                if step:
                    dq += dq_acc[:, columns]
                dq_acc[:, columns] = dq
            held[group] = jnp.concatenate([dk, dv], axis=1)
            return carry

        lax.fori_loop(0, KEY_VALUE_HEADS, one_group, 0)
        for group in range(KEY_VALUE_HEADS):
            dkv = held[group]
            if step:
                dkv_copy(step - 1, group).wait_recv()
                dkv += recv[group, step - 1].astype(f32)
            if step < n - 1:
                send[group, step] = dkv.astype(bf16)
                dkv_copy(step, group).start()
            else:
                for place in range(2):
                    start = place * KV_WIDTH + group * HEAD_SIZE
                    part = dkv[:, place * HEAD_SIZE : (place + 1) * HEAD_SIZE]
                    dkv_ref[:, start : start + HEAD_SIZE] = part.astype(bf16)
        if step < n - 2:
            ring.hop(step + 1)
        wo_chain.step(2 if step == 0 else 1)
    cosine, sine = cos_ref[...], sin_ref[...]
    for head in range(QUERY_HEADS):
        span = slice(head * HEAD_SIZE, (head + 1) * HEAD_SIZE)
        dql_ref[:, span] = rotate_back(dq_acc[:, span], cosine, sine).astype(bf16)
    share_ref[...] = ring.hop(n - 1)
    ring.finish()
    for step in range(n - 1):
        for group in range(KEY_VALUE_HEADS):
            dkv_copy(step, group).wait_send()
    wo_chain.step(len(wo_chain.hops))
    wo_chain.finish()
    for i, (sum_ref, mine, came) in enumerate(
        ((next_sum_ref, next_mine, next_came), (down_sum_ref, down_mine, down_came))
    ):
        loads[i].wait()
        exchanges[i].wait()
        for start in range(0, sum_ref.shape[0], HEAD_SIZE):
            band = slice(start, start + HEAD_SIZE)
            total = mine[band, :].astype(f32) + came[band, :].astype(f32)
            sum_ref[band, :] = total.astype(bf16)


def attention_backward(
    q, ag, kv, lse, delta, kpos, qpos_row, cosine, sine, mine, came, w_out_grad, following,
    following_mine, other_down, mine_down,
):
    n, keys, _ = kv.shape
    rows = q.shape[0]
    chips = sizes()["chip"]
    wo_rows = w_out_grad.shape[0] // 2
    vmem = pl.BlockSpec(memory_space=pltpu.VMEM)
    hbm = pl.BlockSpec(memory_space=pl.ANY)
    return pl.pallas_call(
        functools.partial(attention_back_kernel, n),
        in_specs=[vmem] * 12 + [hbm] * 4,
        out_specs=(vmem,) * 6,
        out_shape=(
            jax.ShapeDtypeStruct((rows, MODEL_WIDTH), bf16),
            jax.ShapeDtypeStruct((keys, 2 * KV_WIDTH), bf16),
            jax.ShapeDtypeStruct((mine.shape[0] // n, mine.shape[1]), f32),
            jax.ShapeDtypeStruct(following.shape, bf16),
            jax.ShapeDtypeStruct(other_down.shape[1:], bf16),
            jax.ShapeDtypeStruct((wo_rows // chips, MODEL_WIDTH), bf16),
        ),
        scratch_shapes=[
            pltpu.VMEM(following.shape, bf16),
            pltpu.VMEM(other_down.shape[1:], bf16),
            pltpu.VMEM(following.shape, bf16),
            pltpu.VMEM(other_down.shape[1:], bf16),
            pltpu.VMEM((rows, MODEL_WIDTH), f32),
            pltpu.VMEM((KEY_VALUE_HEADS, keys, 2 * HEAD_SIZE), f32),
            pltpu.VMEM((KEY_VALUE_HEADS, n - 1, keys, 2 * HEAD_SIZE), bf16),
            pltpu.VMEM((KEY_VALUE_HEADS, n - 1, keys, 2 * HEAD_SIZE), bf16),
            pltpu.SemaphoreType.DMA((KEY_VALUE_HEADS, n - 1)),
            pltpu.SemaphoreType.DMA((KEY_VALUE_HEADS, n - 1)),
            pltpu.SemaphoreType.DMA((2, 3)),
        ]
        + ring_buffers(2, 1, wo_rows, MODEL_WIDTH)
        + [pltpu.VMEM((wo_rows, MODEL_WIDTH), bf16)]
        + ring_buffers(chips, 1, wo_rows // chips, MODEL_WIDTH)
        + ring_buffers(n, 2, mine.shape[0] // n, mine.shape[1]),
        compiler_params=params(collective_id=1, has_side_effects=True),
        cost_estimate=cost(10 * n * rows * keys * MODEL_WIDTH, 4e7, n * rows * keys * QUERY_HEADS),
        name="attention_backward",
    )(
        q, ag, kv, lse, delta, kpos, qpos_row, cosine, sine, mine, came, w_out_grad, following,
        following_mine, other_down, mine_down,
    )


def ring_buffers(count, terms, rows, width):
    sends = count - 1 if terms > 1 else count - 2
    return [
        pltpu.VMEM((sends, rows, width) if sends else (16, HEAD_SIZE), bf16),
        pltpu.VMEM((count - 1, rows, width), bf16),
        pltpu.SemaphoreType.DMA((count - 1,)),
        pltpu.SemaphoreType.DMA((count - 1,)),
    ]


class Chain:
    def __init__(self, rings, stores):
        self.hops = [(r, h) for r in range(len(rings)) for h in range(rings[r].count)]
        self.rings, self.stores, self.done = rings, stores, 0

    def step(self, times=1):
        for _ in range(times):
            if self.done == len(self.hops):
                return
            index, hop = self.hops[self.done]
            self.done += 1
            ring = self.rings[index]
            total = ring.hop(hop)
            if hop == ring.count - 1:
                store = self.stores[index]
                store[...] = total.astype(store.dtype)

    def finish(self):
        assert self.done == len(self.hops)
        for ring in self.rings:
            ring.finish()


FULL_AXES = ("core", "chip", "dp", "ctx")


def sizes():
    exp = lax.axis_size("exp")
    return {"core": 2, "chip": exp // 2, "dp": lax.axis_size("dp"), "ctx": lax.axis_size("ctx")}


class Total:
    def __init__(self, axis, value, recv, send_sem, recv_sem):
        self.axis, self.value, self.recv = axis, value, recv
        self.send_sem, self.recv_sem = send_sem, recv_sem

    def copy(self, hop):
        source = self.recv.at[hop - 1] if hop else self.value
        return remote(
            source, self.recv.at[hop], self.send_sem.at[hop], self.recv_sem.at[hop], self.axis.next
        )

    def run(self):
        count = self.axis.count
        self.copy(0).start()
        total = self.value[...]
        for hop in range(1, count):
            self.copy(hop - 1).wait_recv()
            total += self.recv[hop - 1]
            if hop < count - 1:
                self.copy(hop).start()
        for hop in range(count - 1):
            self.copy(hop).wait_send()
        self.value[...] = total


GAIN_ROWS = 8


def last_kernel(
    plan, piece_ref, down_sum_ref, mine_down_ref, other_down_ref, dql_ref, dkv_ref, normed_ref, wq_ref,
    wk_ref, wv_ref, cos_ref, sin_ref, x_ref, gain_ref, mg_hbm, ffn_gain_ref, wo_sum_ref,
    gate_up_ref, down_ref, dx_ref, gains_ref, wq_out, wkv_out, wo_out, wq_grad, wkv_grad, dkvl,
    mg_band, mg_sem, *scratch,
):
    scratch = list(scratch)

    def take(number):
        taken = scratch[:number]
        del scratch[:number]
        return taken

    axes = {name: Axis(name) for name in FULL_AXES}
    across = axes["dp"].next
    piece = Chain(
        [Ring(axes["ctx"], [piece_ref], gate_up_ref.shape[0], *take(4))], [gate_up_ref]
    )
    came_down, mine_down, down_sem = take(3)
    exchange = remote(
        other_down_ref.at[1], came_down, down_sem.at[0], down_sem.at[1], across
    )
    load_down = pltpu.make_async_copy(mine_down_ref.at[1], mine_down, down_sem.at[2])
    downs = [
        Chain([Ring(axes["ctx"], terms, down_ref.shape[1], *take(4))], [down_ref.at[expert]])
        for expert, terms in enumerate(([down_sum_ref], [mine_down, came_down]))
    ]
    chains = []
    for (names, rows), array, out in zip(
        plan, (wq_grad, wkv_grad, wo_sum_ref), (wq_out, wkv_out, wo_out)
    ):
        rings, stores, source = [], [], array
        for name in names:
            rows //= axes[name].count
            rings.append(Ring(axes[name], [source], rows, *take(4)))
            source = out if name == names[-1] else take(1)[0]
            stores.append(source)
        chains.append(Chain(rings, stores))
    query, kv, out_chain = chains
    totals = [Total(axes[name], gains_ref, *take(3)) for name in FULL_AXES]
    signal_and_wait([device for axis in axes.values() for device in axis.neighbours()])

    quarter = x_ref.shape[0] // 4

    def load_mid_grad(part):
        band = slice(part * quarter, (part + 1) * quarter)
        return pltpu.make_async_copy(mg_hbm.at[band, :], mg_band.at[part % 2], mg_sem.at[part])

    load_mid_grad(0).start()
    load_mid_grad(1).start()
    load_down.start()
    piece.step()
    exchange.start()
    out_chain.step()
    downs[0].step()
    for start in range(0, MODEL_WIDTH, HALF):
        span = slice(start, start + HALF)
        wq_grad[span, :] = dot_tn(normed_ref[:, span], dql_ref[...]).astype(bf16)
    query.step()
    cosine, sine = cos_ref[...], sin_ref[...]
    for head in range(KEY_VALUE_HEADS):
        span = slice(head * HEAD_SIZE, (head + 1) * HEAD_SIZE)
        dkvl[:, span] = rotate_back(dkv_ref[:, span].astype(f32), cosine, sine).astype(bf16)
    dkvl[:, KV_WIDTH:] = dkv_ref[:, KV_WIDTH:]
    for start in range(0, MODEL_WIDTH, WIDTH_TILE):
        span = slice(start, start + WIDTH_TILE)
        wkv_grad[span, :] = dot_tn(normed_ref[:, span], dkvl[...]).astype(bf16)
    query.step(2)
    kv.step()
    piece.step()
    downs[0].step()
    dgain = jnp.zeros((1, MODEL_WIDTH), f32)
    for part in range(4):
        band = slice(part * quarter, (part + 1) * quarter)
        grad = dot_nt(dql_ref[band, :], wq_ref[...])
        grad += dot_nt(dkvl[band, :KV_WIDTH], wk_ref[...])
        grad += dot_nt(dkvl[band, KV_WIDTH:], wv_ref[...])
        x = x_ref[band, :].astype(f32)
        r = lax.rsqrt(jnp.mean(x * x, axis=-1, keepdims=True) + epsilon)
        v = grad * gain_ref[...]
        inner = jnp.mean(v * x, axis=-1, keepdims=True)
        dgain += jnp.sum(grad * x * r, axis=0, keepdims=True)
        load_mid_grad(part).wait()
        mid_grad = mg_band[part % 2]
        dx_ref[band, :] = (mid_grad + r * v - x * (r * r * r * inner)).astype(bf16)
        if part < 2:
            load_mid_grad(part + 2).start()
        if part == 1:
            kv.step()
    gains_ref[0:1, :] = dgain
    gains_ref[1:2, :] = ffn_gain_ref[...]
    gains_ref[2:, :] = jnp.zeros((GAIN_ROWS - 2, MODEL_WIDTH), f32)
    out_chain.step(2)
    piece.step()
    downs[0].step()
    totals[0].run()
    totals[1].run()
    query.step(2)
    kv.step()
    load_down.wait()
    exchange.wait_recv()
    downs[1].step()
    out_chain.step()
    piece.step()
    downs[0].step()
    totals[2].run()
    downs[1].step()
    out_chain.step()
    kv.step(2)
    query.step(2)
    downs[1].step()
    kv.step(2)
    totals[3].run()
    everything = [query, kv, downs[1], downs[0], out_chain, piece]
    while any(chain.done < len(chain.hops) for chain in everything):
        for chain in everything:
            chain.step()
    for chain in everything:
        chain.finish()
    exchange.wait_send()


def last_part(
    piece, down_sum, mine_down, other_down, dql, dkv, normed, wq, wk, wv, cosine, sine, x, gain,
    mg, ffn_gain_part, wo_sum,
):
    counts = sizes()
    n = counts["ctx"]
    share = MODEL_WIDTH // (2 * counts["chip"] * counts["dp"] * n)
    full = FULL_AXES if share % 16 == 0 else FULL_AXES[:3]
    widths = (MODEL_WIDTH, 2 * KV_WIDTH, MODEL_WIDTH)
    plan = [(full, MODEL_WIDTH), (full, MODEL_WIDTH), (full[2:], wo_sum.shape[0])]
    share, down_share = piece.shape[0] // n, mine_down.shape[1] // n
    shapes = [
        jax.ShapeDtypeStruct((share, 2 * FF), f32),
        jax.ShapeDtypeStruct((EXP_DEV, down_share, mine_down.shape[2]), f32),
        jax.ShapeDtypeStruct(x.shape, bf16),
        jax.ShapeDtypeStruct((GAIN_ROWS, MODEL_WIDTH), f32),
    ]
    scratch = [
        pltpu.VMEM((MODEL_WIDTH, MODEL_WIDTH), bf16),
        pltpu.VMEM((MODEL_WIDTH, 2 * KV_WIDTH), bf16),
        pltpu.VMEM((x.shape[0], 2 * KV_WIDTH), bf16),
        pltpu.VMEM((2, x.shape[0] // 4, MODEL_WIDTH), f32),
        pltpu.SemaphoreType.DMA((4,)),
    ]
    scratch += ring_buffers(n, 1, share, 2 * FF)
    scratch += [pltpu.VMEM(mine_down.shape[1:], bf16)] * 2 + [pltpu.SemaphoreType.DMA((3,))]
    for terms in (1, 2):
        scratch += ring_buffers(n, terms, down_share, mine_down.shape[2])
    for (names, rows), width in zip(plan, widths):
        for name in names:
            rows //= counts[name]
            scratch += ring_buffers(counts[name], 1, rows, width)
            if name != names[-1]:
                scratch.append(pltpu.VMEM((rows, width), bf16))
        shapes.append(jax.ShapeDtypeStruct((rows, width), f32 if "ctx" in names else bf16))
    for name in FULL_AXES:
        hops = counts[name] - 1
        scratch += [
            pltpu.VMEM((hops, GAIN_ROWS, MODEL_WIDTH), f32),
            pltpu.SemaphoreType.DMA((hops,)),
            pltpu.SemaphoreType.DMA((hops,)),
        ]
    vmem, hbm = pl.BlockSpec(memory_space=pltpu.VMEM), pl.BlockSpec(memory_space=pl.ANY)
    gate_up, down, dx, gains, *attention = pl.pallas_call(
        functools.partial(last_kernel, plan),
        in_specs=[vmem] * 2 + [hbm] * 2 + [vmem] * 10 + [hbm] + [vmem] * 2,
        out_specs=(vmem,) * 7,
        out_shape=tuple(shapes),
        scratch_shapes=scratch,
        compiler_params=params(collective_id=2, has_side_effects=True),
        cost_estimate=cost(1e10, 4e7),
        name="last_part",
    )(
        piece, down_sum, mine_down, other_down, dql, dkv, normed, wq, wk, wv, cosine, sine, x, gain,
        mg, ffn_gain_part, wo_sum,
    )
    if "ctx" not in full:
        attention = [
            scatter_axis(a.reshape(n, a.shape[0] // n, a.shape[1]), "ctx").astype(f32)
            for a in attention
        ]
    return gate_up, down, dx, gains, attention


def shifted(value, axis, steps):
    count = lax.axis_size(axis)
    return lax.ppermute(value, axis, [(i, (i + steps) % count) for i in range(count)])


def core_swap(value):
    return lax.ppermute(value, "exp", [(i, i ^ 1) for i in range(lax.axis_size("exp"))])


def chip_shift(value, steps):
    count = lax.axis_size("exp")
    return lax.ppermute(value, "exp", [(i, (i + 2 * steps) % count) for i in range(count)])


def return_blocks(parts):
    terms = [parts[0], core_swap(parts[1])]
    for steps in range(1, lax.axis_size("exp") // 2):
        crossed = core_swap(parts[2 * steps])
        both = (crossed.astype(f32) + parts[2 * steps + 1].astype(f32)).astype(bf16)
        terms.append(chip_shift(both, -steps))
    return terms


def ring_part(parts, index, count, step, axis=0):
    return lax.dynamic_index_in_dim(parts, (index - 1 - step) % count, axis, keepdims=False)


def add_low(a, b):
    return (a.astype(f32) + b.astype(f32)).astype(bf16)


def ring_scatter(parts, shift, index, count, axis=0):
    total = ring_part(parts, index, count, 0, axis)
    for step in range(1, count):
        total = add_low(shift(total), ring_part(parts, index, count, step, axis))
    return total


def by_owner(array, axis):
    dp, ctx, exp = (lax.axis_size(a) for a in ("dp", "ctx", "exp"))
    size = array.shape[axis]
    before, after = array.shape[:axis], array.shape[axis + 1 :]
    parts = array.reshape(*before, dp, ctx, exp // 2, 2, size // (dp * ctx * exp), *after)
    order = list(range(axis)) + [axis + i for i in (3, 2, 0, 1, 4)]
    order += list(range(axis + 5, parts.ndim))
    return jnp.transpose(parts, order).reshape(array.shape)


def scatter_axis(parts, axis):
    return ring_scatter(
        parts, lambda v: shifted(v, axis, 1), lax.axis_index(axis), lax.axis_size(axis)
    )


def tie(*values):
    return lax.optimization_barrier(values)


def per_device(
    tokens, attn_gain, w_query, key_matrix, value_matrix, w_out, ffn_gain, expert_gate_up,
    expert_down, expert_ids, gate_weights, span_order, out_grad,
):
    ctx_size, exp_size = lax.axis_size("ctx"), lax.axis_size("exp")
    ctx_here, exp_here = lax.axis_index("ctx"), lax.axis_index("exp")
    experts = EXP_DEV * exp_size
    x, g = tokens[0], out_grad[0]
    rows = x.shape[0]
    capacity = rows * TOPK * 5 // (4 * experts)
    gain_one, gain_two = attn_gain[None, :], ffn_gain[None, :]
    offsets = jnp.arange(HALF, dtype=jnp.int32)

    def device_positions(device):
        pair = lax.dynamic_slice_in_dim(span_order[0], 2 * device, 2, 0)
        return (pair[:, None] * HALF + offsets[None, :]).reshape(-1)

    sources = [(ctx_here - s) % ctx_size for s in range(ctx_size)]
    key_positions = [device_positions(s) for s in sources]
    positions = key_positions[0]
    exponent = jnp.arange(HEAD_SIZE // 2, dtype=f32) * (-2.0 / HEAD_SIZE)
    frequency = jnp.power(f32(rope_base), exponent)
    angles = positions.astype(f32)[:, None] * frequency[None, :]
    cosine, sine = jnp.cos(angles), jnp.sin(angles)
    cosine = jnp.concatenate([cosine, cosine], axis=1)
    sine = jnp.concatenate([-sine, sine], axis=1)

    named = expert_ids[0][:, :, None] == jnp.arange(experts, dtype=jnp.int32)
    member = jnp.any(named, axis=1)
    count = member.astype(jnp.int32)
    place = jnp.where(member, jnp.cumsum(count, axis=0) - count, -1)
    route_gate = jnp.sum(jnp.where(named, gate_weights[0][:, :, None], 0.0), axis=1)
    routing = jnp.stack([place.astype(f32), route_gate]).transpose(0, 2, 1)

    normed, q, kv, att, att_low, lse, mid, nf, g_all, routing_all = forward_to_experts(
        x, gain_one, key_matrix, value_matrix, cosine, sine, positions[:, None],
        jnp.stack(key_positions)[:, None, :], gain_two, w_query, w_out, g, routing,
    )
    routing = jnp.concatenate([routing[None], routing_all[1:]], axis=0)
    routing = lax.dynamic_slice_in_dim(routing, EXP_DEV * exp_here, EXP_DEV, 2)
    pos, gates = routing[:, 0].astype(jnp.int32), routing[:, 1]

    swapped = core_swap(nf)
    nf_blocks = [nf, swapped]
    nf, swapped = tie(nf, swapped)
    y_parts, dx_parts, kept = [], [], None
    for first in range(0, exp_size, 2):
        here = slice(first, first + 2)
        if first:
            same, dx_parts[-1] = tie(chip_shift(nf, first // 2), dx_parts[-1])
            nf_blocks += [core_swap(same), same]
        y_part, dx_part, kept = expert_blocks(
            first, exp_size, capacity, pos[here], gates[here], nf_blocks[here], g, g_all,
            expert_gate_up, expert_down, kept,
        )
        y_parts += y_part
        dx_parts += dx_part
    nf_grad_terms = return_blocks(dx_parts)
    slot_rows, hidden, slot_grad, projected_grad = (
        a.reshape(EXP_DEV, exp_size * capacity, a.shape[-1]) for a in kept
    )
    dp_size, dp_here = lax.axis_size("dp"), lax.axis_index("dp")
    half, down_half = MODEL_WIDTH // dp_size, FF // dp_size
    other = (dp_here - 1) % dp_size
    theirs = [weight_grad(0, 1, other, half, slot_rows, projected_grad)[0]]
    slot_rows, hidden, theirs = tie(slot_rows, hidden, theirs)
    came = shifted(theirs[0], "dp", 1)
    theirs.append(weight_grad(1, 1, other, half, slot_rows, projected_grad)[0])
    mine = [
        weight_grad(e, 1, dp_here, half, slot_rows, projected_grad)[0] for e in range(EXP_DEV)
    ]
    other_down = weight_grad(0, EXP_DEV, other, down_half, hidden, slot_grad)
    mine_down = weight_grad(0, EXP_DEV, dp_here, down_half, hidden, slot_grad)
    nf_grad_terms, mine, mine_down, other_down, y_parts, theirs = tie(
        nf_grad_terms, mine, mine_down, other_down, y_parts, theirs
    )

    mid_grad, mid_grad_low, att_grad, delta, ffn_gain_part = middle_backward(
        nf_grad_terms, mid, g, gain_two, w_out, att
    )
    mid_grad_low, came = tie(mid_grad_low, came)
    w_out_grad = by_owner(dot_tn(att_low, mid_grad_low).astype(bf16), 0)
    y_terms = return_blocks(y_parts)

    dql, dkv, gate_up_first, gate_up_next, down_sum, w_out_sum = attention_backward(
        q, att_grad, kv, lse, delta, jnp.stack(key_positions)[:, :, None], positions[None, :],
        cosine, sine, mine[0], came, w_out_grad, theirs[1], mine[1], other_down, mine_down,
    )
    gate_up_second, down_share, tokens_grad, gains, attention = last_part(
        gate_up_next, down_sum, mine_down, other_down, dql, dkv, by_owner(normed, 1), w_query, key_matrix,
        value_matrix, cosine, sine, x, gain_one, mid_grad, ffn_gain_part, w_out_sum,
    )
    w_query_share, w_kv_share, w_out_share = attention
    layer_output = mid
    for term in y_terms:
        layer_output = layer_output + term.astype(f32)
    layer_output = layer_output.astype(bf16)
    owner = (lax.axis_index("dp") * ctx_size + ctx_here) * exp_size + exp_here
    gain_share = MODEL_WIDTH // (dp_size * ctx_size * exp_size)
    gains = lax.dynamic_slice_in_dim(gains, owner * gain_share, gain_share, 1)
    return (
        layer_output[None],
        tokens_grad[None],
        gains[0],
        w_query_share,
        w_kv_share[:, :KV_WIDTH],
        w_kv_share[:, KV_WIDTH:],
        w_out_share,
        gains[1],
        jnp.stack([gate_up_first, gate_up_second]),
        down_share,
    )


def solution(mesh):
    by_row = P(("dp", "exp"), "ctx", None)
    share = P(("dp", "ctx", "exp"))
    share_rows = P(("dp", "ctx", "exp"), None)
    return jax.shard_map(
        per_device,
        mesh=mesh,
        in_specs=(
            by_row, P(), P(), P(), P(), P(), P(), P("exp", None, None), P("exp", None, None),
            by_row, by_row, P(("dp", "exp"), None), by_row,
        ),
        out_specs=(
            by_row, by_row, share, share_rows, share_rows, share_rows, share_rows, share,
            P("exp", ("dp", "ctx"), None), P("exp", ("dp", "ctx"), None),
        ),
        check_vma=False,
    )
```

time: 552 us -> 486 us (0.88)
  waiting for transfers between devices: 64.6 us -> 14.3 us
  Pallas kernels: 393 us -> 411 us
  starting transfers between devices: 18.3 us -> 6.25 us
  local copies, waits for them, and re-layouts: 30 us -> 21.9 us
  other arithmetic: 27.1 us -> 20 us
  matrix products: 10.5 us -> 4.53 us
    ppermute x6 -> x3, waiting for transfers between devices: 41.2 us -> 0.01 us  [chip_shift(): lax.ppermute(value, 'exp', [(i, (i + 2 * steps) % count) for i in range(c...]
    ppermute x5 -> x1, waiting for transfers between devices: 15.4 us -> 0.01 us  [shifted(): lax.ppermute(value, axis, [(i, (i + steps) % count) for i in range(count)])]
    pallas_call x7 -> x4, Pallas kernels: 254 us -> 270 us  [the longest x1 121 us: last_part(): pl.pallas_call(functools.partial(last_kernel, plan), in_specs=[vmem] * 2...]
    ppermute x11 -> x6, waiting for transfers between devices: 7.96 us -> 14.2 us  [core_swap(): lax.ppermute(value, 'exp', [(i, i ^ 1) for i in range(lax.axis_size('exp'...]
    ppermute x5 -> x1, starting transfers between devices: 7.64 us -> 1.49 us  [shifted(): lax.ppermute(value, axis, [(i, (i + steps) % count) for i in range(count)])]
    dot_general x3 -> x1, matrix products: 10.5 us -> 4.53 us  [dot_tn(): return lax.dot_general(a, b, TN, preferred_element_type=f32)]
    concatenate x4 -> x1, other arithmetic: 5.78 us -> 0.02 us  [per_device(): routing = jnp.concatenate([routing[None], routing_all[1:]], axis=0)]
    ppermute x6 -> x3, starting transfers between devices: 8.74 us -> 3.04 us  [chip_shift(): lax.ppermute(value, 'exp', [(i, (i + 2 * steps) % count) for i in range(c...]
  transfers between devices with their start and end apart: 22 -> 10, of which waited for: 10 -> 4; matrix products, arithmetic and copies ran while one was open for 8% -> 6% of each run, Pallas kernels for 37% -> 63%
where the time goes in v4:
time: 486 us; the launch traced here: 479 us
  Pallas kernels  411 us (85%)
  local copies, waits for them, and re-layouts  21.9 us (5%)
  other arithmetic  20 us (4%)
  waiting for transfers between devices  14.3 us (3%)
  starting transfers between devices  6.25 us (1%)
    pallas_call x1, Pallas kernels, last_part(): pl.pallas_call(functools.partial(last_kernel, plan), in_specs=[vmem] * 2...  121 us
    pallas_call x1, Pallas kernels, attention_backward(): pl.pallas_call(functools.partial(attention_back_kernel, n), in_specs=[vme...  87.8 us
    pallas_call x2, Pallas kernels, expert_blocks(): pl.pallas_call(functools.partial(expert_kernel, first, count), grid=(coun...  79.4 us
    pallas_call x1, Pallas kernels, forward_to_experts(): pl.pallas_call(functools.partial(forward_kernel, n), in_specs=[vmem] * 9...  69.2 us
    pallas_call x6, Pallas kernels, weight_grad(): pl.pallas_call(weight_grad_kernel, grid_spec=pltpu.PrefetchScalarGridSpec...  41.9 us
    ppermute x6, waiting for transfers between devices, core_swap(): lax.ppermute(value, 'exp', [(i, i ^ 1) for i in range(lax.axis_size('exp'...  14.2 us
    pallas_call x1, Pallas kernels, middle_backward(): pl.pallas_call(middle_kernel, out_shape=(jax.ShapeDtypeStruct((rows, MODE...  11.7 us
  transfers between devices with their start and end apart: 10, of which 4 were waited for; matrix products, arithmetic and copies ran while one was open for 6% of the time, Pallas kernels for 63%

profile of v4, /device:TPU:0, one launch (start us, length us, event | category | flops | bytes accessed | tf_op | source)
XLA Modules:
  0.0 479.3 jit_solution(16082267082436514925)
XLA Ops:
  2.2 1.1 reduce-window.6
  3.7 1.3 broadcast_in_dim.68.gain_ref
  11.5 69.2 %forward_to_experts.1 = (bf16[512,1536]{1,0:T(8,128)(2,1)}, bf16[512,1536]{1,0:T(8,128)(2,1)}, bf16[4,512,512]{2,1,0:T(8,128)(2,1)}, f32[512,1536]{1,0:T(8,128)}...) custom-call(bf16[512,1536]{1,0:T(8,128)(2,1)} %bitcast.117, ...), custom_call_target="tpu_custom_call" | custom-call | flops 390070272 | bytes 1250000 | tf_op jit(solution)/shard_map/forward_to_experts/pallas_call | solution.py:230
  81.2 3.4 collective-permute-done.refs_1_
  87.3 1.3 copy.54.pos_col_ref
  89.2 39.8 %expert_blocks.2 = (bf16[512,1536]{1,0:T(8,128)(2,1)}, bf16[512,1536]{1,0:T(8,128)(2,1)}, bf16[512,1536]{1,0:T(8,128)(2,1)}, bf16[512,1536]{1,0:T(8,128)(2,1)}, ...) custom-call(s32[2,2,1,512]{3,2,1,0:T(1,128)} %get-tuple-element.147., ...), custom_call_target="tpu_custom_call" | custom-call | flops 1101004800 | bytes 1875000 | tf_op jit(solution)/shard_map/expert_blocks/pallas_call | solution.py:345
  129.2 1.3 copy.55.pos_col_ref
  130.6 2.3 collective-permute-done.3.refs_0_
  132.9 39.6 %expert_blocks.3 = (bf16[512,1536]{1,0:T(8,128)(2,1)}, bf16[512,1536]{1,0:T(8,128)(2,1)}, bf16[512,1536]{1,0:T(8,128)(2,1)}, bf16[512,1536]{1,0:T(8,128)(2,1)}, ...) custom-call(s32[2,2,1,512]{3,2,1,0:T(1,128)} %get-tuple-element.146., ...), custom_call_target="tpu_custom_call", output_to_operand_aliasing={{4}: (9, {}), {5}: (10, {}), {6}: (11, {}), {7}: (12, {})} | custom-call | flops 1101004800 | bytes 1875000 | tf_op jit(solution)/shard_map/expert_blocks/pallas_call | solution.py:345
  173.0 4.0 collective-permute-done.4
  177.0 3.0 add_convert_fusion.2
  180.0 1.1 collective-permute-start.5
  181.1 6.9 %weight_grad.6 = bf16[1,768,1536]{2,1,0:T(8,128)(2,1)} custom-call(s32[1]{0:T(128)} %bitcast.24.chunk_ref, bf16[2,1280,1536]{2,1,0:T(8,128)(2,1)} %bitcast.97, bf16[2,1280,1536]{2,1,0:T(8,128)(2,1)} %bitcast.101), custom_call_target="tpu_custom_call" | custom-call | flops 94371840 | bytes 625000 | tf_op jit(solution)/shard_map/weight_grad/pallas_call | solution.py:385
  188.0 1.5 collective-permute-start.9
  189.5 6.9 %weight_grad.7 = bf16[1,768,1536]{2,1,0:T(8,128)(2,1)} custom-call(s32[1]{0:T(128)} %bitcast.21.chunk_ref, bf16[2,1280,1536]{2,1,0:T(8,128)(2,1)} %bitcast.98, bf16[2,1280,1536]{2,1,0:T(8,128)(2,1)} %bitcast.102), custom_call_target="tpu_custom_call" | custom-call | flops 94371840 | bytes 625000 | tf_op jit(solution)/shard_map/weight_grad/pallas_call | solution.py:385
  196.4 7.3 %weight_grad.8 = bf16[1,768,1536]{2,1,0:T(8,128)(2,1)} custom-call(s32[1]{0:T(128)} %bitcast.21.chunk_ref, bf16[2,1280,1536]{2,1,0:T(8,128)(2,1)} %bitcast.99, bf16[2,1280,1536]{2,1,0:T(8,128)(2,1)} %bitcast.103), custom_call_target="tpu_custom_call" | custom-call | flops 94371840 | bytes 625000 | tf_op jit(solution)/shard_map/weight_grad/pallas_call | solution.py:385
  203.7 6.9 %weight_grad.9.down_mine_ref.mine_down_ref = bf16[2,384,1536]{2,1,0:T(8,128)(2,1)} custom-call(s32[1]{0:T(128)} %bitcast.21.chunk_ref, bf16[2,1280,768]{2,1,0:T(8,128)(2,1)} %bitcast.107, bf16[2,1280,1536]{2,1,0:T(8,128)(2,1)} %bitcast.105), custom_call_target="tpu_custom_call" | custom-call | flops 94371840 | bytes 625000 | tf_op jit(solution)/shard_map/weight_grad/pallas_call | solution.py:385
  210.6 7.0 %weight_grad.10.down_ref.other_down_ref = bf16[2,384,1536]{2,1,0:T(8,128)(2,1)} custom-call(s32[1]{0:T(128)} %bitcast.24.chunk_ref, bf16[2,1280,768]{2,1,0:T(8,128)(2,1)} %bitcast.108, bf16[2,1280,1536]{2,1,0:T(8,128)(2,1)} %bitcast.106), custom_call_target="tpu_custom_call" | custom-call | flops 94371840 | bytes 625000 | tf_op jit(solution)/shard_map/weight_grad/pallas_call | solution.py:385
  217.5 6.9 %weight_grad.11 = bf16[1,768,1536]{2,1,0:T(8,128)(2,1)} custom-call(s32[1]{0:T(128)} %bitcast.24.chunk_ref, bf16[2,1280,1536]{2,1,0:T(8,128)(2,1)} %bitcast.100, bf16[2,1280,1536]{2,1,0:T(8,128)(2,1)} %bitcast.104), custom_call_target="tpu_custom_call" | custom-call | flops 94371840 | bytes 625000 | tf_op jit(solution)/shard_map/weight_grad/pallas_call | solution.py:385
  225.1 4.6 collective-permute-done.7
  229.6 3.1 add_convert_fusion.1
  233.6 1.3 copy.57.kpos_ref
  235.8 1.6 copy.60.normed_ref
  237.4 11.7 %middle_backward.1 = (f32[512,1536]{1,0:T(8,128)}, bf16[512,1536]{1,0:T(8,128)(2,1)}, bf16[512,1536]{1,0:T(8,128)(2,1)}, f32[16,512]{1,0:T(8,128)}, f32[1,1536]{1,0:T(1,128)}) custom-call(bf16[512,1536]{1,0:T(8,128)(2,1)} %get-tuple-element.105.refs_0_, bf16[512,1536]{1,0:T(8,128)(2,1)} %collective-permute-done.2.refs_1_, ...), custom_call_target="tpu_custom_call" | custom-call | flops 75497472 | bytes 625000 | tf_op jit(solution)/shard_map/middle_backward/pallas_call | solution.py:440
  249.1 4.5 convolution_convert_fusion
  253.7 2.4 copy.56
  256.1 87.8 %attention_backward.1 = (bf16[512,1536]{1,0:T(8,128)(2,1)}, bf16[512,512]{1,0:T(8,128)(2,1)}, f32[192,1536]{1,0:T(8,128)}, bf16[768,1536]{1,0:T(8,128)(2,1)}, bf...) custom-call(bf16[512,1536]{1,0:T(8,128)(2,1)} %get-tuple-element.104.q_ref, ...), custom_call_target="tpu_custom_call" | custom-call | flops 503316480 | bytes 1250000 | tf_op jit(solution)/shard_map/attention_backward/pallas_call | solution.py:648
  343.9 120.9 %last_part.1 = (f32[192,1536]{1,0:T(8,128)}, f32[2,96,1536]{2,1,0:T(8,128)}, bf16[512,1536]{1,0:T(8,128)(2,1)}, f32[8,1536]{1,0:T(8,128)}, f32[48,1536]{1,0:T(8,...) custom-call(bf16[768,1536]{1,0:T(8,128)(2,1)} %get-tuple-element.122.piece_ref, ...), custom_call_target="tpu_custom_call" | custom-call | flops 312500000 | bytes 1250000 | tf_op jit(solution)/shard_map/last_part/pallas_call | solution.py:920
  466.2 1.5 fusion.19
  467.6 3.3 pad_maximum_fusion
  471.1 4.1 fusion
  475.2 1.1 copy.76
  (72 shorter events, 19.0 us)
Async XLA Ops:
  0.6 8.8 %copy-start.8 = (f32[1536]{0:T(1024)S(1)}, f32[1536]{0:T(1024)}, u32[]{:S(2)}) copy-start(f32[1536]{0:T(1024)} %param.19) | copy-start | bytes 18436
  7.8 72.9 %copy-start.7 = (s32[1,1,2,256]{3,1,2,0:T(1,128)}, s32[1,1,2,256]{3,1,2,0:T(1,128)S(1)}, u32[]{:S(2)}) copy-start(s32[1,1,2,256]{3,1,2,0:T(1,128)S(1)} %copy.62) | copy-start | bytes 6148
  80.7 3.8 collective-permute-start
  84.6 44.5 %collective-permute-start.1 = (bf16[512,1536]{1,0:T(8,128)(2,1)}, bf16[512,1536]{1,0:T(8,128)(2,1)}, u32[]{:S(2)}, u32[]{:S(2)}) collective-permute-start(bf16[512,1536]{1,0:T(8,128)(2,1)} %get-tuple-element.79.refs_0_), channel_id=1, source_target_pairs={{0,2},{1,3},{2,0},{3,1},{4,6},{5,7},{6,4},{7,5},{8,10},{9,11},{10,... | collective-permute-start | bytes 4718600 | tf_op jit(solution)/shard_map/ppermute | solution.py:952
  129.1 3.8 collective-permute-start.3
  172.5 4.5 collective-permute-start.4
  172.7 51.8 %collective-permute-start.2 = (bf16[512,1536]{1,0:T(8,128)(2,1)}, bf16[512,1536]{1,0:T(8,128)(2,1)}, u32[]{:S(2)}, u32[]{:S(2)}) collective-permute-start(bf16[512,1536]{1,0:T(8,128)(2,1)} %get-tuple-element.81), channel_id=1, source_target_pairs={{0,1},{1,0},{2,3},{3,2},{4,5},{5,4},{6,7},{7,6},{8,9},{9,8},{10,11... | collective-permute-start | bytes 4718600 | tf_op jit(solution)/shard_map/ppermute | solution.py:947
  180.0 44.5 %collective-permute-start.5 = (bf16[512,1536]{1,0:T(8,128)(2,1)}, bf16[512,1536]{1,0:T(8,128)(2,1)}, u32[]{:S(2)}, u32[]{:S(2)}) collective-permute-start(bf16[512,1536]{1,0:T(8,128)(2,1)} %add_convert_fusion.2), channel_id=1, source_target_pairs={{0,2},{1,3},{2,0},{3,1},{4,6},{5,7},{6,4},{7,5},{8,10},{9,11},{10,... | collective-permute-start | bytes 4718600 | tf_op jit(solution)/shard_map/ppermute | solution.py:952
  188.0 61.2 %collective-permute-start.9 = (bf16[768,1536]{1,0:T(8,128)(2,1)}, bf16[768,1536]{1,0:T(8,128)(2,1)}, u32[]{:S(2)}, u32[]{:S(2)}) collective-permute-start(bf16[768,1536]{1,0:T(8,128)(2,1)} %bitcast.122), channel_id=1, source_target_pairs={{0,16},{16,0},{1,17},{17,1},{2,18},{18,2},{3,19},{19,3},{4,20},{20... | collective-permute-start | bytes 7077896 | tf_op jit(solution)/shard_map/ppermute | solution.py:943
  224.5 5.2 %collective-permute-start.7 = (bf16[512,1536]{1,0:T(8,128)(2,1)}, bf16[512,1536]{1,0:T(8,128)(2,1)S(1)}, u32[]{:S(2)}, u32[]{:S(2)}) collective-permute-start(bf16[512,1536]{1,0:T(8,128)(2,1)} %get-tuple-element.102), channel_id=1, source_target_pairs={{0,1},{1,0},{2,3},{3,2},{4,5},{5,4},{6,7},{7,6},{8,9},{9,8},{10,11... | collective-permute-start | bytes 4718600 | tf_op jit(solution)/shard_map/ppermute | solution.py:947
  224.6 246.4 %collective-permute-start.6 = (bf16[512,1536]{1,0:T(8,128)(2,1)}, bf16[512,1536]{1,0:T(8,128)(2,1)}, u32[]{:S(2)}, u32[]{:S(2)}) collective-permute-start(bf16[512,1536]{1,0:T(8,128)(2,1)} %get-tuple-element.101), channel_id=1, source_target_pairs={{0,1},{1,0},{2,3},{3,2},{4,5},{5,4},{6,7},{7,6},{8,9},{9,8},{10,11... | collective-permute-start | bytes 4718600 | tf_op jit(solution)/shard_map/ppermute | solution.py:947
  229.6 5.3 %copy-start.2 = (bf16[512,1536]{1,0:T(8,128)(2,1)S(1)}, bf16[512,1536]{1,0:T(8,128)(2,1)}, u32[]{:S(2)}) copy-start(bf16[512,1536]{1,0:T(8,128)(2,1)} %get-tuple-element.126) | copy-start | bytes 4718596
  232.7 238.3 %collective-permute-start.8 = (bf16[512,1536]{1,0:T(8,128)(2,1)}, bf16[512,1536]{1,0:T(8,128)(2,1)}, u32[]{:S(2)}, u32[]{:S(2)}) collective-permute-start(bf16[512,1536]{1,0:T(8,128)(2,1)} %add_convert_fusion.1), channel_id=1, source_target_pairs={{0,2},{1,3},{2,0},{3,1},{4,6},{5,7},{6,4},{7,5},{8,10},{9,11},{10,... | collective-permute-start | bytes 4718600 | tf_op jit(solution)/shard_map/ppermute | solution.py:952
  467.6 3.4 copy-start
  467.6 3.5 copy-start.1
  471.0 4.3 copy-start.3
  475.2 1.2 copy-start.6
  475.2 1.9 copy-start.5
  475.2 2.6 copy-start.4
